TPU v7x, 32 devices: a whole 2x2x4 slice. The times are simulated.
32 devices in a mesh: dp: 8 (over y, x, core), expert: 4 (over z).
Axes of the slice: x: 2, y: 2, z: 4, core: 2. Of those that a mesh axis runs over, the one named last changes fastest.
Arguments:
- layer_inputs_matrix: bfloat16 [32768, 768], P(('dp', 'expert')), may hold values from -6 to 6
- upstream_output_sensitivity: bfloat16 [32768, 768], P(('dp', 'expert')), may hold values from -6 to 6
- mixer_layernorm_scale: float32 [768], replicated, may hold values from 0.5 to 1.5
- mixer_layernorm_offset: float32 [768], replicated, may hold values from -1 to 1
- asker_matrix: bfloat16 [768, 768], replicated, may hold values from -0.21875 to 0.21875
- lookup_label_matrix: bfloat16 [768, 768], replicated, may hold values from -0.21875 to 0.21875
- content_matrix: bfloat16 [768, 768], replicated, may hold values from -0.21875 to 0.21875
- mixer_result_matrix: bfloat16 [768, 768], replicated, may hold values from -1.75 to 1.75
- specialist_layernorm_scale: float32 [768], replicated, may hold values from 0.5 to 1.5
- specialist_layernorm_offset: float32 [768], replicated, may hold values from -0.5 to 0.5
- dispatch_projection_matrix: float32 [768, 16], replicated, may hold values from -0.21875 to 0.21875
- specialist_centroids: float32 [4, 16], replicated, may hold values from -5 to 5
- learned_sharpness: float32 [1], replicated, may hold values from 0.25 to 0.45
- specialist_widening_matrix: bfloat16 [4, 768, 3072], P('expert'), may hold values from -0.21875 to 0.21875
- specialist_narrowing_matrix: bfloat16 [4, 3072, 768], P('expert'), may hold values from -0.4375 to 0.4375
- document_labels: int32 [64, 512], P(('dp', 'expert')), may hold values from 0 to 7, never falling along the last dimension, each value on 1 to 256 neighbouring positions
- chosen_specialist: int32 [32768, 1], P(('dp', 'expert')), may hold values from 0 to 3; in each aligned block of 1024 rows (0 to 1023, 1024 to 2047, ...) at most 384 rows name the same one
- placement_ranks: int32 [32, 1024], P(('dp', 'expert')), may hold values from 0 to 1023, each once within a row
Outputs:
- layer_output: bfloat16 [32768, 768], P(('dp', 'expert'))
- tokens_grad: bfloat16 [32768, 768], P(('dp', 'expert'))
- attngain_grad: float32 [768], P(('dp', 'expert'))
- attnshift_grad: float32 [768], P(('dp', 'expert'))
- query_grad: float32 [768, 768], P(('dp', 'expert'))
- key_grad: float32 [768, 768], P(('dp', 'expert'))
- value_grad: float32 [768, 768], P(('dp', 'expert'))
- outer_grad: float32 [768, 768], P(('dp', 'expert'))
- routegain_grad: float32 [768], P(('dp', 'expert'))
- routeshift_grad: float32 [768], P(('dp', 'expert'))
- router_grad: float32 [768, 16], P(('dp', 'expert'))
- centroid_derivative: float32 [4, 16], replicated
- sharpness_derivative: float32 [1], replicated
- hidden_grad: float32 [4, 768, 3072], P('expert', 'dp')
- return_grad: float32 [4, 3072, 768], P('expert', 'dp')
Inputs may be any that keep to these rules, and one draw needn't show every extreme that they name: `chosen_specialist`: within the 1024 rows of one device no expert is named by more than 384 rows, a bound that some block reaches. `document_labels`: ids never fall along a row; a segment has 1 to 256 rows. `placement_ranks`: each row is a permutation; a smaller value is placed first.
All inputs are finite; a program needn't handle non-finite values.
Results may differ from a plain program's by a relative error of at most 0.035.
Values may be sent and summed in bfloat16 or wider, within the bound.
No kernel may reach another device: no remote copies, remote signals or barrier semaphores. Data moves between devices by JAX's collectives and lax.ppermute only.
A program may use at most 256 MiB of HBM per device.

v0:
```python
from functools import partial

import jax
import jax.numpy as jnp
from jax import lax
from jax.sharding import PartitionSpec as P

HEAD_DIM = 64


EPSILON = 1e-05
MASKED = -1e30


def prefix(array, axis, combine, identity):
    size, place = (lax.axis_size(axis), lax.axis_index(axis))
    everything = lax.all_gather(array, axis)
    start = jnp.broadcast_to(jnp.asarray(identity, array.dtype), array.shape)

    def hop(k, before):
        reached = k < place
        new = combine(before, everything[k])
        return jnp.where(reached, new, before)

    return lax.fori_loop(0, size, hop, start)


def layer_norm(values, norm_gain, norm_shift):
    centered = values - jnp.mean(values, axis=-1, keepdims=True)
    variance = jnp.mean(centered * centered, axis=-1, keepdims=True)
    return centered * lax.rsqrt(variance + EPSILON) * norm_gain + norm_shift


def routing_gate_value(normed, router_mat, embed_mat, temper_val, selected_expert):
    projected = jnp.dot(normed, router_mat, precision=lax.Precision.HIGHEST)
    unit_rows = projected * lax.rsqrt(jnp.sum(projected * projected, axis=-1, keepdims=True) + 1.0)
    unit_table = embed_mat * lax.rsqrt(jnp.sum(embed_mat * embed_mat, axis=-1, keepdims=True) + 1.0)
    logits = jnp.dot(unit_rows, unit_table.T, precision=lax.Precision.HIGHEST) / temper_val[0]
    routed = jax.nn.softmax(logits, axis=-1)
    return jnp.sum(routed * selected_expert, axis=-1)


def add_counts(earlier, later):
    return earlier + later


def exact_gelu(values):
    return jax.nn.gelu(values, approximate=False)


def body(
    layer_inputs_matrix,
    upstream_output_sensitivity,
    mixer_layernorm_scale,
    mixer_layernorm_offset,
    asker_matrix,
    lookup_label_matrix,
    content_matrix,
    mixer_result_matrix,
    specialist_layernorm_scale,
    specialist_layernorm_offset,
    dispatch_projection_matrix,
    specialist_centroids,
    learned_sharpness,
    specialist_widening_matrix,
    specialist_narrowing_matrix,
    document_labels,
    chosen_specialist,
    placement_ranks,
):
    rows_here, model_width = layer_inputs_matrix.shape
    seq_total, seq_len = document_labels.shape
    head_count = model_width // HEAD_DIM
    score_scale = HEAD_DIM ** (-0.5)
    local_experts = specialist_widening_matrix.shape[0]
    ffn_width = specialist_widening_matrix.shape[2]
    group_size = lax.axis_size("expert")
    expert_total = local_experts * group_size
    capacity = rows_here // local_experts
    slot_count = 3 * rows_here // (2 * expert_total)
    buffer_rows = expert_total * slot_count
    inputs = layer_inputs_matrix.astype(jnp.float32)
    normed_one, norm_one_back = jax.vjp(
        layer_norm, inputs, mixer_layernorm_scale, mixer_layernorm_offset
    )
    normed_low = normed_one.astype(jnp.bfloat16)

    def heads_of(weight_mat):
        projected = jnp.dot(normed_low, weight_mat, preferred_element_type=jnp.float32)
        return projected.astype(jnp.bfloat16).reshape(seq_total, seq_len, head_count, HEAD_DIM)

    queries = heads_of(asker_matrix)
    keys_low = heads_of(lookup_label_matrix)
    values_low = heads_of(content_matrix)
    allowed = (document_labels[:, :, None] == document_labels[:, None, :])[:, None]

    def raw_scores():
        scores = (
            jnp.einsum("sqhd,skhd->shqk", queries, keys_low, preferred_element_type=jnp.float32)
            * score_scale
        )
        return jnp.where(allowed, scores, MASKED)

    scores = raw_scores()
    largest = jnp.max(scores, axis=-1, keepdims=True)
    weights = jnp.exp(scores - largest)
    log_total = largest + jnp.log(jnp.sum(weights, axis=-1, keepdims=True))
    probs = jnp.exp(scores - log_total)
    attended = jnp.einsum(
        "shqk,skhd->sqhd",
        probs.astype(jnp.bfloat16),
        values_low,
        preferred_element_type=jnp.float32,
    )
    attended_low = attended.astype(jnp.bfloat16).reshape(rows_here, model_width)
    residual = inputs + jnp.dot(
        attended_low, mixer_result_matrix, preferred_element_type=jnp.float32
    )
    second_normalized, norm_two_back = jax.vjp(
        layer_norm, residual, specialist_layernorm_scale, specialist_layernorm_offset
    )
    entering = second_normalized.astype(jnp.bfloat16)
    chosen_ids = chosen_specialist[:, 0]
    expert_ids = lax.broadcasted_iota(jnp.int32, (rows_here, expert_total), 1)
    selected_expert = chosen_ids[:, None] == expert_ids
    chosen_int = selected_expert.astype(jnp.int32)
    order_row = placement_ranks[0]
    earlier_mask = (order_row[None, :] < order_row[:, None]).astype(jnp.bfloat16)
    ahead = jnp.dot(
        earlier_mask, selected_expert.astype(jnp.bfloat16), preferred_element_type=jnp.float32
    )
    rank_local = jnp.sum(jnp.where(selected_expert, ahead, 0.0), axis=-1).astype(jnp.int32)
    tallies = jnp.sum(chosen_int, axis=0)
    prior = prefix(tallies, "expert", add_counts, jnp.zeros_like(tallies))
    slot_index = jnp.sum(chosen_int * prior[None, :], axis=-1).astype(jnp.int32) + rank_local
    kept = slot_index < capacity
    position = jnp.where(kept, chosen_ids * slot_count + rank_local, buffer_rows)
    row_numbers = jnp.arange(rows_here, dtype=jnp.int32)
    source_rows = (
        jnp.full((buffer_rows + 1,), rows_here, jnp.int32)
        .at[position]
        .set(row_numbers)[:buffer_rows]
    )
    zero_row = jnp.zeros((1, model_width), jnp.bfloat16)
    outgoing = jnp.concatenate([entering, zero_row], axis=0)[source_rows].reshape(
        expert_total, slot_count, model_width
    )
    arrived = lax.all_to_all(outgoing, "expert", split_axis=0, concat_axis=0, tiled=True)
    item_count = arrived.shape[1]
    grouped = arrived.reshape(group_size, local_experts, item_count, model_width)
    hidden_pre = jnp.einsum(
        "nemd,edf->nemf", grouped, specialist_widening_matrix, preferred_element_type=jnp.float32
    )
    active = exact_gelu(hidden_pre).astype(jnp.bfloat16)
    produced = jnp.einsum(
        "nemf,efd->nemd", active, specialist_narrowing_matrix, preferred_element_type=jnp.float32
    )
    produced = produced.astype(jnp.bfloat16).reshape(expert_total, item_count, model_width)
    returned = lax.all_to_all(produced, "expert", split_axis=0, concat_axis=0, tiled=True)
    extra = (hidden_pre.reshape(expert_total, item_count, ffn_width),)
    outcome = (returned, arrived) + extra
    returned = outcome[0]
    arrived = outcome[1]
    padded_out = jnp.concatenate([returned.reshape(buffer_rows, model_width), zero_row], axis=0)
    per_token = padded_out[position].astype(jnp.float32)
    selected_expert_float = selected_expert.astype(jnp.float32)
    kept_float = kept.astype(jnp.float32)
    gate, dispatcher_reverse = jax.vjp(
        partial(routing_gate_value, selected_expert=selected_expert_float),
        second_normalized,
        dispatch_projection_matrix,
        specialist_centroids,
        learned_sharpness,
    )
    weighted = gate * kept_float
    layer_output = (residual + weighted[:, None] * per_token).astype(jnp.bfloat16)
    upstream = upstream_output_sensitivity.astype(jnp.float32)
    mixing_coefficient_derivative = jnp.sum(upstream * per_token, axis=-1) * kept_float
    sent_grad = (weighted[:, None] * upstream).astype(jnp.bfloat16)
    grad_out = jnp.concatenate([sent_grad, zero_row], axis=0)[source_rows].reshape(
        expert_total, slot_count, model_width
    )
    arrived_grad = lax.all_to_all(grad_out, "expert", split_axis=0, concat_axis=0, tiled=True)
    grouped_in = arrived.reshape(group_size, local_experts, slot_count, model_width)
    grouped_grad = arrived_grad.reshape(group_size, local_experts, slot_count, model_width)
    hidden_pre = outcome[2].reshape(group_size, local_experts, slot_count, ffn_width)
    active, gelu_back = jax.vjp(exact_gelu, hidden_pre)
    active_low = active.astype(jnp.bfloat16)
    active_grad = jnp.einsum(
        "nemd,efd->nemf",
        grouped_grad,
        specialist_narrowing_matrix,
        preferred_element_type=jnp.float32,
    )
    pre_grad = gelu_back(active_grad)[0].astype(jnp.bfloat16)
    input_back = jnp.einsum(
        "nemf,edf->nemd", pre_grad, specialist_widening_matrix, preferred_element_type=jnp.float32
    )
    input_back = input_back.astype(jnp.bfloat16).reshape(expert_total, slot_count, model_width)
    back_home = lax.all_to_all(input_back, "expert", split_axis=0, concat_axis=0, tiled=True)
    hidden_full = jnp.einsum(
        "nemd,nemf->edf", grouped_in, pre_grad, preferred_element_type=jnp.float32
    )
    return_full = jnp.einsum(
        "nemf,nemd->efd", active_low, grouped_grad, preferred_element_type=jnp.float32
    )
    hidden_grad, return_grad = (
        lax.psum_scatter(
            hidden_full.astype(jnp.bfloat16), "dp", scatter_dimension=1, tiled=True
        ).astype(jnp.float32),
        lax.psum_scatter(
            return_full.astype(jnp.bfloat16), "dp", scatter_dimension=1, tiled=True
        ).astype(jnp.float32),
    )
    padded_back = jnp.concatenate([back_home.reshape(buffer_rows, model_width), zero_row], axis=0)
    expert_input_grad = padded_back[position].astype(jnp.float32)
    dispatcher_piece, dispatcher_complete, centroid_picked, sharpness_picked = dispatcher_reverse(
        mixing_coefficient_derivative
    )
    two_part, routegain_full, routeshift_full = norm_two_back(expert_input_grad + dispatcher_piece)
    residual_grad = upstream + two_part
    branch_grad = residual_grad.astype(jnp.bfloat16)
    outer_full = jnp.dot(attended_low.T, branch_grad, preferred_element_type=jnp.float32)
    attended_grad = jnp.dot(branch_grad, mixer_result_matrix.T, preferred_element_type=jnp.float32)
    attended_grad = attended_grad.astype(jnp.bfloat16).reshape(
        seq_total, seq_len, head_count, HEAD_DIM
    )
    probs = jnp.exp(raw_scores() - log_total)
    prob_grad = jnp.einsum(
        "sqhd,skhd->shqk", attended_grad, values_low, preferred_element_type=jnp.float32
    )
    values_grad = jnp.einsum(
        "shqk,sqhd->skhd",
        probs.astype(jnp.bfloat16),
        attended_grad,
        preferred_element_type=jnp.float32,
    )
    values_grad = values_grad.astype(jnp.bfloat16).reshape(rows_here, model_width)
    centered_grad = jnp.sum(prob_grad * probs, axis=-1, keepdims=True)
    score_grad = (probs * (prob_grad - centered_grad)).astype(jnp.bfloat16)
    queries_grad = (
        jnp.einsum("shqk,skhd->sqhd", score_grad, keys_low, preferred_element_type=jnp.float32)
        * score_scale
    )
    queries_grad = queries_grad.astype(jnp.bfloat16).reshape(rows_here, model_width)
    keys_grad = (
        jnp.einsum("shqk,sqhd->skhd", score_grad, queries, preferred_element_type=jnp.float32)
        * score_scale
    )
    keys_grad = keys_grad.astype(jnp.bfloat16).reshape(rows_here, model_width)
    query_full = jnp.dot(normed_low.T, queries_grad, preferred_element_type=jnp.float32)
    key_full = jnp.dot(normed_low.T, keys_grad, preferred_element_type=jnp.float32)
    value_full = jnp.dot(normed_low.T, values_grad, preferred_element_type=jnp.float32)
    one_grad = jnp.dot(queries_grad, asker_matrix.T, preferred_element_type=jnp.float32)
    one_grad = one_grad + jnp.dot(
        keys_grad, lookup_label_matrix.T, preferred_element_type=jnp.float32
    )
    one_grad = one_grad + jnp.dot(values_grad, content_matrix.T, preferred_element_type=jnp.float32)
    one_part, attngain_full, attnshift_full = norm_one_back(one_grad)
    tokens_grad = (residual_grad + one_part).astype(jnp.bfloat16)
    summed = (
        lax.psum_scatter(query_full, ("dp", "expert"), scatter_dimension=0, tiled=True),
        lax.psum_scatter(key_full, ("dp", "expert"), scatter_dimension=0, tiled=True),
        lax.psum_scatter(value_full, ("dp", "expert"), scatter_dimension=0, tiled=True),
        lax.psum_scatter(outer_full, ("dp", "expert"), scatter_dimension=0, tiled=True),
        lax.psum_scatter(dispatcher_complete, ("dp", "expert"), scatter_dimension=0, tiled=True),
        lax.psum_scatter(attngain_full, ("dp", "expert"), scatter_dimension=0, tiled=True),
        lax.psum_scatter(attnshift_full, ("dp", "expert"), scatter_dimension=0, tiled=True),
        lax.psum_scatter(routegain_full, ("dp", "expert"), scatter_dimension=0, tiled=True),
        lax.psum_scatter(routeshift_full, ("dp", "expert"), scatter_dimension=0, tiled=True),
    )
    centroid_derivative, sharpness_derivative = lax.psum(
        (centroid_picked, sharpness_picked), ("dp", "expert")
    )
    return (
        layer_output,
        tokens_grad,
        summed[5],
        summed[6],
        summed[0],
        summed[1],
        summed[2],
        summed[3],
        summed[7],
        summed[8],
        summed[4],
        centroid_derivative,
        sharpness_derivative,
        hidden_grad,
        return_grad,
    )


def solution(mesh):
    placed = (
        P(("dp", "expert"), None),
        P(("dp", "expert"), None),
        P(),
        P(),
        P(),
        P(),
        P(),
        P(),
        P(),
        P(),
        P(),
        P(),
        P(),
        P("expert", None, None),
        P("expert", None, None),
        P(("dp", "expert"), None),
        P(("dp", "expert"), None),
        P(("dp", "expert"), None),
    )
    return jax.shard_map(
        body,
        mesh=mesh,
        in_specs=placed,
        out_specs=(
            P(("dp", "expert"), None),
            P(("dp", "expert"), None),
            P(("dp", "expert")),
            P(("dp", "expert")),
            P(("dp", "expert"), None),
            P(("dp", "expert"), None),
            P(("dp", "expert"), None),
            P(("dp", "expert"), None),
            P(("dp", "expert")),
            P(("dp", "expert")),
            P(("dp", "expert"), None),
            P(),
            P(),
            P("expert", "dp", None),
            P("expert", "dp", None),
        ),
        check_vma=False,
    )
```

profile of v0, /device:TPU:0, one launch (start us, length us, event | category | flops | bytes accessed | tf_op | source)
XLA Modules:
  0.0 994.3 jit_solution(7341003072041419520)
XLA Ops:
  10.4 9.9 all-reduce.4
  25.9 4.3 scatter_custom_fusion
  30.6 4.2 convolution_convert_fusion.3
  37.7 3.9 reshape.257
  41.5 4.1 convolution_convert_fusion.4
  48.2 3.8 reshape.256
  52.0 2.8 convolution_convert_fusion.5
  57.4 3.8 reshape.255
  61.2 12.3 %fusion = (f32[2,12,512]{2,1,0:T(8,128)S(1)}, f32[2,12,512,512]{2,3,1,0:T(8,128)}) fusion(pred[2,512,512]{1,2,0:T(8,128)(4,1)S(1)} %broadcast_compare_fusion, bf16[2,512,12,64]{1,0,3,2:T(2,128)(2,1)} %reshape.257, bf16[2,512,12,64]{1,0,3,2:T(2,128)(2,1)} %reshape.256), kind=kOutput, calls=%fused_computation.13 | convolution fusion | flops 824168448 | bytes 28884992 | tf_op jit(solution)/shard_map/sqhd,skhd->shqk/dot_general | solution.py:99
  73.5 11.1 %exponential_reduce_fusion = f32[2,12,512]{2,1,0:T(8,128)S(1)} fusion(f32[2,12,512,512]{2,3,1,0:T(8,128)} %get-tuple-element.144, f32[2,12,512]{2,1,0:T(8,128)S(1)} %get-tuple-element.143, pred[2,512,512]{1,2,0:T(8,128)(4,1)S(1)} %broadcast_compare_fusion), kind=kLoop, calls=%fused_computation.11 | loop fusion | flops 25153536 | bytes 25788416 | tf_op jit(solution)/shard_map/reduce_sum | solution.py:107
  84.7 11.9 %fusion.76 = bf16[2,512,12,64]{1,3,2,0:T(8,128)(2,1)S(1)} fusion(bf16[2,512,12,64]{1,0,3,2:T(2,128)(2,1)S(1)} %copy-done.16, f32[2,12,512,512]{2,3,1,0:T(8,128)} %get-tuple-element.144, f32[2,12,512]{2,1,0:T(8,128)S(1)} %log_add_fusion, pred[2,512,512]{1,2,0:T(8,128)(4,1)S(1)} %broadcast_compare_fusion), kind=kOutput, calls=%fused_computation.113 | convolution fusion | flops 831258624 | bytes 28884992 | tf_op jit(solution)/shard_map/shqk,skhd->sqhd/dot_general | solution.py:109
  102.8 5.6 gather_fusion
  108.5 55.9 %all_to_all.20 = bf16[4,384,768]{2,1,0:T(8,128)(2,1)S(1)} all-to-all(bf16[4,384,768]{2,1,0:T(8,128)(2,1)} %bitcast.219), channel_id=1, replica_groups=mesh['dp'=8,'expert'=4] {'expert'}, dimensions={0} | all-to-all | bytes 4718592 | tf_op jit(solution)/shard_map/all_to_all | solution.py:148
  164.4 10.3 %fusion.35 = f32[4,384,3072]{2,1,0:T(8,128)S(1)} fusion(bf16[4,384,768]{2,1,0:T(8,128)(2,1)S(1)} %all_to_all.20, bf16[1,768,3072]{2,1,0:T(8,128)(2,1)} %param.33), kind=kOutput, calls=%fused_computation.64 | convolution fusion | flops 7247757312 | bytes 25952256 | tf_op jit(solution)/shard_map/nemd,edf->nemf/dot_general | solution.py:151
  174.7 6.5 copy-done.93
  181.1 48.0 %fusion.56 = bf16[4,384,768]{2,1,0:T(8,128)(2,1)} fusion(bf16[1,3072,768]{2,1,0:T(8,128)(2,1)S(1)} %bitcast.244, f32[4,384,3072]{2,1,0:T(8,128)S(1)} %fusion.35), kind=kOutput, calls=%fused_computation.93 | convolution fusion | flops 7555645440 | bytes 25952256 | tf_op jit(solution)/shard_map/nemf,efd->nemd/dot_general | solution.py:155
  229.2 3.8 all-to-all-start.1
  235.2 5.2 multiply_reduce_fusion.5
  242.5 43.1 %all-to-all-done.1 = bf16[4,384,768]{2,1,0:T(8,128)(2,1)S(1)} async-done(((bf16[4,384,768]{2,1,0:T(8,128)(2,1)}), bf16[4,384,768]{2,1,0:T(8,128)(2,1)S(1)}, u32[]{:S(2)}, u32[]{:S(2)}) %all-to-all-start.1) | async-done | bytes 2359328 | tf_op jit(solution)/shard_map/all_to_all | solution.py:159
  288.9 5.5 gather_fusion.1
  298.3 5.6 gather_fusion.2
  303.9 56.9 %all_to_all.21 = bf16[4,384,768]{2,1,0:T(8,128)(2,1)S(1)} all-to-all(bf16[4,384,768]{2,1,0:T(8,128)(2,1)} %bitcast.218), channel_id=1, replica_groups=mesh['dp'=8,'expert'=4] {'expert'}, dimensions={0} | all-to-all | bytes 4718592 | tf_op jit(solution)/shard_map/all_to_all | solution.py:183
  362.3 48.0 %fusion.40 = bf16[1,3072,768]{2,1,0:T(8,128)(2,1)} fusion(bf16[4,384,768]{2,1,0:T(8,128)(2,1)S(1)} %all_to_all.21, f32[4,384,3072]{2,1,0:T(8,128)} %copy-done.93), kind=kOutput, calls=%fused_computation.67 | convolution fusion | flops 7556825088 | bytes 25952256 | tf_op jit(solution)/shard_map/nemf,nemd->efd/dot_general | solution.py:204
  410.6 50.8 %fusion.7 = bf16[4,1,384,3072]{3,2,0,1:T(8,128)(2,1)S(1)} fusion(f32[4,384,3072]{2,1,0:T(8,128)} %copy-done.93, bf16[4,384,768]{2,1,0:T(8,128)(2,1)} %copy-done.22, bf16[1,3072,768]{2,1,0:T(8,128)(2,1)} %param.34), kind=kOutput, calls=%fused_computation.22 | convolution fusion | flops 7587495936 | bytes 35389440 | tf_op jit(solution)/shard_map/nemd,efd->nemf/dot_general | solution.py:189
  461.4 3.6 copy-done.92
  465.0 9.3 fusion.37
  474.4 12.6 %fusion.59 = bf16[4,384,768]{2,1,0:T(8,128)(2,1)} fusion(bf16[1,768,3072]{2,1,0:T(8,128)(2,1)} %param.33, bf16[4,1,384,3072]{3,2,0,1:T(8,128)(2,1)} %copy-done.92), kind=kOutput, calls=%fused_computation.94 | convolution fusion | flops 7248936960 | bytes 16515072 | tf_op jit(solution)/shard_map/nemf,edf->nemd/dot_general | solution.py:196
  486.9 3.8 all-to-all-start.3
  496.4 47.2 %all-to-all-done.3 = bf16[4,384,768]{2,1,0:T(8,128)(2,1)S(1)} async-done(((bf16[4,384,768]{2,1,0:T(8,128)(2,1)}), bf16[4,384,768]{2,1,0:T(8,128)(2,1)S(1)}, u32[]{:S(2)}, u32[]{:S(2)}) %all-to-all-start.3) | async-done | bytes 2359328 | tf_op jit(solution)/shard_map/all_to_all | solution.py:200
  546.9 5.5 gather_fusion.3
  552.4 6.2 multiply_reduce_fusion.1
  567.4 2.9 reshape.267
  570.3 5.4 fusion.143
  575.9 11.7 %fusion.77 = bf16[2,512,12,64]{1,3,2,0:T(8,128)(2,1)S(1)} fusion(bf16[2,512,12,64]{1,0,3,2:T(2,128)(2,1)S(1)} %reshape.267, f32[2,12,512,512]{2,3,1,0:T(8,128)} %get-tuple-element.144, f32[2,12,512]{2,1,0:T(8,128)S(1)} %copy-done.31, pred[2,512,512]{1,2,0:T(8,128)(4,1)S(1)} %copy-done.13), kind=kOutput, calls=%fused_computation.114 | convolution fusion | flops 831258624 | bytes 28884992 | tf_op jit(solution)/shard_map/shqk,sqhd->skhd/dot_general | solution.py:232
  590.9 3.3 fusion.127
  594.2 17.9 %multiply_reduce_fusion = (f32[2,12,512]{2,1,0:T(8,128)S(1)}, f32[2,12,512,512]{2,3,1,0:T(8,128)}) fusion(f32[2,12,512,512]{2,3,1,0:T(8,128)} %get-tuple-element.144, f32[2,12,512]{2,1,0:T(8,128)S(1)} %copy-done.31, pred[2,512,512]{1,2,0:T(8,128)(4,1)S(1)} %copy-done.13, bf16[2,512,12,64]{1,0,3,2:T(2,128)(2,1)} %reshape.255, ...), kind=kOutput, calls=%fused_computation.9 | convolution fusion | flops 836751360 | bytes 54099968 | tf_op jit(solution)/shard_map/sqhd,skhd->shqk/dot_general | solution.py:229
  612.4 22.3 %multiply_convert_fusion = bf16[2,12,512,512]{2,3,1,0:T(8,128)(2,1)} fusion(f32[2,12,512,512]{2,3,1,0:T(8,128)} %get-tuple-element.154, f32[2,12,512,512]{2,3,1,0:T(8,128)} %get-tuple-element.144, f32[2,12,512]{2,1,0:T(8,128)S(1)} %get-tuple-element.153, f32[2,12,512]{2,1,0:T(8,128)S(1)} %copy-done.31, pred[2,512,512]{1,2,0:T(8,128)(4,1)S(1)} %copy-done.13), kind=kLoop, calls=%fused_computation.8 | loop fusion | flops 37748736 | bytes 63537152 | tf_op jit(solution)/shard_map/convert_element_type | solution.py:240
  634.7 8.5 fusion.79
  646.5 3.4 fusion.129
  650.6 4.3 fusion.65
  654.9 6.8 fusion.78
  664.8 3.3 fusion.131
  669.0 3.4 fusion.142
  679.6 39.6 %all-reduce.10 = (f32[768]{0:T(1024)S(1)}, f32[768]{0:T(1024)S(1)}, f32[768]{0:T(1024)S(1)}, f32[768]{0:T(1024)S(1)}, f32[768,16]{0,1:T(8,128)S(1)}, /*index=5*/f32[4,16]{1,0:T(4,128)}, f32[1]{0:T(128)}) all-reduce(f32[768]{0:T(1024)S(1)} %get-tuple-element.112, ...), channel_id=3, replica_groups=mesh['dp'=8,'expert'=4] {'dp','expert'}, use_global_device_ids=true, to_apply=%region_26.27.clone | all-reduce | flops 15425 | bytes 123400
  722.2 4.9 add_convert_fusion
  731.6 47.0 %reduce-scatter.12.cloned.1.call-done = f32[24,768]{1,0:T(8,128)} async-done(((f32[768,768]{1,0:T(8,128)}), f32[24,768]{1,0:T(8,128)}) %reduce-scatter.12.cloned.1.call-update) | async-done | bytes 73744 | tf_op jit(solution)/shard_map/reduce_scatter | solution.py:264
  778.5 103.8 %reduce-scatter.10.cloned.1.call-done = f32[24,768]{1,0:T(8,128)} async-done(((f32[768,768]{1,0:T(8,128)}), f32[24,768]{1,0:T(8,128)}) %reduce-scatter.10.cloned.1.call-update) | async-done | bytes 73744 | tf_op jit(solution)/shard_map/reduce_scatter | solution.py:263
  882.3 104.6 %reduce-scatter.8.cloned.1.call-done = f32[24,768]{1,0:T(8,128)} async-done(((f32[768,768]{1,0:T(8,128)}), f32[24,768]{1,0:T(8,128)}) %reduce-scatter.8.cloned.1.call-update) | async-done | bytes 73744 | tf_op jit(solution)/shard_map/reduce_scatter | solution.py:262
  (286 shorter events, 78.0 us)
Async XLA Ops:
  7.2 44.8 %copy-start = (bf16[768,768]{1,0:T(8,128)(2,1)S(1)}, bf16[768,768]{1,0:T(8,128)(2,1)}, u32[]{:S(2)}) copy-start(bf16[768,768]{1,0:T(8,128)(2,1)} %param.26) | copy-start | bytes 3538948
  7.2 18.1 %copy-start.47 = (s32[1024,1]{0,1:T(1,128)S(1)}, s32[1024,1]{0,1:T(1,128)}, u32[]{:S(2)}) copy-start(s32[1024,1]{0,1:T(1,128)} %param.36) | copy-start | bytes 12292
  7.2 17.4 %copy-start.3 = (bf16[1024,768]{1,0:T(8,128)(2,1)S(1)}, bf16[1024,768]{1,0:T(8,128)(2,1)}, u32[]{:S(2)}) copy-start(bf16[1024,768]{1,0:T(8,128)(2,1)} %param.20) | copy-start | bytes 4718596
  7.2 23.0 %copy-start.74 = (s32[2,512]{1,0:T(2,128)S(1)}, s32[2,512]{1,0:T(2,128)}, u32[]{:S(2)}) copy-start(s32[2,512]{1,0:T(2,128)} %param.35) | copy-start | bytes 12292
  7.2 23.4 %copy-start.55 = (f32[768]{0:T(1024)S(1)}, f32[768]{0:T(1024)}, u32[]{:S(2)}) copy-start(f32[768]{0:T(1024)} %param.22) | copy-start | bytes 9220
  7.2 23.4 %copy-start.90 = (f32[768]{0:T(1024)S(1)}, f32[768]{0:T(1024)}, u32[]{:S(2)}) copy-start(f32[768]{0:T(1024)} %param.23) | copy-start | bytes 9220
  21.3 8.9 copy-start.69
  24.6 27.4 %copy-start.45 = (f32[1024]{0:T(1024)}, f32[1024]{0:T(1024)S(1)}, u32[]{:S(2)}) copy-start(f32[1024]{0:T(1024)S(1)} %broadcast_multiply_fusion.1) | copy-start | bytes 12292
  25.2 5.0 copy-start.64
  25.2 26.8 %copy-start.58 = (f32[1024]{0:T(1024)}, f32[1024]{0:T(1024)S(1)}, u32[]{:S(2)}) copy-start(f32[1024]{0:T(1024)S(1)} %fusion.112) | copy-start | bytes 12292
  30.2 72.6 %copy-start.49 = (s32[2048]{0:T(1024)}, s32[2048]{0:T(1024)S(1)}, u32[]{:S(2)}) copy-start(s32[2048]{0:T(1024)S(1)} %pad_clamp_fusion) | copy-start | bytes 24580
  30.6 54.0 %copy-start.12 = (pred[2,512,512]{1,2,0:T(8,128)(4,1)}, pred[2,512,512]{1,2,0:T(8,128)(4,1)S(1)}, u32[]{:S(2)}) copy-start(pred[2,512,512]{1,2,0:T(8,128)(4,1)S(1)} %broadcast_compare_fusion) | copy-start | bytes 1572868
  73.5 11.2 %copy-start.16 = (bf16[2,512,12,64]{1,0,3,2:T(2,128)(2,1)S(1)}, bf16[2,512,12,64]{1,0,3,2:T(2,128)(2,1)}, u32[]{:S(2)}) copy-start(bf16[2,512,12,64]{1,0,3,2:T(2,128)(2,1)} %reshape.255) | copy-start | bytes 4718596
  84.7 11.9 %copy-start.30 = (f32[2,12,512]{2,1,0:T(8,128)}, f32[2,12,512]{2,1,0:T(8,128)S(1)}, u32[]{:S(2)}) copy-start(f32[2,12,512]{2,1,0:T(8,128)S(1)} %log_add_fusion) | copy-start | bytes 147460
  108.4 72.7 %slice-start = ((s8[4718592]{0:T(1024)(128)(4,1)}), s8[4194304]{0:T(1024)(128)(4,1)S(1)}, s32[]{:S(2)}) async-start(s8[4718592]{0:T(1024)(128)(4,1)} %bitcast.243), calls=%async_computation.16 | async-start | bytes 8388608
  164.4 10.3 %copy-start.20 = (bf16[4,384,768]{2,1,0:T(8,128)(2,1)}, bf16[4,384,768]{2,1,0:T(8,128)(2,1)S(1)}, u32[]{:S(2)}) copy-start(bf16[4,384,768]{2,1,0:T(8,128)(2,1)S(1)} %all_to_all.20) | copy-start | bytes 7077892
  164.4 16.8 %slice-start.1 = ((s8[4718592]{0:T(1024)(128)(4,1)}), s8[524288]{0:T(1024)(128)(4,1)S(1)}, s32[]{:S(2)}) async-start(s8[4718592]{0:T(1024)(128)(4,1)} %bitcast.243), calls=%async_computation.17 | async-start | bytes 1048576
  174.7 6.5 copy-start.93
  229.2 6.0 copy-start.34
  229.2 6.0 copy-start.37
  229.2 6.0 copy-start.43
  229.2 6.0 copy-start.53
  229.2 56.4 %all-to-all-start.1 = ((bf16[4,384,768]{2,1,0:T(8,128)(2,1)}), bf16[4,384,768]{2,1,0:T(8,128)(2,1)S(1)}, u32[]{:S(2)}, u32[]{:S(2)}) async-start(bf16[4,384,768]{2,1,0:T(8,128)(2,1)} %fusion.56), calls=%async_computation.1 | async-start | bytes 4718592 | tf_op jit(solution)/shard_map/all_to_all | solution.py:159
  233.0 494.2 %reduce-scatter.18.cloned.1.call-start = ((), (), s32[]{:S(2)}) async-start(), calls=%async_computation.15 | async-start | bytes 5308416 | tf_op jit(solution)/shard_map/reduce_scatter | solution.py:211
  233.2 7.3 copy-start.81
  233.2 8.7 copy-start.80
  235.2 6.1 copy-start.83
  241.3 44.3 %copy-start.72 = (f32[1024]{0:T(1024)}, f32[1024]{0:T(1024)S(1)}, u32[]{:S(2)}) copy-start(f32[1024]{0:T(1024)S(1)} %get-tuple-element.140) | copy-start | bytes 12292
  241.9 55.0 %copy-start.51 = (f32[1024]{0:T(1024)}, f32[1024]{0:T(1024)S(1)}, u32[]{:S(2)}) copy-start(f32[1024]{0:T(1024)S(1)} %fusion.123) | copy-start | bytes 12292
  410.4 54.7 %copy-start.21 = (bf16[4,384,768]{2,1,0:T(8,128)(2,1)S(1)}, bf16[4,384,768]{2,1,0:T(8,128)(2,1)}, u32[]{:S(2)}) copy-start(bf16[4,384,768]{2,1,0:T(8,128)(2,1)} %copy-done.20) | copy-start | bytes 7077892
  410.4 319.0 %reduce-scatter.16.cloned.1.call-start = ((), (), s32[]{:S(2)}) async-start(), calls=%async_computation.14 | async-start | bytes 5308416 | tf_op jit(solution)/shard_map/reduce_scatter | solution.py:208
  486.9 5.0 copy-start.41
  486.9 56.6 %all-to-all-start.3 = ((bf16[4,384,768]{2,1,0:T(8,128)(2,1)}), bf16[4,384,768]{2,1,0:T(8,128)(2,1)S(1)}, u32[]{:S(2)}, u32[]{:S(2)}) async-start(bf16[4,384,768]{2,1,0:T(8,128)(2,1)} %fusion.59), calls=%async_computation.3 | async-start | bytes 4718592 | tf_op jit(solution)/shard_map/all_to_all | solution.py:200
  490.7 240.9 %reduce-scatter.14.cloned.1.call-start = ((), (), s32[]{:S(2)}) async-start(), calls=%async_computation.13 | async-start | bytes 2433024 | tf_op jit(solution)/shard_map/reduce_scatter | solution.py:265
  546.9 5.5 copy-start.35
  552.4 6.2 copy-start.67
  552.4 6.3 copy-start.2
  552.4 6.3 copy-start.11
  552.4 6.3 copy-start.38
  552.4 6.3 copy-start.44
  552.4 6.3 copy-start.63
  570.2 5.7 copy-start.17
  570.3 5.7 copy-start.13
  570.3 5.7 copy-start.31
  575.7 202.9 %reduce-scatter.12.cloned.1.call-start = ((), (), s32[]{:S(2)}) async-start(), calls=%async_computation.12 | async-start | bytes 2433024 | tf_op jit(solution)/shard_map/reduce_scatter | solution.py:264
  612.1 270.2 %reduce-scatter.10.cloned.1.call-start = ((), (), s32[]{:S(2)}) async-start(), calls=%async_computation.11 | async-start | bytes 2433024 | tf_op jit(solution)/shard_map/reduce_scatter | solution.py:263
  612.4 22.3 %copy-start.10 = (bf16[2,512,12,64]{1,0,3,2:T(2,128)(2,1)S(1)}, bf16[2,512,12,64]{1,0,3,2:T(2,128)(2,1)}, u32[]{:S(2)}) copy-start(bf16[2,512,12,64]{1,0,3,2:T(2,128)(2,1)} %reshape.256) | copy-start | bytes 4718596
  649.9 337.1 %reduce-scatter.8.cloned.1.call-start = ((), (), s32[]{:S(2)}) async-start(), calls=%async_computation.10 | async-start | bytes 2433024 | tf_op jit(solution)/shard_map/reduce_scatter | solution.py:262
  (56 other events, 127.0 us)
Sparse Core Ops, SparseCore 0:
  410.5 52.9 reduce-scatter.17
  474.5 52.9 reduce-scatter.15
  575.8 98.1 reduce-scatter.13
  680.6 97.9 reduce-scatter.11
  784.2 98.0 reduce-scatter.9
  888.9 97.9 reduce-scatter.7
where the time goes:
time: 1000 us; the launch traced here: 994 us
  waiting for transfers between devices  346 us (35%)
  matrix products  305 us (30%)
  blocking collectives  162 us (16%)
  local copies, waits for them, and re-layouts  92.5 us (9%)
  other arithmetic  61.4 us (6%)
  between operations  18 us (2%)
    reduce_scatter x1, waiting for transfers between devices, body(): lax.psum_scatter(query_full, ('dp', 'expert'), scatter_dimension=0, tiled...  105 us
    reduce_scatter x1, waiting for transfers between devices, body(): lax.psum_scatter(key_full, ('dp', 'expert'), scatter_dimension=0, tiled=T...  104 us
    all_to_all x1, blocking collectives, body(): lax.all_to_all(grad_out, 'expert', split_axis=0, concat_axis=0, tiled=True)  56.9 us
    all_to_all x1, blocking collectives, body(): lax.all_to_all(outgoing, 'expert', split_axis=0, concat_axis=0, tiled=True)  55.9 us
    dot_general x1, matrix products, body(): jnp.einsum('nemd,efd->nemf', grouped_grad, specialist_narrowing_matrix, p...  50.8 us
    unnamed x2, blocking collectives  49.5 us
    dot_general x1, matrix products, body(): jnp.einsum('nemf,nemd->efd', active_low, grouped_grad, preferred_element_...  48 us
    dot_general x1, matrix products, body(): jnp.einsum('nemf,efd->nemd', active, specialist_narrowing_matrix, preferr...  48 us
  transfers between devices with their start and end apart: 8, of which 5 were waited for; matrix products, arithmetic and copies ran while one was open for 22% of the time, Pallas kernels for 0%

commit v1 on v0

v1 whole, which is shorter than its diff:
```python
from functools import partial

import jax
import jax.numpy as jnp
from jax import lax
from jax.sharding import PartitionSpec as P

HEAD_DIM = 64


EPSILON = 1e-05
MASKED = -1e30


def layer_norm(values, norm_gain, norm_shift):
    centered = values - jnp.mean(values, axis=-1, keepdims=True)
    variance = jnp.mean(centered * centered, axis=-1, keepdims=True)
    return centered * lax.rsqrt(variance + EPSILON) * norm_gain + norm_shift


def routing_gate_value(normed, router_mat, embed_mat, temper_val, selected_expert):
    projected = jnp.dot(normed, router_mat, precision=lax.Precision.HIGHEST)
    unit_rows = projected * lax.rsqrt(jnp.sum(projected * projected, axis=-1, keepdims=True) + 1.0)
    unit_table = embed_mat * lax.rsqrt(jnp.sum(embed_mat * embed_mat, axis=-1, keepdims=True) + 1.0)
    logits = jnp.dot(unit_rows, unit_table.T, precision=lax.Precision.HIGHEST) / temper_val[0]
    routed = jax.nn.softmax(logits, axis=-1)
    return jnp.sum(routed * selected_expert, axis=-1)


def exact_gelu(values):
    return jax.nn.gelu(values, approximate=False)


def halves(axis):
    size = lax.axis_size(axis)
    bits = []
    mask = 1
    while mask < size:
        bits.append(mask)
        mask *= 2
    return bits


def swap(values, axis, mask):
    size = lax.axis_size(axis)
    return lax.ppermute(values, axis, [(i, i ^ mask) for i in range(size)])


def shift(values, axis, step):
    size = lax.axis_size(axis)
    return lax.ppermute(values, axis, [(i, (i + step) % size) for i in range(size)])


def pick(values, index, axis):
    return lax.dynamic_index_in_dim(values, index, axis, keepdims=False)


def scatter_sum_dp(values, order=None):
    size = lax.axis_size("dp")
    bits = halves("dp")
    place = lax.axis_index("dp")
    left = values.reshape((2,) * len(bits) + values.shape[1:])
    axes = list(reversed(bits))
    for mask in order or bits:
        axis = axes.index(mask)
        mine = (place // mask) % 2
        left = pick(left, mine, axis) + swap(pick(left, 1 - mine, axis), "dp", mask)
        axes.remove(mask)
    return left


def split_scatter_sum_dp(values):
    bits = halves("dp")
    if len(bits) != 3:
        return scatter_sum_dp(values)
    place = lax.axis_index("dp")
    left = values.reshape((2, 2, 2) + values.shape[1:])
    mine = place % 2
    left = pick(left, mine, 2) + swap(pick(left, 1 - mine, 2), "dp", 1)
    cut = values.shape[-1] // 2
    parts = []
    for order, part in (((2, 4), left[..., :cut]), ((4, 2), left[..., cut:])):
        axes = [4, 2]
        for mask in order:
            axis = axes.index(mask)
            mine = (place // mask) % 2
            part = pick(part, mine, axis) + swap(pick(part, 1 - mine, axis), "dp", mask)
            axes.remove(mask)
        parts.append(part)
    return jnp.concatenate(parts, axis=-1)


def scatter_sum_expert(values):
    size = lax.axis_size("expert")
    place = lax.axis_index("expert")
    total = pick(values, place, 0).astype(jnp.float32)
    if size > 8:
        return lax.psum_scatter(values, "expert", scatter_dimension=0, tiled=False).astype(
            jnp.float32
        )
    for step in range(1, size):
        block = pick(values, lax.rem(place + step, size), 0)
        total = total + shift(block, "expert", step).astype(jnp.float32)
    return total


def exchange(blocks, sign):
    size = lax.axis_size("expert")
    if size <= 8:
        return [blocks[0]] + [shift(blocks[k], "expert", sign * k) for k in range(1, size)]
    stacked = jnp.stack(blocks)
    place = lax.axis_index("expert")
    across = (jnp.arange(size) - place) * sign % size
    there = lax.all_to_all(stacked[across], "expert", 0, 0, tiled=True)
    source = (place - sign * jnp.arange(size)) % size
    home = there[source]
    return [home[k] for k in range(size)]


def body(
    layer_inputs_matrix,
    upstream_output_sensitivity,
    mixer_layernorm_scale,
    mixer_layernorm_offset,
    asker_matrix,
    lookup_label_matrix,
    content_matrix,
    mixer_result_matrix,
    specialist_layernorm_scale,
    specialist_layernorm_offset,
    dispatch_projection_matrix,
    specialist_centroids,
    learned_sharpness,
    specialist_widening_matrix,
    specialist_narrowing_matrix,
    document_labels,
    chosen_specialist,
    placement_ranks,
):
    rows_here, model_width = layer_inputs_matrix.shape
    seq_total, seq_len = document_labels.shape
    head_count = model_width // HEAD_DIM
    score_scale = HEAD_DIM ** (-0.5)
    group_size = lax.axis_size("expert")
    expert_total = group_size
    place = lax.axis_index("expert")
    capacity = rows_here
    slot_count = 3 * rows_here // (2 * expert_total)
    buffer_rows = expert_total * slot_count
    wide = specialist_widening_matrix[0]
    narrow = specialist_narrowing_matrix[0]
    chosen_ids = chosen_specialist[:, 0]
    expert_ids = lax.broadcasted_iota(jnp.int32, (rows_here, expert_total), 1)
    selected_expert = chosen_ids[:, None] == expert_ids
    chosen_int = selected_expert.astype(jnp.int32)
    order_row = placement_ranks[0]
    earlier_mask = (order_row[None, :] < order_row[:, None]).astype(jnp.bfloat16)
    ahead = jnp.dot(
        earlier_mask, selected_expert.astype(jnp.bfloat16), preferred_element_type=jnp.float32
    )
    rank_local = jnp.sum(jnp.where(selected_expert, ahead, 0.0), axis=-1).astype(jnp.int32)
    tallies = jnp.sum(chosen_int, axis=0)
    position = (chosen_ids - place) % group_size * slot_count + rank_local
    spots = jnp.arange(buffer_rows, dtype=jnp.int32)
    to_spots = spots[:, None] == position[None, :]
    from_spots = position[:, None] == spots[None, :]

    def send_out(rows):
        placed = jnp.dot(to_spots.astype(jnp.bfloat16), rows, preferred_element_type=jnp.float32)
        placed = placed.astype(jnp.bfloat16).reshape(expert_total, slot_count, model_width)
        return exchange([placed[k] for k in range(expert_total)], 1)

    def take_home(blocks):
        rows = jnp.concatenate(exchange(blocks, -1), axis=0)
        return jnp.dot(from_spots.astype(jnp.bfloat16), rows, preferred_element_type=jnp.float32)

    upstream_there = send_out(upstream_output_sensitivity)
    if group_size <= 8:
        prior = jnp.zeros_like(tallies)
        for step in range(1, group_size):
            prior = prior + jnp.where(place >= step, shift(tallies, "expert", step), 0)
    else:
        all_tallies = lax.all_gather(tallies, "expert")
        before = jnp.arange(group_size) < place
        prior = jnp.sum(jnp.where(before[:, None], all_tallies, 0), axis=0)
    slot_index = jnp.sum(chosen_int * prior[None, :], axis=-1) + rank_local
    kept_float = (slot_index < capacity).astype(jnp.float32)

    inputs = layer_inputs_matrix.astype(jnp.float32)
    normed_one, norm_one_back = jax.vjp(
        layer_norm, inputs, mixer_layernorm_scale, mixer_layernorm_offset
    )
    normed_low = normed_one.astype(jnp.bfloat16)

    def heads_of(weight_mat):
        projected = jnp.dot(normed_low, weight_mat, preferred_element_type=jnp.float32)
        return projected.astype(jnp.bfloat16).reshape(seq_total, seq_len, head_count, HEAD_DIM)

    queries = heads_of(asker_matrix)
    keys_low = heads_of(lookup_label_matrix)
    values_low = heads_of(content_matrix)
    allowed = (document_labels[:, :, None] == document_labels[:, None, :])[:, None]

    def raw_scores():
        scores = (
            jnp.einsum("sqhd,skhd->shqk", queries, keys_low, preferred_element_type=jnp.float32)
            * score_scale
        )
        return jnp.where(allowed, scores, MASKED)

    scores = raw_scores()
    largest = jnp.max(scores, axis=-1, keepdims=True)
    weights = jnp.exp(scores - largest)
    log_total = largest + jnp.log(jnp.sum(weights, axis=-1, keepdims=True))
    probs = jnp.exp(scores - log_total)
    attended = jnp.einsum(
        "shqk,skhd->sqhd",
        probs.astype(jnp.bfloat16),
        values_low,
        preferred_element_type=jnp.float32,
    )
    attended_low = attended.astype(jnp.bfloat16).reshape(rows_here, model_width)
    residual = inputs + jnp.dot(
        attended_low, mixer_result_matrix, preferred_element_type=jnp.float32
    )
    second_normalized, norm_two_back = jax.vjp(
        layer_norm, residual, specialist_layernorm_scale, specialist_layernorm_offset
    )
    entering = second_normalized.astype(jnp.bfloat16)
    entering_there = send_out(entering)
    selected_expert_float = selected_expert.astype(jnp.float32)
    gate, dispatcher_reverse = jax.vjp(
        partial(routing_gate_value, selected_expert=selected_expert_float),
        second_normalized,
        dispatch_projection_matrix,
        specialist_centroids,
        learned_sharpness,
    )
    weighted = gate * kept_float
    weight_spots = jnp.sum(jnp.where(to_spots, weighted[None, :], 0.0), axis=1)
    weight_spots = weight_spots.reshape(expert_total, slot_count)
    weight_there = exchange([weight_spots[k] for k in range(expert_total)], 1)

    ways = 4 if group_size == 4 else 1
    each = group_size // ways

    def gather_up(blocks):
        return [jnp.concatenate(blocks[k * each : (k + 1) * each]) for k in range(ways)]

    entered, graded, weighed = map(gather_up, (entering_there, upstream_there, weight_there))
    produced, returned, gate_parts, actives, pres = [], [], [], [], []
    for rows, grads in zip(entered, graded):
        hidden_pre = jnp.dot(rows, wide, preferred_element_type=jnp.float32)
        active, gelu_back = jax.vjp(exact_gelu, hidden_pre)
        active = active.astype(jnp.bfloat16)
        out = jnp.dot(active, narrow, preferred_element_type=jnp.float32)
        out = out.astype(jnp.bfloat16)
        gate_parts.append(jnp.sum(out.astype(jnp.float32) * grads.astype(jnp.float32), axis=-1))
        produced.append(out)
        active_grad = jnp.dot(grads, narrow.T, preferred_element_type=jnp.float32)
        pre_grad = gelu_back(active_grad)[0].astype(jnp.bfloat16)
        back = jnp.dot(pre_grad, wide.T, preferred_element_type=jnp.float32)
        returned.append(back.astype(jnp.bfloat16))
        actives.append(active)
        pres.append(pre_grad)

    def spread(chunks):
        return [chunk.reshape((each, -1) + chunk.shape[1:])[k] for chunk in chunks for k in range(each)]

    expert_input_grad = take_home(spread(returned))
    gate_rows = jnp.concatenate(exchange(spread(gate_parts), -1))
    gate_home = jnp.sum(jnp.where(from_spots, gate_rows[None, :], 0.0), axis=1)
    hidden_full = sum(
        jnp.dot(
            (rows.astype(jnp.float32) * w[:, None]).astype(jnp.bfloat16).T,
            p,
            preferred_element_type=jnp.float32,
        )
        for rows, w, p in zip(entered, weighed, pres)
    )
    return_full = sum(
        jnp.dot(
            a.T,
            (rows.astype(jnp.float32) * w[:, None]).astype(jnp.bfloat16),
            preferred_element_type=jnp.float32,
        )
        for rows, w, a in zip(graded, weighed, actives)
    )
    dp_size = lax.axis_size("dp")

    def expert_sum(full):
        blocks = full.astype(jnp.bfloat16).reshape((dp_size, -1) + full.shape[1:])
        return split_scatter_sum_dp(blocks).astype(jnp.float32)[None]

    hidden_grad = expert_sum(hidden_full)
    return_grad = expert_sum(return_full)
    per_token = take_home(spread(produced))
    layer_output = (residual + weighted[:, None] * per_token).astype(jnp.bfloat16)

    upstream = upstream_output_sensitivity.astype(jnp.float32)
    dispatcher_piece, dispatcher_complete, centroid_picked, sharpness_picked = dispatcher_reverse(
        gate_home * kept_float
    )
    two_part, routegain_full, routeshift_full = norm_two_back(
        expert_input_grad * weighted[:, None] + dispatcher_piece
    )
    residual_grad = upstream + two_part
    branch_grad = residual_grad.astype(jnp.bfloat16)
    outer_full = jnp.dot(attended_low.T, branch_grad, preferred_element_type=jnp.float32)
    attended_grad = jnp.dot(branch_grad, mixer_result_matrix.T, preferred_element_type=jnp.float32)
    attended_grad = attended_grad.astype(jnp.bfloat16).reshape(
        seq_total, seq_len, head_count, HEAD_DIM
    )
    probs = jnp.exp(raw_scores() - log_total)
    prob_grad = jnp.einsum(
        "sqhd,skhd->shqk", attended_grad, values_low, preferred_element_type=jnp.float32
    )
    values_grad = jnp.einsum(
        "shqk,sqhd->skhd",
        probs.astype(jnp.bfloat16),
        attended_grad,
        preferred_element_type=jnp.float32,
    )
    values_grad = values_grad.astype(jnp.bfloat16).reshape(rows_here, model_width)
    centered_grad = jnp.sum(prob_grad * probs, axis=-1, keepdims=True)
    score_grad = (probs * (prob_grad - centered_grad)).astype(jnp.bfloat16)
    queries_grad = (
        jnp.einsum("shqk,skhd->sqhd", score_grad, keys_low, preferred_element_type=jnp.float32)
        * score_scale
    )
    queries_grad = queries_grad.astype(jnp.bfloat16).reshape(rows_here, model_width)
    keys_grad = (
        jnp.einsum("shqk,sqhd->skhd", score_grad, queries, preferred_element_type=jnp.float32)
        * score_scale
    )
    keys_grad = keys_grad.astype(jnp.bfloat16).reshape(rows_here, model_width)
    query_full = jnp.dot(normed_low.T, queries_grad, preferred_element_type=jnp.float32)
    key_full = jnp.dot(normed_low.T, keys_grad, preferred_element_type=jnp.float32)
    value_full = jnp.dot(normed_low.T, values_grad, preferred_element_type=jnp.float32)
    one_grad = jnp.dot(queries_grad, asker_matrix.T, preferred_element_type=jnp.float32)
    one_grad = one_grad + jnp.dot(
        keys_grad, lookup_label_matrix.T, preferred_element_type=jnp.float32
    )
    one_grad = one_grad + jnp.dot(values_grad, content_matrix.T, preferred_element_type=jnp.float32)
    one_part, attngain_full, attnshift_full = norm_one_back(one_grad)
    tokens_grad = (residual_grad + one_part).astype(jnp.bfloat16)

    def full_sum(full):
        low = full.astype(jnp.bfloat16)
        blocks = low.reshape((dp_size, group_size, -1) + full.shape[1:])
        return scatter_sum_expert(split_scatter_sum_dp(blocks))

    outer_grad = full_sum(outer_full)
    query_grad = full_sum(query_full)
    key_grad = full_sum(key_full)
    value_grad = full_sum(value_full)
    small = jnp.concatenate(
        [
            dispatcher_complete.reshape(-1),
            routegain_full,
            routeshift_full,
            centroid_picked.reshape(-1),
            sharpness_picked,
        ]
    )
    small = lax.psum(small, ("dp", "expert"))
    norms = lax.psum(jnp.stack([attngain_full, attnshift_full]), ("dp", "expert"))
    devices = dp_size * group_size
    here = lax.axis_index("dp") * group_size + place
    own = model_width // devices
    route = dispatch_projection_matrix.shape[1]
    router_total = small[: model_width * route].reshape(model_width, route)
    rest = small[model_width * route :]
    mine = lambda vector, axis=0: lax.dynamic_slice_in_dim(vector, here * own, own, axis)
    centroid_total = rest[2 * model_width : 2 * model_width + expert_total * route]
    return (
        layer_output,
        tokens_grad,
        mine(norms[0]),
        mine(norms[1]),
        query_grad,
        key_grad,
        value_grad,
        outer_grad,
        mine(rest[:model_width]),
        mine(rest[model_width : 2 * model_width]),
        mine(router_total),
        centroid_total.reshape(expert_total, route),
        rest[2 * model_width + expert_total * route :],
        hidden_grad,
        return_grad,
    )


def solution(mesh):
    placed = (
        P(("dp", "expert"), None),
        P(("dp", "expert"), None),
        P(),
        P(),
        P(),
        P(),
        P(),
        P(),
        P(),
        P(),
        P(),
        P(),
        P(),
        P("expert", None, None),
        P("expert", None, None),
        P(("dp", "expert"), None),
        P(("dp", "expert"), None),
        P(("dp", "expert"), None),
    )
    return jax.shard_map(
        body,
        mesh=mesh,
        in_specs=placed,
        out_specs=(
            P(("dp", "expert"), None),
            P(("dp", "expert"), None),
            P(("dp", "expert")),
            P(("dp", "expert")),
            P(("dp", "expert"), None),
            P(("dp", "expert"), None),
            P(("dp", "expert"), None),
            P(("dp", "expert"), None),
            P(("dp", "expert")),
            P(("dp", "expert")),
            P(("dp", "expert"), None),
            P(),
            P(),
            P("expert", "dp", None),
            P("expert", "dp", None),
        ),
        check_vma=False,
    )
```

time: 1000 us -> 639 us (0.64)
  waiting for transfers between devices: 346 us -> 63.6 us
  blocking collectives: 162 us -> 40.1 us
  starting transfers between devices: 9.21 us -> 87.7 us
  local copies, waits for them, and re-layouts: 92.5 us -> 73.2 us
  between operations: 18 us -> 5.03 us
    reduce_scatter x6 -> x0, waiting for transfers between devices: 255 us -> none  [the longest x1 105 us: body(): lax.psum_scatter(query_full, ('dp', 'expert'), scatter_dimension=0, tiled...]
    all_to_all x2 -> x0, blocking collectives: 113 us -> none  [the longest x1 56.9 us: body(): lax.all_to_all(grad_out, 'expert', split_axis=0, concat_axis=0, tiled=True)]
    all_to_all x2 -> x0, waiting for transfers between devices: 90.3 us -> none  [the longest x1 47.2 us: body(): lax.all_to_all(input_back, 'expert', split_axis=0, concat_axis=0, tiled=T...]
    ppermute x0 -> x63, starting transfers between devices: none -> 87.7 us  [the longest x33 56.8 us: shift(): lax.ppermute(values, axis, [(i, (i + step) % size) for i in range(size)])]
    ppermute x0 -> x63, waiting for transfers between devices: none -> 63.6 us  [the longest x33 35.4 us: shift(): lax.ppermute(values, axis, [(i, (i + step) % size) for i in range(size)])]
    unnamed x2 -> x0, blocking collectives: 49.5 us -> none
    psum x0 -> x1, blocking collectives: none -> 40.1 us  [body(): lax.psum(jnp.stack([attngain_full, attnshift_full]), ('dp', 'expert'))]
    gather x4 -> x0, local copies, waits for them, and re-layouts: 22.2 us -> none  [the longest x1 5.65 us: body(): jnp.concatenate([entering, zero_row], axis=0)[source_rows]]
  transfers between devices with their start and end apart: 8 -> 63, of which waited for: 5 -> 18; matrix products, arithmetic and copies ran while one was open for 22% -> 68% of each run, Pallas kernels for 0% -> 0%
where the time goes in v1:
time: 639 us; the launch traced here: 635 us
  matrix products  302 us (47%)
  starting transfers between devices  87.7 us (14%)
  local copies, waits for them, and re-layouts  73.2 us (11%)
  waiting for transfers between devices  63.6 us (10%)
  other arithmetic  63.1 us (10%)
  blocking collectives  40.1 us (6%)
    ppermute x33, starting transfers between devices, shift(): lax.ppermute(values, axis, [(i, (i + step) % size) for i in range(size)])  56.8 us
    dot_general x4, matrix products, body(): hidden_pre = jnp.dot(rows, wide, preferred_element_type=jnp.float32)  55.4 us
    psum x1, blocking collectives, body(): lax.psum(jnp.stack([attngain_full, attnshift_full]), ('dp', 'expert'))  40.1 us
    ppermute x33, waiting for transfers between devices, shift(): lax.ppermute(values, axis, [(i, (i + step) % size) for i in range(size)])  35.4 us
    dot_general x4, matrix products, body(): jnp.dot(a.T, (rows.astype(jnp.float32) * w[:, None]).astype(jnp.bfloat16)...  33.6 us
    ppermute x30, starting transfers between devices, swap(): return lax.ppermute(values, axis, [(i, i ^ mask) for i in range(size)])  30.9 us
    ppermute x30, waiting for transfers between devices, swap(): return lax.ppermute(values, axis, [(i, i ^ mask) for i in range(size)])  28.2 us
    dot_general x4, matrix products, body(): jnp.dot((rows.astype(jnp.float32) * w[:, None]).astype(jnp.bfloat16).T, p...  27.7 us
  transfers between devices with their start and end apart: 63, of which 18 were waited for; matrix products, arithmetic and copies ran while one was open for 68% of the time, Pallas kernels for 0%

profile of v1, /device:TPU:0, one launch (start us, length us, event | category | flops | bytes accessed | tf_op | source)
XLA Modules:
  0.0 634.8 jit_solution(11441117389774266160)
XLA Ops:
  1.6 5.1 collective-permute-start.2
  10.0 4.5 fusion.71
  22.3 4.1 convolution_convert_fusion.3
  29.0 3.8 reshape.336
  32.9 4.1 convolution_convert_fusion.4
  39.6 3.9 reshape.335
  43.4 4.1 convolution_convert_fusion.5
  50.1 3.8 reshape.334
  54.0 12.3 %fusion = (f32[2,12,512]{2,1,0:T(8,128)S(1)}, f32[2,12,512,512]{2,3,1,0:T(8,128)}) fusion(pred[2,512,512]{1,2,0:T(8,128)(4,1)S(1)} %broadcast_compare_fusion, bf16[2,512,12,64]{1,0,3,2:T(2,128)(2,1)} %reshape.336, bf16[2,512,12,64]{1,0,3,2:T(2,128)(2,1)} %reshape.335), kind=kOutput, calls=%fused_computation.5 | convolution fusion | flops 824168448 | bytes 28884992 | tf_op jit(solution)/shard_map/sqhd,skhd->shqk/dot_general | solution.py:206
  66.3 11.1 %exponential_reduce_fusion = f32[2,12,512]{2,1,0:T(8,128)S(1)} fusion(f32[2,12,512,512]{2,3,1,0:T(8,128)} %get-tuple-element.125, f32[2,12,512]{2,1,0:T(8,128)S(1)} %get-tuple-element.124, pred[2,512,512]{1,2,0:T(8,128)(4,1)S(1)} %broadcast_compare_fusion), kind=kLoop, calls=%fused_computation.3 | loop fusion | flops 25153536 | bytes 25788416 | tf_op jit(solution)/shard_map/reduce_sum | solution.py:214
  77.5 11.6 %fusion.126 = bf16[2,512,12,64]{1,3,2,0:T(8,128)(2,1)S(1)} fusion(bf16[2,512,12,64]{1,0,3,2:T(2,128)(2,1)S(1)} %copy-done.15, f32[2,12,512,512]{2,3,1,0:T(8,128)} %get-tuple-element.125, f32[2,12,512]{2,1,0:T(8,128)S(1)} %log_add_fusion, pred[2,512,512]{1,2,0:T(8,128)(4,1)S(1)} %broadcast_compare_fusion), kind=kOutput, calls=%fused_computation.198 | convolution fusion | flops 831258624 | bytes 28884992 | tf_op jit(solution)/shard_map/shqk,skhd->sqhd/dot_general | solution.py:216
  103.6 12.9 %multiply_convert_fusion.4 = (bf16[384,3072]{1,0:T(8,128)(2,1)S(1)}, f32[384,3072]{1,0:T(8,128)S(1)}, f32[384,3072]{1,0:T(8,128)}) fusion(bf16[1,768,3072]{2,1,0:T(8,128)(2,1)S(1)} %bitcast.399, bf16[1536,768]{1,0:T(8,128)(2,1)S(1)} %fusion.70), kind=kOutput, calls=%fused_computation.109 | convolution fusion | flops 1888616448 | bytes 17104896 | tf_op jit(solution)/shard_map/dot_general | solution.py:253
  116.5 5.7 add_convert_fusion.5
  140.2 14.8 %multiply_convert_fusion.2 = (bf16[384,3072]{1,0:T(8,128)(2,1)S(1)}, f32[384,3072]{1,0:T(8,128)}, f32[384,3072]{1,0:T(8,128)}) fusion(bf16[384,768]{1,0:T(8,128)(2,1)} %copy-done.45, bf16[1,768,3072]{2,1,0:T(8,128)(2,1)} %param.31), kind=kOutput, calls=%fused_computation.83 | convolution fusion | flops 1888616448 | bytes 17104896 | tf_op jit(solution)/shard_map/dot_general | solution.py:253
  155.0 32.3 %collective-permute-done.11 = bf16[384,768]{1,0:T(8,128)(2,1)S(1)} collective-permute-done((bf16[384,768]{1,0:T(8,128)(2,1)}, bf16[384,768]{1,0:T(8,128)(2,1)S(1)}, u32[]{:S(2)}, u32[]{:S(2)}) %collective-permute-start.11) | collective-permute-done | bytes 589856 | tf_op jit(solution)/shard_map/ppermute | solution.py:51
  190.2 8.5 %collective-permute-start.6 = (bf16[384,768]{1,0:T(8,128)(2,1)}, bf16[384,768]{1,0:T(8,128)(2,1)}, u32[]{:S(2)}, u32[]{:S(2)}) collective-permute-start(bf16[384,768]{1,0:T(8,128)(2,1)} %get-tuple-element.133), channel_id=1, source_target_pairs={{0,2},{1,3},{2,0},{3,1},{4,6},{5,7},{6,4},{7,5},{8,10},{9,11},{10,... | collective-permute-start | bytes 1769480 | tf_op jit(solution)/shard_map/ppermute | solution.py:51
  198.7 14.2 %multiply_convert_fusion.1 = (bf16[384,3072]{1,0:T(8,128)(2,1)S(1)}, f32[384,3072]{1,0:T(8,128)S(1)}, f32[384,3072]{1,0:T(8,128)}) fusion(bf16[384,768]{1,0:T(8,128)(2,1)S(1)} %collective-permute-done.7, bf16[1,768,3072]{2,1,0:T(8,128)(2,1)} %param.31), kind=kOutput, calls=%fused_computation.70 | convolution fusion | flops 1888616448 | bytes 17104896 | tf_op jit(solution)/shard_map/dot_general | solution.py:253
  213.0 6.6 %add_convert_fusion.3 = bf16[384,3072]{1,0:T(8,128)(2,1)S(1)} fusion(f32[384,3072]{1,0:T(8,128)} %get-tuple-element.81, f32[384,3072]{1,0:T(8,128)} %get-tuple-element.131, bf16[384,768]{1,0:T(8,128)(2,1)S(1)} %collective-permute-done.11, bf16[1,3072,768]{2,1,0:T(8,128)(2,1)S(1)} %bitcast.397), kind=kOutput, calls=%fused_computation.67 | convolution fusion | flops 1828454400 | bytes 17104896 | tf_op jit(solution)/shard_map/dot_general | solution.py:260
  225.8 3.6 collective-permute-start.17
  229.3 13.5 %multiply_convert_fusion.3 = (bf16[384,3072]{1,0:T(8,128)(2,1)S(1)}, f32[384,3072]{1,0:T(8,128)}, f32[384,3072]{1,0:T(8,128)}) fusion(bf16[384,768]{1,0:T(8,128)(2,1)S(1)} %collective-permute-done.3, bf16[1,768,3072]{2,1,0:T(8,128)(2,1)S(1)} %bitcast.401), kind=kOutput, calls=%fused_computation.96 | convolution fusion | flops 1888616448 | bytes 17104896 | tf_op jit(solution)/shard_map/dot_general | solution.py:253
  242.9 5.8 add_convert_fusion.2
  251.7 4.0 fusion.166
  255.9 5.3 add_convert_fusion.4
  268.4 3.5 fusion.108
  272.0 4.3 fusion.262
  277.6 6.8 %fusion.190 = f32[3072,768]{1,0:T(8,128)} fusion(bf16[384,3072]{1,0:T(8,128)(2,1)S(1)} %copy-done.20, f32[384]{0:T(512)S(1)} %get-tuple-element.121, bf16[1536,768]{1,0:T(8,128)(2,1)} %copy-done.26), kind=kOutput, calls=%fused_computation.250 | convolution fusion | flops 1812824064 | bytes 12387840 | tf_op jit(solution)/shard_map/dot_general | solution.py:282
  284.5 6.3 fusion.178
  299.9 8.2 %fusion.188 = f32[3072,768]{1,0:T(8,128)} fusion(bf16[384,3072]{1,0:T(8,128)(2,1)} %copy-done.21, bf16[384,768]{1,0:T(8,128)(2,1)} %collective-permute-done.9, f32[384]{0:T(512)S(1)} %collective-permute-done.50), kind=kOutput, calls=%fused_computation.249 | convolution fusion | flops 1812824064 | bytes 12387840 | tf_op jit(solution)/shard_map/dot_general | solution.py:282
  308.1 5.3 fusion.179
  314.5 5.2 fusion.186
  319.8 5.2 fusion.180
  325.6 13.4 %add_convert_fusion = bf16[3072,768]{1,0:T(8,128)(2,1)} fusion(f32[3072,768]{1,0:T(8,128)} %fusion.186, f32[3072,768]{1,0:T(8,128)} %fusion.190, f32[3072,768]{1,0:T(8,128)} %fusion.188, bf16[384,3072]{1,0:T(8,128)(2,1)S(1)} %copy-done.23, bf16[384,768]{1,0:T(8,128)(2,1)S(1)} %copy-done.52, f32[384]{0:T(512)S(1)} %collective-permute-done.52), kind=kOutput, calls=%fused_computation.7 | convolution fusion | flops 1822261248 | bytes 35980800 | tf_op jit(solution)/shard_map/dot_general | solution.py:282
  339.0 10.9 %add_convert_fusion.1 = bf16[768,3072]{1,0:T(8,128)(2,1)S(1)} fusion(f32[768,3072]{1,0:T(8,128)} %fusion.180, f32[768,3072]{1,0:T(8,128)} %fusion.178, f32[768,3072]{1,0:T(8,128)} %fusion.179, bf16[384,3072]{1,0:T(8,128)(2,1)S(1)} %copy-done.25, bf16[384,768]{1,0:T(8,128)(2,1)S(1)} %copy-done.54, f32[384]{0:T(512)S(1)} %collective-permute-done.52), kind=kOutput, calls=%fused_computation.8 | convolution fusion | flops 1822261248 | bytes 35980800 | tf_op jit(solution)/shard_map/dot_general | solution.py:274
  350.0 5.0 dynamic-slice_bitcast_fusion
  358.3 5.7 multiply_reduce_fusion.1
  376.9 12.7 %fusion.127 = bf16[2,512,12,64]{1,3,2,0:T(8,128)(2,1)} fusion(bf16[2,512,12,64]{1,0,3,2:T(2,128)(2,1)} %reshape.338, f32[2,12,512,512]{2,3,1,0:T(8,128)} %get-tuple-element.125, f32[2,12,512]{2,1,0:T(8,128)S(1)} %copy-done.56, pred[2,512,512]{1,2,0:T(8,128)(4,1)S(1)} %copy-done.14), kind=kOutput, calls=%fused_computation.199 | convolution fusion | flops 831258624 | bytes 28884992 | tf_op jit(solution)/shard_map/shqk,sqhd->skhd/dot_general | solution.py:318
  389.6 18.1 %multiply_reduce_fusion = (f32[2,12,512]{2,1,0:T(8,128)S(1)}, f32[2,12,512,512]{2,3,1,0:T(8,128)}) fusion(f32[2,12,512,512]{2,3,1,0:T(8,128)} %get-tuple-element.125, f32[2,12,512]{2,1,0:T(8,128)S(1)} %copy-done.56, pred[2,512,512]{1,2,0:T(8,128)(4,1)S(1)} %copy-done.14, bf16[2,512,12,64]{1,0,3,2:T(2,128)(2,1)S(1)} %copy-done.16, ...), kind=kOutput, calls=%fused_computation.1 | convolution fusion | flops 836751360 | bytes 54099968 | tf_op jit(solution)/shard_map/sqhd,skhd->shqk/dot_general | solution.py:315
  407.7 21.9 %multiply_convert_fusion = bf16[2,12,512,512]{2,3,1,0:T(8,128)(2,1)} fusion(f32[2,12,512,512]{2,3,1,0:T(8,128)} %get-tuple-element.147, f32[2,12,512,512]{2,3,1,0:T(8,128)} %get-tuple-element.125, f32[2,12,512]{2,1,0:T(8,128)S(1)} %get-tuple-element.146, f32[2,12,512]{2,1,0:T(8,128)S(1)} %copy-done.56, pred[2,512,512]{1,2,0:T(8,128)(4,1)S(1)} %copy-done.14), kind=kLoop, calls=%fused_computation | loop fusion | flops 37748736 | bytes 63537152 | tf_op jit(solution)/shard_map/convert_element_type | solution.py:326
  429.7 9.7 %fusion.129 = bf16[2,512,12,64]{1,3,2,0:T(8,128)(2,1)} fusion(bf16[2,12,512,512]{2,3,1,0:T(8,128)(2,1)} %multiply_convert_fusion, bf16[2,512,12,64]{1,0,3,2:T(2,128)(2,1)S(1)} %copy-done.11), kind=kOutput, calls=%fused_computation.201 | convolution fusion | flops 806879232 | bytes 15728640 | tf_op jit(solution)/shard_map/shqk,sqhd->skhd/dot_general | solution.py:333
  439.4 6.8 %fusion.128 = bf16[2,512,12,64]{1,3,2,0:T(8,128)(2,1)S(1)} fusion(bf16[2,12,512,512]{2,3,1,0:T(8,128)(2,1)} %multiply_convert_fusion, bf16[2,512,12,64]{1,0,3,2:T(2,128)(2,1)S(1)} %copy-done.9), kind=kOutput, calls=%fused_computation.200 | convolution fusion | flops 806879232 | bytes 15728640 | tf_op jit(solution)/shard_map/shqk,skhd->sqhd/dot_general | solution.py:328
  463.7 40.1 %all-reduce = (f32[2,768]{1,0:T(2,128)S(1)}, f32[13889]{0:T(1024)S(1)}) all-reduce(f32[2,768]{1,0:T(2,128)S(1)} %pad_maximum_fusion.1, f32[13889]{0:T(1024)S(1)} %concatenate.59), channel_id=1, replica_groups=mesh['dp'=8,'expert'=4] {'dp','expert'}, use_global_device_ids=true, to_apply=%region_28.29 | all-reduce | flops 15425 | bytes 123400 | tf_op jit(solution)/shard_map/psum | solution.py:367
  504.5 4.2 convolution_convert_fusion.8
  508.7 5.7 add_convert_fusion.7
  524.4 5.9 add_convert_fusion.6
  592.2 4.1 collective-permute-start.25
  607.6 9.7 %collective-permute-done.61 = bf16[2,384,384]{2,1,0:T(8,128)(2,1)S(1)} collective-permute-done((bf16[2,384,384]{2,1,0:T(8,128)(2,1)S(1)}, bf16[2,384,384]{2,1,0:T(8,128)(2,1)S(1)}, u32[]{:S(2)}, u32[]{:S(2)}) %collective-permute-start.61) | collective-permute-done | bytes 589856 | tf_op jit(solution)/shard_map/ppermute | solution.py:46
  619.6 5.2 collective-permute-done.56
  627.1 5.1 collective-permute-done.57
  (559 shorter events, 204.8 us)
Async XLA Ops:
  1.6 131.4 %collective-permute-start.2 = (s32[4]{0:T(128)S(1)}, s32[4]{0:T(128)S(1)}, u32[]{:S(2)}, u32[]{:S(2)}) collective-permute-start(s32[4]{0:T(128)S(1)} %convert_reduce_fusion.1), channel_id=1, source_target_pairs={{0,3},{1,0},{2,1},{3,2},{4,7},{5,4},{6,5},{7,6},{8,11},{9,8},{10,9... | collective-permute-start | bytes 56 | tf_op jit(solution)/shard_map/ppermute | solution.py:51
  6.7 127.6 %collective-permute-start.1 = (s32[4]{0:T(128)S(1)}, s32[4]{0:T(128)S(1)}, u32[]{:S(2)}, u32[]{:S(2)}) collective-permute-start(s32[4]{0:T(128)S(1)} %convert_reduce_fusion.1), channel_id=1, source_target_pairs={{0,2},{1,3},{2,0},{3,1},{4,6},{5,7},{6,4},{7,5},{8,10},{9,11},{10,... | collective-permute-start | bytes 56 | tf_op jit(solution)/shard_map/ppermute | solution.py:51
  6.7 128.2 %collective-permute-start = (s32[4]{0:T(128)S(1)}, s32[4]{0:T(128)S(1)}, u32[]{:S(2)}, u32[]{:S(2)}) collective-permute-start(s32[4]{0:T(128)S(1)} %convert_reduce_fusion.1), channel_id=1, source_target_pairs={{0,1},{1,2},{2,3},{3,0},{4,5},{5,6},{6,7},{7,4},{8,9},{9,10},{10,1... | collective-permute-start | bytes 56 | tf_op jit(solution)/shard_map/ppermute | solution.py:51
  15.7 235.9 %collective-permute-start.9 = (bf16[384,768]{1,0:T(8,128)(2,1)}, bf16[384,768]{1,0:T(8,128)(2,1)}, u32[]{:S(2)}, u32[]{:S(2)}) collective-permute-start(bf16[384,768]{1,0:T(8,128)(2,1)} %get-tuple-element.93), channel_id=1, source_target_pairs={{0,1},{1,2},{2,3},{3,0},{4,5},{5,6},{6,7},{7,4},{8,9},{9,10},{10,1... | collective-permute-start | bytes 1769480 | tf_op jit(solution)/shard_map/ppermute | solution.py:51
  98.4 38.7 %collective-permute-start.5 = (bf16[384,768]{1,0:T(8,128)(2,1)}, bf16[384,768]{1,0:T(8,128)(2,1)S(1)}, u32[]{:S(2)}, u32[]{:S(2)}) collective-permute-start(bf16[384,768]{1,0:T(8,128)(2,1)} %get-tuple-element.92), channel_id=1, source_target_pairs={{0,2},{1,3},{2,0},{3,1},{4,6},{5,7},{6,4},{7,5},{8,10},{9,11},{10,... | collective-permute-start | bytes 1769480 | tf_op jit(solution)/shard_map/ppermute | solution.py:51
  132.9 89.6 %collective-permute-start.13 = (bf16[384,768]{1,0:T(8,128)(2,1)}, bf16[384,768]{1,0:T(8,128)(2,1)S(1)}, u32[]{:S(2)}, u32[]{:S(2)}) collective-permute-start(bf16[384,768]{1,0:T(8,128)(2,1)} %get-tuple-element.94), channel_id=1, source_target_pairs={{0,3},{1,0},{2,1},{3,2},{4,7},{5,4},{6,5},{7,6},{8,11},{9,8},{10,9... | collective-permute-start | bytes 1769480 | tf_op jit(solution)/shard_map/ppermute | solution.py:51
  134.3 53.0 %collective-permute-start.11 = (bf16[384,768]{1,0:T(8,128)(2,1)}, bf16[384,768]{1,0:T(8,128)(2,1)S(1)}, u32[]{:S(2)}, u32[]{:S(2)}) collective-permute-start(bf16[384,768]{1,0:T(8,128)(2,1)} %get-tuple-element.95), channel_id=1, source_target_pairs={{0,2},{1,3},{2,0},{3,1},{4,6},{5,7},{6,4},{7,5},{8,10},{9,11},{10,... | collective-permute-start | bytes 1769480 | tf_op jit(solution)/shard_map/ppermute | solution.py:51
  134.8 90.9 %collective-permute-start.3 = (bf16[384,768]{1,0:T(8,128)(2,1)}, bf16[384,768]{1,0:T(8,128)(2,1)S(1)}, u32[]{:S(2)}, u32[]{:S(2)}) collective-permute-start(bf16[384,768]{1,0:T(8,128)(2,1)} %get-tuple-element.90), channel_id=1, source_target_pairs={{0,1},{1,2},{2,3},{3,0},{4,5},{5,6},{6,7},{7,4},{8,9},{9,10},{10,1... | collective-permute-start | bytes 1769480 | tf_op jit(solution)/shard_map/ppermute | solution.py:51
  137.9 52.3 %collective-permute-start.7 = (bf16[384,768]{1,0:T(8,128)(2,1)}, bf16[384,768]{1,0:T(8,128)(2,1)S(1)}, u32[]{:S(2)}, u32[]{:S(2)}) collective-permute-start(bf16[384,768]{1,0:T(8,128)(2,1)} %get-tuple-element.91), channel_id=1, source_target_pairs={{0,3},{1,0},{2,1},{3,2},{4,7},{5,4},{6,5},{7,6},{8,11},{9,8},{10,9... | collective-permute-start | bytes 1769480 | tf_op jit(solution)/shard_map/ppermute | solution.py:51
  190.2 74.1 %collective-permute-start.16 = (f32[384]{0:T(512)S(1)}, f32[384]{0:T(512)S(1)}, u32[]{:S(2)}, u32[]{:S(2)}) collective-permute-start(f32[384]{0:T(512)S(1)} %get-tuple-element.132), channel_id=1, source_target_pairs={{0,2},{1,3},{2,0},{3,1},{4,6},{5,7},{6,4},{7,5},{8,10},{9,11},{10,... | collective-permute-start | bytes 4616 | tf_op jit(solution)/shard_map/ppermute | solution.py:51
  190.2 318.5 %collective-permute-start.6 = (bf16[384,768]{1,0:T(8,128)(2,1)}, bf16[384,768]{1,0:T(8,128)(2,1)}, u32[]{:S(2)}, u32[]{:S(2)}) collective-permute-start(bf16[384,768]{1,0:T(8,128)(2,1)} %get-tuple-element.133), channel_id=1, source_target_pairs={{0,2},{1,3},{2,0},{3,1},{4,6},{5,7},{6,4},{7,5},{8,10},{9,11},{10,... | collective-permute-start | bytes 1769480 | tf_op jit(solution)/shard_map/ppermute | solution.py:51
  222.6 133.9 %collective-permute-start.12 = (bf16[384,768]{1,0:T(8,128)(2,1)}, bf16[384,768]{1,0:T(8,128)(2,1)}, u32[]{:S(2)}, u32[]{:S(2)}) collective-permute-start(bf16[384,768]{1,0:T(8,128)(2,1)} %fusion.146), channel_id=1, source_target_pairs={{0,2},{1,3},{2,0},{3,1},{4,6},{5,7},{6,4},{7,5},{8,10},{9,11},{10,... | collective-permute-start | bytes 1769480 | tf_op jit(solution)/shard_map/ppermute | solution.py:51
  225.8 40.4 %collective-permute-start.17 = (f32[384]{0:T(512)S(1)}, f32[384]{0:T(512)S(1)}, u32[]{:S(2)}, u32[]{:S(2)}) collective-permute-start(f32[384]{0:T(512)S(1)} %get-tuple-element.129), channel_id=1, source_target_pairs={{0,1},{1,2},{2,3},{3,0},{4,5},{5,6},{6,7},{7,4},{8,9},{9,10},{10,1... | collective-permute-start | bytes 4616 | tf_op jit(solution)/shard_map/ppermute | solution.py:51
  255.6 10.6 %collective-permute-start.15 = (f32[384]{0:T(512)S(1)}, f32[384]{0:T(512)S(1)}, u32[]{:S(2)}, u32[]{:S(2)}) collective-permute-start(f32[384]{0:T(512)S(1)} %get-tuple-element.135), channel_id=1, source_target_pairs={{0,3},{1,0},{2,1},{3,2},{4,7},{5,4},{6,5},{7,6},{8,11},{9,8},{10,9... | collective-permute-start | bytes 4616 | tf_op jit(solution)/shard_map/ppermute | solution.py:51
  264.3 244.3 %collective-permute-start.8 = (bf16[384,768]{1,0:T(8,128)(2,1)}, bf16[384,768]{1,0:T(8,128)(2,1)}, u32[]{:S(2)}, u32[]{:S(2)}) collective-permute-start(bf16[384,768]{1,0:T(8,128)(2,1)} %get-tuple-element.130), channel_id=1, source_target_pairs={{0,1},{1,2},{2,3},{3,0},{4,5},{5,6},{6,7},{7,4},{8,9},{9,10},{10,1... | collective-permute-start | bytes 1769480 | tf_op jit(solution)/shard_map/ppermute | solution.py:51
  266.2 91.6 %collective-permute-start.14 = (bf16[384,768]{1,0:T(8,128)(2,1)}, bf16[384,768]{1,0:T(8,128)(2,1)}, u32[]{:S(2)}, u32[]{:S(2)}) collective-permute-start(bf16[384,768]{1,0:T(8,128)(2,1)} %fusion.149), channel_id=1, source_target_pairs={{0,1},{1,2},{2,3},{3,0},{4,5},{5,6},{6,7},{7,4},{8,9},{9,10},{10,1... | collective-permute-start | bytes 1769480 | tf_op jit(solution)/shard_map/ppermute | solution.py:51
  291.1 5.6 collective-permute-start.50
  296.7 16.6 %collective-permute-start.51 = (f32[384]{0:T(512)}, f32[384]{0:T(512)S(1)}, u32[]{:S(2)}, u32[]{:S(2)}) collective-permute-start(f32[384]{0:T(512)} %get-tuple-element.119), channel_id=1, source_target_pairs={{0,2},{1,3},{2,0},{3,1},{4,6},{5,7},{6,4},{7,5},{8,10},{9,11},{10,... | collective-permute-start | bytes 4616 | tf_op jit(solution)/shard_map/ppermute | solution.py:51
  313.4 11.6 %collective-permute-start.52 = (f32[384]{0:T(512)S(1)}, f32[384]{0:T(512)S(1)}, u32[]{:S(2)}, u32[]{:S(2)}) collective-permute-start(f32[384]{0:T(512)S(1)} %copy-done.106), channel_id=1, source_target_pairs={{0,3},{1,0},{2,1},{3,2},{4,7},{5,4},{6,5},{7,6},{8,11},{9,8},{10,9... | collective-permute-start | bytes 4616 | tf_op jit(solution)/shard_map/ppermute | solution.py:51
  325.0 32.8 %collective-permute-start.10 = (bf16[384,768]{1,0:T(8,128)(2,1)}, bf16[384,768]{1,0:T(8,128)(2,1)}, u32[]{:S(2)}, u32[]{:S(2)}) collective-permute-start(bf16[384,768]{1,0:T(8,128)(2,1)} %fusion.143), channel_id=1, source_target_pairs={{0,3},{1,0},{2,1},{3,2},{4,7},{5,4},{6,5},{7,6},{8,11},{9,8},{10,9... | collective-permute-start | bytes 1769480 | tf_op jit(solution)/shard_map/ppermute | solution.py:51
  356.5 152.2 %collective-permute-start.4 = (bf16[384,768]{1,0:T(8,128)(2,1)}, bf16[384,768]{1,0:T(8,128)(2,1)}, u32[]{:S(2)}, u32[]{:S(2)}) collective-permute-start(bf16[384,768]{1,0:T(8,128)(2,1)} %get-tuple-element.136), channel_id=1, source_target_pairs={{0,3},{1,0},{2,1},{3,2},{4,7},{5,4},{6,5},{7,6},{8,11},{9,8},{10,9... | collective-permute-start | bytes 1769480 | tf_op jit(solution)/shard_map/ppermute | solution.py:51
  357.8 240.8 %collective-permute-start.58 = (bf16[2,2,384,768]{3,2,1,0:T(8,128)(2,1)}, bf16[2,2,384,768]{3,2,1,0:T(8,128)(2,1)}, u32[]{:S(2)}, u32[]{:S(2)}) collective-permute-start(bf16[2,2,384,768]{3,2,1,0:T(8,128)(2,1)} %dynamic-slice_bitcast_fusion), channel_id=1, source_target_pairs={{0,4},{4,0},{8,12},{12,8},{16,20},{20,16},{24,28},{28,24},{1,5},{5... | collective-permute-start | bytes 7077896 | tf_op jit(solution)/shard_map/ppermute | solution.py:46
  357.8 245.3 %collective-permute-start.53 = (bf16[2,2,96,3072]{3,2,1,0:T(8,128)(2,1)}, bf16[2,2,96,3072]{3,2,1,0:T(8,128)(2,1)}, u32[]{:S(2)}, u32[]{:S(2)}) collective-permute-start(bf16[2,2,96,3072]{3,2,1,0:T(8,128)(2,1)} %dynamic-slice_bitcast_fusion.1), channel_id=1, source_target_pairs={{0,4},{4,0},{8,12},{12,8},{16,20},{20,16},{24,28},{28,24},{1,5},{5... | collective-permute-start | bytes 7077896 | tf_op jit(solution)/shard_map/ppermute | solution.py:46
  518.9 20.7 %collective-permute-start.42 = (bf16[2,2,4,24,768]{4,3,2,1,0:T(8,128)(2,1)}, bf16[2,2,4,24,768]{4,3,2,1,0:T(8,128)(2,1)}, u32[]{:S(2)}, u32[]{:S(2)}) collective-permute-start(bf16[2,2,4,24,768]{4,3,2,1,0:T(8,128)(2,1)} %dynamic-slice_bitcast_fusion.6), channel_id=1, source_target_pairs={{0,4},{4,0},{8,12},{12,8},{16,20},{20,16},{24,28},{28,24},{1,5},{5... | collective-permute-start | bytes 1769480 | tf_op jit(solution)/shard_map/ppermute | solution.py:46
  520.8 20.6 %collective-permute-start.34 = (bf16[2,2,4,24,768]{4,3,2,1,0:T(8,128)(2,1)}, bf16[2,2,4,24,768]{4,3,2,1,0:T(8,128)(2,1)}, u32[]{:S(2)}, u32[]{:S(2)}) collective-permute-start(bf16[2,2,4,24,768]{4,3,2,1,0:T(8,128)(2,1)} %dynamic-slice_bitcast_fusion.7), channel_id=1, source_target_pairs={{0,4},{4,0},{8,12},{12,8},{16,20},{20,16},{24,28},{28,24},{1,5},{5... | collective-permute-start | bytes 1769480 | tf_op jit(solution)/shard_map/ppermute | solution.py:46
  522.4 22.6 %collective-permute-start.26 = (bf16[2,2,4,24,768]{4,3,2,1,0:T(8,128)(2,1)S(1)}, bf16[2,2,4,24,768]{4,3,2,1,0:T(8,128)(2,1)}, u32[]{:S(2)}, u32[]{:S(2)}) collective-permute-start(bf16[2,2,4,24,768]{4,3,2,1,0:T(8,128)(2,1)S(1)} %dynamic-slice_bitcast_fusion.8), channel_id=1, source_target_pairs={{0,4},{4,0},{8,12},{12,8},{16,20},{20,16},{24,28},{28,24},{1,5},{5... | collective-permute-start | bytes 1769480 | tf_op jit(solution)/shard_map/ppermute | solution.py:46
  539.6 7.4 %collective-permute-start.18 = (bf16[2,2,4,24,768]{4,3,2,1,0:T(8,128)(2,1)S(1)}, bf16[2,2,4,24,768]{4,3,2,1,0:T(8,128)(2,1)S(1)}, u32[]{:S(2)}, u32[]{:S(2)}) collective-permute-start(bf16[2,2,4,24,768]{4,3,2,1,0:T(8,128)(2,1)S(1)} %dynamic-slice_bitcast_fusion.9), channel_id=1, source_target_pairs={{0,4},{4,0},{8,12},{12,8},{16,20},{20,16},{24,28},{28,24},{1,5},{5... | collective-permute-start | bytes 1769480 | tf_op jit(solution)/shard_map/ppermute | solution.py:46
  541.5 7.3 %collective-permute-start.43 = (bf16[2,4,24,384]{3,2,1,0:T(8,128)(2,1)S(1)}, bf16[2,4,24,384]{3,2,1,0:T(8,128)(2,1)S(1)}, u32[]{:S(2)}, u32[]{:S(2)}) collective-permute-start(bf16[2,4,24,384]{3,2,1,0:T(8,128)(2,1)S(1)} %dynamic-slice_bitcast_fusion.15), channel_id=1, source_target_pairs={{0,8},{4,12},{8,0},{12,4},{16,24},{20,28},{24,16},{28,20},{1,9},{5... | collective-permute-start | bytes 442376 | tf_op jit(solution)/shard_map/ppermute | solution.py:46
  545.0 8.8 %collective-permute-start.45 = (bf16[2,4,24,384]{3,2,1,0:T(8,128)(2,1)S(1)}, bf16[2,4,24,384]{3,2,1,0:T(8,128)(2,1)S(1)}, u32[]{:S(2)}, u32[]{:S(2)}) collective-permute-start(bf16[2,4,24,384]{3,2,1,0:T(8,128)(2,1)S(1)} %dynamic-slice_bitcast_fusion.14), channel_id=1, source_target_pairs={{0,16},{4,20},{8,24},{12,28},{16,0},{20,4},{24,8},{28,12},{1,17},{... | collective-permute-start | bytes 442376 | tf_op jit(solution)/shard_map/ppermute | solution.py:46
  552.3 6.1 collective-permute-start.27
  553.8 6.7 %collective-permute-start.29 = (bf16[2,4,24,384]{3,2,1,0:T(8,128)(2,1)S(1)}, bf16[2,4,24,384]{3,2,1,0:T(8,128)(2,1)S(1)}, u32[]{:S(2)}, u32[]{:S(2)}) collective-permute-start(bf16[2,4,24,384]{3,2,1,0:T(8,128)(2,1)S(1)} %dynamic-slice_bitcast_fusion.18), channel_id=1, source_target_pairs={{0,16},{4,20},{8,24},{12,28},{16,0},{20,4},{24,8},{28,12},{1,17},{... | collective-permute-start | bytes 442376 | tf_op jit(solution)/shard_map/ppermute | solution.py:46
  554.3 6.4 %collective-permute-start.19 = (bf16[2,4,24,384]{3,2,1,0:T(8,128)(2,1)S(1)}, bf16[2,4,24,384]{3,2,1,0:T(8,128)(2,1)S(1)}, u32[]{:S(2)}, u32[]{:S(2)}) collective-permute-start(bf16[2,4,24,384]{3,2,1,0:T(8,128)(2,1)S(1)} %dynamic-slice_bitcast_fusion.21), channel_id=1, source_target_pairs={{0,8},{4,12},{8,0},{12,4},{16,24},{20,28},{24,16},{28,20},{1,9},{5... | collective-permute-start | bytes 442376 | tf_op jit(solution)/shard_map/ppermute | solution.py:46
  560.7 6.6 %collective-permute-start.46 = (bf16[4,24,384]{2,1,0:T(8,128)(2,1)S(1)}, bf16[4,24,384]{2,1,0:T(8,128)(2,1)S(1)}, u32[]{:S(2)}, u32[]{:S(2)}) collective-permute-start(bf16[4,24,384]{2,1,0:T(8,128)(2,1)S(1)} %dynamic-slice_bitcast_fusion.22), channel_id=1, source_target_pairs={{0,8},{4,12},{8,0},{12,4},{16,24},{20,28},{24,16},{28,20},{1,9},{5... | collective-permute-start | bytes 221192 | tf_op jit(solution)/shard_map/ppermute | solution.py:46
  573.1 6.3 collective-permute-start.47
  579.4 6.1 collective-permute-start.39
  580.1 5.6 collective-permute-start.40
  585.5 5.8 collective-permute-start.31
  591.2 5.8 collective-permute-start.23
  591.2 5.8 collective-permute-start.24
  592.2 5.8 collective-permute-start.25
  600.9 16.3 %collective-permute-start.61 = (bf16[2,384,384]{2,1,0:T(8,128)(2,1)S(1)}, bf16[2,384,384]{2,1,0:T(8,128)(2,1)S(1)}, u32[]{:S(2)}, u32[]{:S(2)}) collective-permute-start(bf16[2,384,384]{2,1,0:T(8,128)(2,1)S(1)} %dynamic-slice_bitcast_fusion.2), channel_id=1, source_target_pairs={{0,16},{4,20},{8,24},{12,28},{16,0},{20,4},{24,8},{28,12},{1,17},{... | collective-permute-start | bytes 1769480 | tf_op jit(solution)/shard_map/ppermute | solution.py:46
  602.3 16.5 %collective-permute-start.59 = (bf16[2,384,384]{2,1,0:T(8,128)(2,1)S(1)}, bf16[2,384,384]{2,1,0:T(8,128)(2,1)S(1)}, u32[]{:S(2)}, u32[]{:S(2)}) collective-permute-start(bf16[2,384,384]{2,1,0:T(8,128)(2,1)S(1)} %dynamic-slice_bitcast_fusion.3), channel_id=1, source_target_pairs={{0,8},{4,12},{8,0},{12,4},{16,24},{20,28},{24,16},{28,20},{1,9},{5... | collective-permute-start | bytes 1769480 | tf_op jit(solution)/shard_map/ppermute | solution.py:46
  605.3 19.5 %collective-permute-start.56 = (bf16[2,96,1536]{2,1,0:T(8,128)(2,1)S(1)}, bf16[2,96,1536]{2,1,0:T(8,128)(2,1)S(1)}, u32[]{:S(2)}, u32[]{:S(2)}) collective-permute-start(bf16[2,96,1536]{2,1,0:T(8,128)(2,1)S(1)} %dynamic-slice_bitcast_fusion.4), channel_id=1, source_target_pairs={{0,16},{4,20},{8,24},{12,28},{16,0},{20,4},{24,8},{28,12},{1,17},{... | collective-permute-start | bytes 1769480 | tf_op jit(solution)/shard_map/ppermute | solution.py:46
  606.8 19.5 %collective-permute-start.54 = (bf16[2,96,1536]{2,1,0:T(8,128)(2,1)S(1)}, bf16[2,96,1536]{2,1,0:T(8,128)(2,1)S(1)}, u32[]{:S(2)}, u32[]{:S(2)}) collective-permute-start(bf16[2,96,1536]{2,1,0:T(8,128)(2,1)S(1)} %dynamic-slice_bitcast_fusion.5), channel_id=1, source_target_pairs={{0,8},{4,12},{8,0},{12,4},{16,24},{20,28},{24,16},{28,20},{1,9},{5... | collective-permute-start | bytes 1769480 | tf_op jit(solution)/shard_map/ppermute | solution.py:46
  617.4 14.8 %collective-permute-start.62 = (bf16[384,384]{1,0:T(8,128)(2,1)S(1)}, bf16[384,384]{1,0:T(8,128)(2,1)S(1)}, u32[]{:S(2)}, u32[]{:S(2)}) collective-permute-start(bf16[384,384]{1,0:T(8,128)(2,1)S(1)} %dynamic-slice_bitcast_fusion.10), channel_id=1, source_target_pairs={{0,8},{4,12},{8,0},{12,4},{16,24},{20,28},{24,16},{28,20},{1,9},{5... | collective-permute-start | bytes 884744 | tf_op jit(solution)/shard_map/ppermute | solution.py:46
  618.9 13.4 %collective-permute-start.60 = (bf16[384,384]{1,0:T(8,128)(2,1)S(1)}, bf16[384,384]{1,0:T(8,128)(2,1)S(1)}, u32[]{:S(2)}, u32[]{:S(2)}) collective-permute-start(bf16[384,384]{1,0:T(8,128)(2,1)S(1)} %dynamic-slice_bitcast_fusion.11), channel_id=1, source_target_pairs={{0,16},{4,20},{8,24},{12,28},{16,0},{20,4},{24,8},{28,12},{1,17},{... | collective-permute-start | bytes 884744 | tf_op jit(solution)/shard_map/ppermute | solution.py:46
  624.9 7.3 %collective-permute-start.57 = (bf16[96,1536]{1,0:T(8,128)(2,1)S(1)}, bf16[96,1536]{1,0:T(8,128)(2,1)S(1)}, u32[]{:S(2)}, u32[]{:S(2)}) collective-permute-start(bf16[96,1536]{1,0:T(8,128)(2,1)S(1)} %dynamic-slice_bitcast_fusion.12), channel_id=1, source_target_pairs={{0,8},{4,12},{8,0},{12,4},{16,24},{20,28},{24,16},{28,20},{1,9},{5... | collective-permute-start | bytes 884744 | tf_op jit(solution)/shard_map/ppermute | solution.py:46
  626.4 7.0 %collective-permute-start.55 = (bf16[96,1536]{1,0:T(8,128)(2,1)S(1)}, bf16[96,1536]{1,0:T(8,128)(2,1)S(1)}, u32[]{:S(2)}, u32[]{:S(2)}) collective-permute-start(bf16[96,1536]{1,0:T(8,128)(2,1)S(1)} %dynamic-slice_bitcast_fusion.13), channel_id=1, source_target_pairs={{0,16},{4,20},{8,24},{12,28},{16,0},{20,4},{24,8},{28,12},{1,17},{... | collective-permute-start | bytes 884744 | tf_op jit(solution)/shard_map/ppermute | solution.py:46
  (146 other events, 1712.3 us)

commit v2 on v0

v2 whole, which is shorter than its diff:
```python
from functools import partial

import jax
import jax.numpy as jnp
from jax import lax
from jax.experimental import pallas as pl
from jax.experimental.pallas import tpu as pltpu
from jax.sharding import PartitionSpec as P

HEAD_DIM = 64
EPSILON = 1e-05
MASKED = -1e30
BF = jnp.bfloat16
F32 = jnp.float32
VMEM_LIMIT = 56 * 1024 * 1024
TAIL = 16
COST = 1
NN = (((1,), (0,)), ((), ()))
NT = (((1,), (1,)), ((), ()))
TN = (((0,), (0,)), ((), ()))


def mxu(left, right, dims=NN):
    return lax.dot_general(left, right, dims, preferred_element_type=F32)


def split_high(values):
    high = values.astype(BF)
    low = (values - high.astype(F32)).astype(BF)
    return high, low


def mxu_wide(left, right, dims=NN):
    left_high, left_low = split_high(left)
    right_high, right_low = split_high(right)
    return (
        mxu(left_high, right_high, dims)
        + mxu(left_high, right_low, dims)
        + mxu(left_low, right_high, dims)
    )


def kernel_call(body, cost, deps=(), **kwargs):
    deps = jax.tree.leaves(deps)
    inputs = len(kwargs["in_specs"])
    kwargs["in_specs"] = list(kwargs["in_specs"]) + [pl.BlockSpec(memory_space=pl.ANY)] * len(deps)

    def run(*refs):
        body(*refs[:inputs], *refs[inputs + len(deps) :])

    call = pl.pallas_call(
        run,
        compiler_params=pltpu.CompilerParams(
            vmem_limit_bytes=VMEM_LIMIT,
            dimension_semantics=("arbitrary",) * len(kwargs.get("grid", ())),
        ),
        cost_estimate=pl.CostEstimate(flops=cost[0] // COST, bytes_accessed=cost[1] // COST, transcendentals=0),
        **kwargs,
    )
    return lambda *args: call(*args, *deps)


def whole(shape):
    return pl.BlockSpec(shape, lambda *_: (0,) * len(shape))


def route_kernel(slots, place_ref, order_ref, chosen_ref, rows_ref, pos_ref, rank_ref, sent_ref):
    group = sent_ref.shape[0]
    order = order_ref[...].astype(F32)
    count = order.shape[1]
    chosen = chosen_ref[...]
    chosen_wide = jnp.transpose(jnp.broadcast_to(chosen.astype(F32), (128, count)))
    order_col = jnp.transpose(jnp.broadcast_to(order, (128, count)))[:, :1]
    before = (order_col < order) & (chosen_wide[:, :1] == chosen.astype(F32))
    rank = jnp.sum(before.astype(F32), axis=0, keepdims=True).astype(jnp.int32)
    place = place_ref[0]
    pos = jnp.where(chosen >= place, chosen - place, chosen - place + group) * slots + rank
    pos_ref[...] = pos
    rank_ref[...] = rank
    lanes = lax.broadcasted_iota(jnp.int32, (count, 128), 1).astype(F32)
    rows = rows_ref[...]
    tally = jnp.sum((chosen_wide == lanes).astype(F32), axis=0, keepdims=True)
    upper = jnp.floor(tally * (1.0 / 256.0))
    place_row = lax.broadcasted_iota(jnp.int32, (TAIL, 128), 0)
    tail = jnp.where(place_row == 0, upper, jnp.where(place_row == 1, tally - 256.0 * upper, 0.0))
    tail = jnp.concatenate([tail, jnp.zeros((TAIL, rows.shape[1] - 128), F32)], axis=1).astype(BF)
    for k in range(group):
        spots = lax.broadcasted_iota(jnp.int32, (slots, count), 0) + k * slots
        sent_ref[k, :slots, :] = mxu((spots == chosen * slots + rank).astype(F32).astype(BF), rows).astype(BF)
        sent_ref[k, slots:, :] = tail


def norm_of(values, gain, shift):
    centered = values - jnp.mean(values, axis=-1, keepdims=True)
    scale = lax.rsqrt(jnp.mean(centered * centered, axis=-1, keepdims=True) + EPSILON)
    unit = centered * scale
    return unit, scale, unit * gain + shift


def router_of(projected, table, temper):
    scale = lax.rsqrt(jnp.sum(projected * projected, axis=0, keepdims=True) + 1.0)
    unit = projected * scale
    table_scale = lax.rsqrt(jnp.sum(table * table, axis=1, keepdims=True) + 1.0)
    unit_table = table * table_scale
    logits = lax.dot_general(
        unit_table, unit, NN, precision=lax.Precision.HIGHEST, preferred_element_type=F32
    ) / temper
    return scale, unit, table_scale, unit_table, logits


def softmax_rows(logits, experts):
    valid = lax.broadcasted_iota(jnp.int32, logits.shape, 0) < experts
    logits = jnp.where(valid, logits, MASKED)
    weights = jnp.exp(logits - jnp.max(logits, axis=0, keepdims=True))
    return weights / jnp.sum(weights, axis=0, keepdims=True)


def same_label(label_ref):
    labels = label_ref[0].astype(F32)
    column = jnp.transpose(jnp.broadcast_to(labels, (128, labels.shape[1])))[:, :1]
    return jnp.where(column == labels, 0.0, MASKED)


def attend_kernel(experts, slots, x_ref, label_ref, gain_one_ref, shift_one_ref, wq_ref,
                  wk_ref, wv_ref, wo_ref, gain_two_ref, shift_two_ref, router_ref, table_ref, temper_ref,
                  chosen_ref, pos_ref, turned_ref, q_ref, k_ref, v_ref, att_ref, lse_ref, residual_ref,
                  projected_ref, *rest):
    sent_refs, bias_ref, lse_cols_ref = rest[:-2], rest[-2], rest[-1]
    step = pl.program_id(0)
    x = x_ref[...].astype(F32)
    rows, width = x.shape
    normed = norm_of(x, gain_one_ref[...], shift_one_ref[...])[2].astype(BF)
    turned_ref[...] = jnp.transpose(normed)
    q_ref[...] = (mxu(normed, wq_ref[...]).astype(BF).astype(F32) * HEAD_DIM ** (-0.5)).astype(BF)
    k_ref[...] = mxu(normed, wk_ref[...]).astype(BF)
    v_ref[...] = mxu(normed, wv_ref[...]).astype(BF)
    bias_ref[...] = same_label(label_ref)
    lane = lax.broadcasted_iota(jnp.int32, (rows, 128), 1)
    low_lanes = lane < HEAD_DIM
    lse_cols = jnp.zeros((rows, 128), F32)
    for pair in range(width // 128):
        columns = slice(pair * 128, pair * 128 + 128)
        q_pair, k_pair, v_pair = q_ref[:, columns], k_ref[:, columns], v_ref[:, columns]
        outs = []
        for half in range(2):
            own = low_lanes if half == 0 else jnp.logical_not(low_lanes)
            q_own = jnp.where(own, q_pair.astype(F32), 0.0).astype(BF)
            scores = mxu(q_own, k_pair, NT) + bias_ref[...]
            largest = jnp.max(scores, axis=-1, keepdims=True)
            weights = jnp.exp(scores - largest)
            total = jnp.sum(weights, axis=-1, keepdims=True)
            outs.append(mxu(weights.astype(BF), v_pair) * (1.0 / total))
            lse_cols = jnp.where(lane == pair * 2 + half, largest + jnp.log(total), lse_cols)
        att_ref[:, columns] = jnp.where(low_lanes, outs[0], outs[1]).astype(BF)
    lse_cols_ref[...] = lse_cols
    lse_ref[...] = jnp.transpose(lse_cols_ref[...])[: lse_ref.shape[0]]
    residual = x + mxu(att_ref[...], wo_ref[...])
    residual_ref[...] = residual
    normed_two = norm_of(residual, gain_two_ref[...], shift_two_ref[...])[2]
    projected = lax.dot_general(
        router_ref[...], normed_two, NT, precision=lax.Precision.HIGHEST, preferred_element_type=F32
    )
    projected_ref[...] = projected
    logits = router_of(projected, table_ref[...], temper_ref[0])[4]
    routed = softmax_rows(logits, experts)
    selected = chosen_ref[...] == lax.broadcasted_iota(jnp.int32, logits.shape, 0)
    gate = jnp.sum(jnp.where(selected, routed, 0.0), axis=0, keepdims=True)
    high = gate.astype(BF).astype(F32)
    mid = (gate - high).astype(BF).astype(F32)
    low = gate - high - mid
    place = lax.broadcasted_iota(jnp.int32, (TAIL, rows), 0)
    pieces = jnp.where(place == 0, high, jnp.where(place == 1, mid, jnp.where(place == 2, low, 0.0)))
    pieces = pieces.astype(BF)
    entering = normed_two.astype(BF)
    pos = pos_ref[...]
    for k in range(len(sent_refs)):
        spots = lax.broadcasted_iota(jnp.int32, (slots, rows), 0) + k * slots
        here = (spots == pos).astype(F32).astype(BF)
        sent = mxu(here, entering)
        gates = mxu(pieces, here, NT)
        tail = jnp.concatenate([gates, jnp.zeros((TAIL, width - slots), F32)], axis=1)

        @pl.when(step == 0)
        def _():
            sent_refs[k][:slots, :] = sent.astype(BF)
            sent_refs[k][slots:, :] = tail.astype(BF)

        @pl.when(step > 0)
        def _():
            sent_refs[k][:slots, :] = (sent_refs[k][:slots, :].astype(F32) + sent).astype(BF)
            sent_refs[k][slots:, :] = (sent_refs[k][slots:, :].astype(F32) + tail).astype(BF)


def gelu_parts(values):
    share = 0.5 * lax.erf(values * 0.5**0.5) + 0.5
    return share, jnp.exp(values * values * (-0.5)) * (2.0 * 3.141592653589793) ** (-0.5)


def pack_offsets(counts_ref, ids):
    offsets, total = [], 0
    for k in ids:
        offsets.append(pl.multiple_of(total, 16))
        total = total + (counts_ref[k] + 15) // 16 * 16
    return offsets, total


def source_of(place_ref, k, group):
    return lax.rem(place_ref[0] - k + group, group)


def expert_kernel(ids, earlier, block, counts_ref, place_ref, u_ref, *refs):
    chunks = len(ids)
    x_refs = refs[:chunks]
    wide_ref, narrow_ref = refs[chunks : chunks + 2]
    past_refs = refs[chunks + 2 : chunks + 2 + (len(earlier) > 0)]
    rest = refs[chunks + 2 + len(past_refs) :]
    out_ref, back_refs = rest[0], rest[1 : 1 + chunks]
    act_ref, pre_ref, xs, us, out_sum, back_sum, sums = rest[1 + chunks :]
    step, steps = pl.program_id(0), pl.num_programs(0)
    rows = x_refs[0].shape[0] - TAIL
    offsets, total = pack_offsets(counts_ref, ids)

    @pl.when(step == 0)
    def _():
        xs[...] = jnp.zeros_like(xs)
        us[...] = jnp.zeros_like(us)
        out_sum[...] = jnp.zeros_like(out_sum)
        back_sum[...] = jnp.zeros_like(back_sum)
        for k in range(chunks):
            xs[pl.ds(offsets[k], rows), :] = x_refs[k][:rows, :]
            us[pl.ds(offsets[k], rows), :] = u_ref[source_of(place_ref, ids[k], u_ref.shape[0]), :rows, :]

    def one(i, carry):
        here = pl.ds(pl.multiple_of(i * block, block), block)
        wide, narrow = wide_ref[...], narrow_ref[...]
        hidden = mxu(xs[here, :], wide)
        grad = mxu(us[here, :], narrow, NT)
        share, density = gelu_parts(hidden)
        act = (hidden * share).astype(BF)
        act_ref[here, :] = act
        pre = (grad * (share + hidden * density)).astype(BF)
        pre_ref[here, :] = pre
        out_sum[here, :] += mxu(act, narrow)
        back_sum[here, :] += mxu(pre, wide, NT)
        return carry

    blocks = (total + block - 1) // block
    lax.fori_loop(0, blocks, one, 0)

    def none(i, carry):
        here = pl.ds(pl.multiple_of(i * block, block), block)
        act_ref[here, :] = jnp.zeros((block, act_ref.shape[1]), BF)
        pre_ref[here, :] = jnp.zeros((block, pre_ref.shape[1]), BF)
        return carry

    lax.fori_loop(blocks, act_ref.shape[0] // block, none, 0)

    @pl.when(step == steps - 1)
    def _():
        for past_ref in past_refs:
            for k in earlier:
                at = source_of(place_ref, k, u_ref.shape[0])
                out_ref[at] = past_ref[at]
        out = out_sum[...].astype(BF).astype(F32)
        gates = jnp.sum(out * us[...].astype(F32), axis=1, keepdims=True)
        sums[...] = jnp.broadcast_to(gates, sums.shape)
        for k in range(chunks):
            here = pl.ds(offsets[k], rows)
            out_ref[source_of(place_ref, ids[k], u_ref.shape[0])] = out_sum[here, :].astype(BF)
            back_refs[k][:rows, :] = back_sum[here, :].astype(BF)
            gate = jnp.transpose(sums[here, :])[:1]
            high = gate.astype(BF).astype(F32)
            mid = (gate - high).astype(BF).astype(F32)
            place = lax.broadcasted_iota(jnp.int32, (TAIL, rows), 0)
            tail = jnp.where(place == 0, high, jnp.where(place == 1, mid, jnp.where(place == 2, gate - high - mid, 0.0)))
            tail = jnp.concatenate([tail, jnp.zeros((TAIL, out.shape[1] - rows), F32)], axis=1)
            back_refs[k][rows:, :] = tail.astype(BF)


def expert_call(counts, place, ids, earlier, past, xs, us, wide, narrow, deps, block=384, parts=4):
    chunks, (tailed, width), hidden = len(xs), xs[0].shape, wide.shape[1]
    rows = tailed - TAIL
    cut, most = hidden // parts, chunks * rows
    sd = jax.ShapeDtypeStruct
    smem = pl.BlockSpec(memory_space=pltpu.SMEM)
    chunk, every = whole((tailed, width)), (us.shape[0], rows, width)
    inner = pl.BlockSpec((most, cut), lambda f: (0, f))
    out, *rest = kernel_call(
        partial(expert_kernel, ids, earlier, block),
        (8 * most * width * hidden * 3 // 4, 4 * width * hidden + 4 * most * hidden),
        deps,
        grid=(parts,),
        in_specs=[smem] * 2 + [whole(us.shape)] + [chunk] * chunks
        + [pl.BlockSpec((width, cut), lambda f: (0, f)), pl.BlockSpec((cut, width), lambda f: (f, 0))]
        + [whole(every)] * len(past),
        out_specs=[whole(every)] + [chunk] * chunks + [inner, inner],
        out_shape=[sd(every, BF)] + [sd((tailed, width), BF)] * chunks + [sd((most, hidden), BF)] * 2,
        scratch_shapes=[pltpu.VMEM((most, width), BF)] * 2
        + [pltpu.VMEM((most, width), F32)] * 2 + [pltpu.VMEM((most, 128), F32)],
    )(counts, place, us, *xs, wide, narrow, *past)
    return out, rest[:chunks], rest[chunks], rest[chunks + 1]


def pack_weighed(ids, counts_ref, x_refs, rows_of, depth, packed_ref, turned_ref):
    rows = x_refs[0].shape[0] - TAIL
    offsets, _ = pack_offsets(counts_ref, ids)
    packed_ref[...] = jnp.zeros_like(packed_ref)
    lanes = lax.broadcasted_iota(jnp.int32, (128, rows), 1)
    for k in range(len(ids)):
        gates = jnp.sum(x_refs[k][rows:, :rows].astype(F32), axis=0, keepdims=True)
        gates = jnp.where(lanes < counts_ref[ids[k]], gates, 0.0)
        gates = jnp.transpose(gates)[:, :1]
        packed_ref[pl.ds(offsets[k], rows), :] = (rows_of(k).astype(F32) * gates).astype(BF)
    turned_ref[...] = jnp.transpose(packed_ref[:depth])


def pack_units(sets, counts_ref, part_refs, packed_ref):
    offsets, _ = pack_offsets(counts_ref, sum(sets, ()))
    first = 0
    for part, part_ref in zip(sets, part_refs):
        packed_ref[pl.ds(offsets[first], part_ref.shape[0]), :] = part_ref[...]
        first += len(part)


def wide_kernel(sets, depth, counts_ref, spot_ref, *refs):
    ids = sum(sets, ())
    x_refs, pre_refs = refs[: len(ids)], refs[len(ids) : len(ids) + len(sets)]
    keep_ref, send_ref, packed, turned, pres = refs[len(ids) + len(sets) :]
    rows = x_refs[0].shape[0] - TAIL

    @pl.when(pl.program_id(0) == 0)
    def _():
        pres[...] = jnp.zeros_like(pres)
        pack_weighed(ids, counts_ref, x_refs, lambda k: x_refs[k][:rows, :], depth, packed, turned)

    pack_units(sets, counts_ref, pre_refs, pres)
    put_halves(spot_ref[0], keep_ref, send_ref, slice(None), mxu(turned[...], pres[:depth]).astype(BF))


def narrow_kernel(sets, depth, counts_ref, spot_ref, place_ref, u_ref, *refs):
    ids = sum(sets, ())
    x_refs, act_refs = refs[: len(ids)], refs[len(ids) : len(ids) + len(sets)]
    keep_ref, send_ref, packed, turned, acts = refs[len(ids) + len(sets) :]
    rows = x_refs[0].shape[0] - TAIL
    step = pl.program_id(0)

    @pl.when(step == 0)
    def _():
        acts[...] = jnp.zeros_like(acts)
        rows_of = lambda k: u_ref[source_of(place_ref, ids[k], u_ref.shape[0]), :rows, :]
        pack_weighed(ids, counts_ref, x_refs, rows_of, depth, packed, turned)

    pack_units(sets, counts_ref, act_refs, acts)
    narrow = mxu(turned[...], acts[:depth]).astype(BF)
    spot = spot_ref[0]
    cut = keep_ref.shape[2]
    count = narrow.shape[1] // cut
    for k in range(count):
        part = narrow[:, k * cut : (k + 1) * cut]
        at = (step * count + k) // 2 ^ (spot // 2)

        @pl.when(spot % 2 == k % 2)
        def _():
            keep_ref[at] = part

        @pl.when(spot % 2 != k % 2)
        def _():
            send_ref[at] = part


def weight_calls(counts, spot, place, sets, xs, us, acts, pres, blocks, depth, deps, parts=4):
    chunks, (tailed, width), hidden = len(xs), xs[0].shape, acts[0].shape[1]
    half = blocks // 2
    cut, most = hidden // parts, chunks * (tailed - TAIL)
    smem = pl.BlockSpec(memory_space=pltpu.SMEM)
    inner = [pl.BlockSpec((act.shape[0], cut), lambda f: (0, f)) for act in acts]
    common = dict(
        cost=(2 * depth * width * hidden, 2 * width * hidden + 2 * most * hidden),
        grid=(parts,),
        scratch_shapes=[pltpu.VMEM((most, width), BF), pltpu.VMEM((width, depth), BF), pltpu.VMEM((most, cut), BF)],
    )
    chunk_specs = [whole((tailed, width))] * chunks
    wide = kernel_call(
        partial(wide_kernel, sets, depth),
        in_specs=[smem] * 2 + chunk_specs + inner,
        out_specs=[pl.BlockSpec((half, width // blocks, cut), lambda f: (0, 0, f))] * 2,
        out_shape=[jax.ShapeDtypeStruct((half, width // blocks, hidden), BF)] * 2,
        **common,
    )(counts, spot, *xs, *pres)
    narrow = kernel_call(
        partial(narrow_kernel, sets, depth),
        deps=[deps, wide],
        in_specs=[smem] * 3 + [whole(us.shape)] + chunk_specs + inner,
        out_specs=[whole((half, width, hidden // blocks))] * 2,
        out_shape=[jax.ShapeDtypeStruct((half, width, hidden // blocks), BF)] * 2,
        **common,
    )(counts, spot, place, us, *xs, *acts)
    return *wide, *narrow


def weight_first_kernel(keep_wide, came_wide, keep_narrow, came_narrow, *out_refs):
    rows, hidden = keep_wide.shape[1:]
    cut = keep_narrow.shape[2]
    for k, out_ref in enumerate(out_refs):
        out_ref[:, :hidden] = (keep_wide[k].astype(F32) + came_wide[k].astype(F32)).astype(BF)
        for slab in range(keep_narrow.shape[1] // rows):
            here = slice(slab * rows, (slab + 1) * rows)
            total = keep_narrow[k, here, :].astype(F32) + came_narrow[k, here, :].astype(F32)
            out_ref[:, hidden + slab * cut : hidden + (slab + 1) * cut] = total.astype(BF)


def weight_last_kernel(cut, *refs):
    wide_ref, narrow_ref = refs[-2:]
    rows, hidden = wide_ref.shape
    total = sum(ref[...].astype(F32) for ref in refs[:-2])
    wide_ref[...] = total[:, :hidden]
    for slab in range(narrow_ref.shape[1] // rows):
        piece = total[:, hidden + slab * cut : hidden + (slab + 1) * cut]
        narrow_ref[:, slab * rows : (slab + 1) * rows] = jnp.transpose(piece)


def as_column(row):
    return jnp.transpose(jnp.broadcast_to(row, (128, row.shape[1])))[:, :1]


def weight_row(gate, chosen, rank, prior, experts_padded, capacity):
    shape = (experts_padded, chosen.shape[1])
    selected = chosen == lax.broadcasted_iota(jnp.int32, shape, 0)
    before = jnp.sum(jnp.where(selected, prior, 0), axis=0, keepdims=True)
    return selected, (before + rank < capacity).astype(F32)


def put_halves(spot, keep_ref, send_ref, columns, values):
    half, rows = keep_ref.shape[:2]
    for block in range(2 * half):
        part = values[block * rows : (block + 1) * rows]

        @pl.when(spot % 2 == block % 2)
        def _():
            keep_ref[(block // 2) ^ (spot // 2), :, columns] = part

        @pl.when(spot % 2 != block % 2)
        def _():
            send_ref[(block // 2) ^ (spot // 2), :, columns] = part


EXACT = 32


def split_exact(values):
    lane = lax.broadcasted_iota(jnp.int32, values.shape, 1)
    high = values.astype(BF).astype(F32)
    mid = (values - high).astype(BF).astype(F32)
    low = values - high - mid
    band = (lane - EXACT) // 16
    mid, low = pltpu.roll(mid, 16, 1), pltpu.roll(low, 32, 1)
    return jnp.where(band == 0, high, jnp.where(band == 1, mid, jnp.where(band == 2, low, values)))


def join_exact(values):
    lane = lax.broadcasted_iota(jnp.int32, values.shape, 1)
    total = values + pltpu.roll(values, 128 - 16, 1) + pltpu.roll(values, 128 - 32, 1)
    return jnp.where((lane >= EXACT) & (lane < EXACT + 16), total, values)


def home_kernel(experts, slots, capacity, chunks, extra_rows, temper_ref, prior_ref, chosen_ref, rank_ref, pos_ref,
                residual_ref, upstream_ref, att_ref, projected_ref, table_ref, router_ref, gain_ref, shift_ref,
                wo_ref, heads_ref, *refs):
    back_refs = refs[:chunks]
    (weight_ref, grad_ref, att_grad_ref, delta_ref, outer_ref, extra_ref, tiny_ref,
     _, spots_ref, outer_sum, extra_sum, table_sum) = refs[chunks + 1 :]
    step, steps = pl.program_id(0), pl.num_programs(0)
    slots_all = spots_ref.shape[0]
    rows, width = residual_ref.shape
    route = projected_ref.shape[0]

    @pl.when(step == 0)
    def _():
        outer_sum[...] = jnp.zeros_like(outer_sum)
        extra_sum[...] = jnp.zeros_like(extra_sum)
        table_sum[...] = jnp.zeros_like(table_sum)
        for k in range(chunks):
            spots_ref[k * slots : (k + 1) * slots, :] = back_refs[k][:slots, :]

    temper = temper_ref[0]
    table = table_ref[...]
    projected = projected_ref[...]
    scale, unit, table_scale, unit_table, logits = router_of(projected, table, temper)
    routed = softmax_rows(logits, experts)
    selected, kept = weight_row(None, chosen_ref[...], rank_ref[...], prior_ref[...], table.shape[0], capacity)
    gate = jnp.sum(jnp.where(selected, routed, 0.0), axis=0, keepdims=True)
    weight = gate * kept
    weight_ref[...] = weight
    pos = pos_ref[...]
    gate_grad = jnp.zeros((1, rows), F32)
    for k in range(chunks):
        here = (lax.broadcasted_iota(jnp.int32, (slots, rows), 0) + k * slots == pos).astype(F32).astype(BF)
        gate_grad += jnp.sum(mxu(back_refs[k][slots:, :slots], here), axis=0, keepdims=True)
    gate_grad = gate_grad * kept
    logit_grad = gate_grad * routed * (selected.astype(F32) - gate)
    highest = dict(precision=lax.Precision.HIGHEST, preferred_element_type=F32)
    unit_grad = lax.dot_general(unit_table, logit_grad, TN, **highest) / temper
    table_sum[:, :route] += lax.dot_general(logit_grad, unit, NT, **highest) / temper
    sharp = -jnp.sum(logit_grad * logits, keepdims=True) / temper
    projected_grad = scale * unit_grad - scale * scale * scale * projected * jnp.sum(
        projected * unit_grad, axis=0, keepdims=True
    )
    padded = jnp.concatenate([projected_grad, jnp.zeros((128 - route, rows), F32)], axis=0)
    route_part = mxu_wide(jnp.transpose(padded), router_ref[...])
    column = pos.astype(F32)
    both = jnp.concatenate([column, weight, jnp.zeros((126, rows), F32)], axis=0)
    both = jnp.transpose(both)
    pos_column, weight_column = both[:, :1].astype(jnp.int32), both[:, 1:2]
    lanes = lax.broadcasted_iota(jnp.int32, (rows, slots_all), 1)
    home = mxu((lanes == pos_column).astype(F32).astype(BF), spots_ref[...])
    y_grad = home * weight_column + route_part
    unit_two, norm_scale, normed_two = norm_of(residual_ref[...], gain_ref[...], shift_ref[...])
    inner = y_grad * gain_ref[...]
    two_part = norm_scale * (
        inner
        - jnp.mean(inner, axis=-1, keepdims=True)
        - unit_two * jnp.mean(inner * unit_two, axis=-1, keepdims=True)
    )
    residual_grad = upstream_ref[...].astype(F32) + two_part
    grad_ref[...] = residual_grad
    branch = residual_grad.astype(BF)
    att = att_ref[...]
    outer_sum[...] += mxu(jnp.transpose(att), branch)
    att_grad = mxu(branch, wo_ref[...], NT).astype(BF)
    att_grad_ref[...] = att_grad
    product_high, product_low = split_high(att_grad.astype(F32) * att.astype(F32))
    heads = heads_ref[...]
    delta_ref[...] = mxu(heads, product_high, NT) + mxu(heads, product_low, NT)
    extra_sum[:route, :] += mxu_wide(projected_grad, normed_two)
    extra_sum[route : route + 1, :] += jnp.sum(y_grad * unit_two, axis=0, keepdims=True)
    extra_sum[route + 1 : route + 2, :] += jnp.sum(y_grad, axis=0, keepdims=True)
    extra_sum[route + 2 : route + 3, :128] += jnp.broadcast_to(sharp, (1, 128))

    @pl.when(step == steps - 1)
    def _():
        table_grad = table_sum[...]
        wide_table = jnp.concatenate([table, jnp.zeros((table.shape[0], 128 - route), F32)], axis=1)
        summed = jnp.sum(wide_table * table_grad, axis=1, keepdims=True)
        table_grad = table_scale * table_grad - table_scale * table_scale * table_scale * wide_table * summed
        sharp_row = jnp.broadcast_to(extra_sum[route + 2 : route + 3, :128], (8, 128))
        tiny = jnp.concatenate([table_grad, sharp_row], axis=0)
        tiny_ref[...] = tiny
        outer_ref[...] = outer_sum[...].astype(BF)
        extra = jnp.transpose(extra_sum[...])
        if chunks <= 8:
            tiny = jnp.concatenate([tiny, jnp.zeros((128 - tiny.shape[0], 128), F32)], axis=0)
            tiny = pltpu.roll(jnp.transpose(tiny)[: extra_rows], EXACT, 1)
            lane = lax.broadcasted_iota(jnp.int32, tiny.shape, 1)
            tiny = split_exact(jnp.where((lane >= EXACT) & (lane < EXACT + 16), tiny, 0.0))
            tiny = jnp.concatenate([tiny] * (extra.shape[0] // extra_rows), axis=0)
            lane = lax.broadcasted_iota(jnp.int32, tiny.shape, 1)
            extra = jnp.where(lane < EXACT, extra, tiny)
        extra_ref[...] = extra.astype(BF)


def score_back_kernel(pairs, heads_before, weights, spot_ref, label_ref, q_ref, k_ref, v_ref, att_grad_ref, lse_ref,
                      delta_ref, turned_ref, *refs):
    count = 3 + 2 * weights
    scratch = refs[-1 - weights :]
    out_refs = refs[-1 - weights - count : -1 - weights]
    more_refs = refs[: -1 - weights - count]
    dq_ref, dk_ref, dv_ref = out_refs[:3]
    bias_ref = scratch[0]
    rows = q_ref.shape[0]
    bias_ref[...] = same_label(label_ref)
    low_lanes = lax.broadcasted_iota(jnp.int32, (rows, 128), 1) < HEAD_DIM
    for pair in range(pairs):
        columns = slice(pair * 128, pair * 128 + 128)
        q_pair, k_pair, v_pair = q_ref[:, columns], k_ref[:, columns], v_ref[:, columns]
        g_pair = att_grad_ref[:, columns]
        k_turned = jnp.transpose(k_pair)
        dk = jnp.zeros((rows, 128), F32)
        dv = jnp.zeros((rows, 128), F32)
        dq_turned = []
        for half in range(2):
            own = low_lanes if half == 0 else jnp.logical_not(low_lanes)
            q_own = jnp.where(own, q_pair.astype(F32), 0.0).astype(BF)
            g_own = jnp.where(own, g_pair.astype(F32), 0.0).astype(BF)
            head = heads_before + pair * 2 + half
            probs = jnp.exp(mxu(k_pair, q_own, NT) + bias_ref[...] - lse_ref[head : head + 1, :])
            prob_grad = mxu(v_pair, g_own, NT)
            score_grad = (probs * (prob_grad - delta_ref[head : head + 1, :])).astype(BF)
            dv += mxu(probs.astype(BF), g_own)
            dk += mxu(score_grad, q_own)
            dq_turned.append(mxu(k_turned[half * HEAD_DIM : (half + 1) * HEAD_DIM], score_grad))
        dq = jnp.transpose(jnp.concatenate(dq_turned, axis=0)) * HEAD_DIM ** (-0.5)
        dq_ref[:, columns] = dq.astype(BF)
        dk_ref[:, columns] = dk.astype(BF)
        dv_ref[:, columns] = dv.astype(BF)
    if weights:
        weight_sums(spot_ref[0], turned_ref, (dq_ref, dk_ref, dv_ref), more_refs, out_refs[3], out_refs[4], scratch[1])


def weight_sums(spot, turned_ref, grad_refs, more_refs, keep_ref, send_ref, total_ref):
    step, steps = pl.program_id(0), pl.num_programs(0)
    width = grad_refs[0].shape[1]
    for part, ref in enumerate(grad_refs):
        columns = slice(part * width, (part + 1) * width)
        product = mxu(turned_ref[...], ref[...])

        @pl.when(step == 0)
        def _():
            total_ref[:, columns] = product

        @pl.when(step > 0)
        def _():
            total_ref[:, columns] += product

    @pl.when(step == steps - 1)
    def _():
        start = len(grad_refs) * width
        put_halves(spot, keep_ref, send_ref, slice(0, start), total_ref[...].astype(BF))
        for more_ref in more_refs:
            columns = slice(start, start + more_ref.shape[1])
            put_halves(spot, keep_ref, send_ref, columns, more_ref[...])
            start += more_ref.shape[1]


def tokens_kernel(groups, spot_ref, turned_ref, x_ref, grad_ref, wq_ref, wk_ref, wv_ref, gain_ref, shift_ref, *refs):
    tokens_ref, keep_ref, send_ref, sums_ref, joined_ref, total_ref, turned_sums_ref = refs[3 * groups :]
    step, steps = pl.program_id(0), pl.num_programs(0)
    one_grad = 0.0
    for part, w_ref in enumerate((wq_ref, wk_ref, wv_ref)):
        start = 0
        for group in range(groups):
            piece = refs[3 * group + part]
            joined_ref[part, :, start : start + piece.shape[1]] = piece[...]
            start += piece.shape[1]
        one_grad += mxu(joined_ref[part], w_ref[...], NT)
    unit, scale, _ = norm_of(x_ref[...].astype(F32), gain_ref[...], shift_ref[...])
    inner = one_grad * gain_ref[...]
    one_part = scale * (
        inner
        - jnp.mean(inner, axis=-1, keepdims=True)
        - unit * jnp.mean(inner * unit, axis=-1, keepdims=True)
    )
    tokens_ref[...] = (grad_ref[...] + one_part).astype(BF)

    @pl.when(step == 0)
    def _():
        sums_ref[...] = jnp.zeros_like(sums_ref)

    sums_ref[0:1, :] += jnp.sum(one_grad * unit, axis=0, keepdims=True)
    sums_ref[1:2, :] += jnp.sum(one_grad, axis=0, keepdims=True)

    @pl.when(step == steps - 1)
    def _():
        turned_sums_ref[...] = jnp.transpose(sums_ref[...]).astype(BF)

    weight_sums(
        spot_ref[0], turned_ref, refs[3 * groups - 3 : 3 * groups], [turned_sums_ref], keep_ref, send_ref, total_ref
    )


def first_sum_kernel(exact, keep_ref, came_ref, *out_refs):
    for k, out_ref in enumerate(out_refs):
        out_ref[...] = (keep_ref[k].astype(F32) + came_ref[k].astype(F32)).astype(BF)
        if exact is not None:
            block = keep_ref[k, :, exact : exact + 128].astype(F32) + came_ref[k, :, exact : exact + 128].astype(F32)
            out_ref[:, exact : exact + 128] = split_exact(join_exact(block)).astype(BF)


def second_sum_kernel(exact, place_ref, *refs):
    own_ref, send_refs, sum_ref = refs[4], refs[5:-1], refs[-1]
    sum_ref[...] = sum(ref[...].astype(F32) for ref in refs[:4])
    if exact is not None:
        sum_ref[:, exact : exact + 128] = split_exact(join_exact(sum_ref[:, exact : exact + 128]))
    size = own_ref.shape[0]
    group = len(send_refs) + 1
    own_ref[...] = sum_ref[pl.ds(pl.multiple_of(place_ref[0] * size, 8), size), :]
    for k, send_ref in enumerate(send_refs):
        there = lax.rem(place_ref[0] + k + 1, group)
        block = sum_ref[pl.ds(pl.multiple_of(there * size, 8), size), :]
        filler = jnp.zeros((send_ref.shape[0] - size, block.shape[1]), F32)
        send_ref[...] = jnp.concatenate([block, filler], axis=0).astype(BF)


def third_sum_kernel(exact, own_ref, *refs):
    total_ref = refs[-1]
    size = own_ref.shape[0]
    total_ref[...] = own_ref[...] + sum(ref[...].astype(F32)[:size] for ref in refs[:-1])
    if exact is not None:
        total_ref[:, exact : exact + 128] = join_exact(total_ref[:, exact : exact + 128])


def output_kernel(place_ref, residual_ref, weight_ref, pos_ref, out_ref, layer_ref, spots_ref):
    chunks, slots = out_ref.shape[:2]

    @pl.when(pl.program_id(0) == 0)
    def _():
        for k in range(chunks):
            spots_ref[k * slots : (k + 1) * slots, :] = out_ref[lax.rem(place_ref[0] + k, chunks)]

    rows = residual_ref.shape[0]
    both = jnp.concatenate([pos_ref[...].astype(F32), weight_ref[...], jnp.zeros((126, rows), F32)], axis=0)
    both = jnp.transpose(both)
    pos_column, weight_column = both[:, :1].astype(jnp.int32), both[:, 1:2]
    lanes = lax.broadcasted_iota(jnp.int32, (rows, spots_ref.shape[0]), 1)
    home = mxu((lanes == pos_column).astype(F32).astype(BF), spots_ref[...])
    layer_ref[...] = (residual_ref[...] + home * weight_column).astype(BF)


def swap(values, axis, mask):
    size = lax.axis_size(axis)
    return lax.ppermute(values, axis, [(i, i ^ mask) for i in range(size)])


def shift(values, axis, step):
    size = lax.axis_size(axis)
    return lax.ppermute(values, axis, [(i, (i + step) % size) for i in range(size)])


def pick(values, index, axis):
    return lax.dynamic_index_in_dim(values, index, axis, keepdims=False)


def first_sum(keep, send, exact=None, deps=()):
    half, rows, width = keep.shape
    came = swap(send, "dp", 1)
    return kernel_call(
        partial(first_sum_kernel, exact),
        (half * rows * width, 6 * half * rows * width),
        deps,
        in_specs=[pl.BlockSpec()] * 2,
        out_shape=[jax.ShapeDtypeStruct((rows, width), BF)] * half,
    )(keep, came)


def second_sum(parts, place_vec, exact=None, deps=()):
    group = lax.axis_size("expert")
    came = [parts[0]] + [swap(parts[k], "dp", 2 * k) for k in range(1, len(parts))]
    rows, width = parts[0].shape
    if group > 8:
        return sum(part.astype(F32) for part in came)
    size = rows // group
    padded = (size + 15) // 16 * 16
    sd = jax.ShapeDtypeStruct
    return kernel_call(
        partial(second_sum_kernel, exact),
        (4 * rows * width, 12 * rows * width),
        deps,
        in_specs=[pl.BlockSpec(memory_space=pltpu.SMEM)] + [pl.BlockSpec()] * len(came),
        out_shape=[sd((size, width), F32)] + [sd((padded, width), BF)] * (group - 1),
        scratch_shapes=[pltpu.VMEM((rows, width), F32)],
    )(place_vec, *came)


def third_sum(parts, exact=None, deps=()):
    group = lax.axis_size("expert")
    if group > 8:
        return lax.psum_scatter(parts, "expert", scatter_dimension=0, tiled=True)
    came = [shift(parts[k], "expert", k) for k in range(1, group)]
    return kernel_call(
        partial(third_sum_kernel, exact),
        (4 * parts[0].size, 12 * parts[0].size),
        deps,
        in_specs=[pl.BlockSpec()] * group,
        out_shape=jax.ShapeDtypeStruct(parts[0].shape, F32),
    )(parts[0], *came)


def small_sum(values):
    group = lax.axis_size("expert")
    if group > 8:
        return lax.psum(values, ("dp", "expert"))
    values = values + swap(values, "dp", 1)
    values = values + sum(swap(values, "dp", mask) for mask in range(2, lax.axis_size("dp"), 2))
    return values + sum(shift(values, "expert", k) for k in range(1, group))


def exchange(blocks, sign):
    size = lax.axis_size("expert")
    if size <= 8:
        return [blocks[0]] + [shift(blocks[k], "expert", sign * k) for k in range(1, size)]
    stacked = jnp.stack(blocks)
    place = lax.axis_index("expert")
    across = (jnp.arange(size) - place) * sign % size
    there = lax.all_to_all(stacked[across], "expert", 0, 0, tiled=True)
    source = (place - sign * jnp.arange(size)) % size
    home = there[source]
    return [home[k] for k in range(size)]


WAYS = 4
SETS = ((0, 2), (1, 3))
CUTS = (384, 384)


def body(
    layer_inputs_matrix,
    upstream_output_sensitivity,
    mixer_layernorm_scale,
    mixer_layernorm_offset,
    asker_matrix,
    lookup_label_matrix,
    content_matrix,
    mixer_result_matrix,
    specialist_layernorm_scale,
    specialist_layernorm_offset,
    dispatch_projection_matrix,
    specialist_centroids,
    learned_sharpness,
    specialist_widening_matrix,
    specialist_narrowing_matrix,
    document_labels,
    chosen_specialist,
    placement_ranks,
):
    rows, width = layer_inputs_matrix.shape
    seqs, length = document_labels.shape
    head_count = width // HEAD_DIM
    group = lax.axis_size("expert")
    place = lax.axis_index("expert")
    dp_size = lax.axis_size("dp")
    wide, narrow = specialist_widening_matrix[0], specialist_narrowing_matrix[0]
    hidden = wide.shape[1]
    route = dispatch_projection_matrix.shape[1]
    slots = 3 * rows // (2 * group)
    spots = group * slots
    experts_padded = (group + 7) // 8 * 8
    sd = jax.ShapeDtypeStruct
    smem = pl.BlockSpec(memory_space=pltpu.SMEM)
    int32 = jnp.int32
    place_vec = place.astype(int32).reshape(1)
    spot_vec = lax.axis_index("dp").astype(int32).reshape(1)
    vec = lambda v: v.reshape(1, -1)
    gain_one, shift_one = vec(mixer_layernorm_scale), vec(mixer_layernorm_offset)
    gain_two, shift_two = vec(specialist_layernorm_scale), vec(specialist_layernorm_offset)
    router = dispatch_projection_matrix.T
    table = jnp.zeros((experts_padded, route), F32).at[:group].set(specialist_centroids)
    labels = document_labels.reshape(seqs, 1, length)
    chosen = chosen_specialist.reshape(1, rows)

    row_block = pl.BlockSpec((length, width), lambda s: (s, 0))
    line = pl.BlockSpec((1, length), lambda s: (0, s))
    label_spec = pl.BlockSpec((1, 1, length), lambda s: (s, 0, 0))
    turned_block = pl.BlockSpec((width, length), lambda s: (0, s))
    heads_block = pl.BlockSpec((16, length), lambda s: (0, s))
    weight_spec = whole((width, width))
    vec_spec = whole((1, width))
    chunk_spec, tailed_spec = whole((slots, width)), whole((slots + TAIL, width))
    table_spec = whole((experts_padded, route))

    tailed = slots + TAIL
    pos, rank, upstream_sent = kernel_call(
        partial(route_kernel, slots),
        (2 * spots * rows * width, 8 * rows * width),
        in_specs=[smem] + [pl.BlockSpec()] * 3,
        out_shape=[sd((1, rows), int32)] * 2 + [sd((group, tailed, width), BF)],
    )(place_vec, placement_ranks, chosen, upstream_output_sensitivity)
    upstream_there = lax.all_to_all(upstream_sent, "expert", 0, 0, tiled=True)

    turned, queries, keys, values, attended, lse, residual, projected, *entering_sent = kernel_call(
        partial(attend_kernel, group, slots),
        (10 * rows * width * width + 4 * rows * length * width * 4, 20 * rows * width),
        grid=(seqs,),
        in_specs=[row_block, label_spec] + [vec_spec] * 2 + [weight_spec] * 4 + [vec_spec] * 2
        + [whole((route, width)), table_spec, smem, line, line],
        out_specs=[turned_block] + [row_block] * 4
        + [heads_block, row_block, pl.BlockSpec((route, length), lambda s: (0, s))] + [tailed_spec] * group,
        out_shape=[sd((width, rows), BF)] + [sd((rows, width), BF)] * 4
        + [sd((16, rows), F32), sd((rows, width), F32), sd((route, rows), F32)]
        + [sd((tailed, width), BF)] * group,
        scratch_shapes=[pltpu.VMEM((length, length), F32), pltpu.VMEM((length, 128), F32)],
    )(
        layer_inputs_matrix, labels, gain_one, shift_one, asker_matrix, lookup_label_matrix,
        content_matrix, mixer_result_matrix, gain_two, shift_two, router, table, learned_sharpness, chosen, pos,
    )
    entering_there = exchange(entering_sent, 1)
    tails = upstream_there[:, slots : slots + 2, :experts_padded].astype(F32)
    tallies = (tails[:, 0] * 256.0 + tails[:, 1]).astype(int32)
    sources = jnp.arange(group)
    prior = jnp.sum(jnp.where(sources[:, None] < place, tallies, 0), axis=0).reshape(experts_padded, 1)
    named = jnp.sum(jnp.where(jnp.arange(experts_padded) == place, tallies, 0), axis=1)
    earlier = jnp.sum(jnp.where(sources[:, None] < sources[None, :], named[:, None], 0), axis=0)
    counts = jnp.clip(rows - earlier, 0, named)
    relative = (place - sources) % group
    counts = jnp.sum(jnp.where(relative[:, None] == sources[None, :], counts[None, :], 0), axis=1)

    each = group // WAYS
    if each > 1:
        valid = jnp.arange(slots)[None, :] < counts[:, None]
        counts = jnp.full((WAYS,), each * slots, int32)

        def join(blocks, masks):
            chunks = []
            for k in range(0, group, each):
                tail = [jnp.where(masks[j], blocks[j][slots:, :slots], 0) for j in range(k, k + each)]
                tail = jnp.concatenate(tail, axis=1)
                tail = jnp.pad(tail, ((0, 0), (0, width - tail.shape[1])))
                chunks.append(jnp.concatenate([blocks[j][:slots] for j in range(k, k + each)] + [tail]))
            return chunks

        def split(chunks, with_tail):
            pieces = []
            for chunk in chunks:
                for j in range(each):
                    piece = chunk[j * slots : (j + 1) * slots]
                    if with_tail:
                        tail = chunk[each * slots :, j * slots : (j + 1) * slots]
                        piece = jnp.concatenate([piece, jnp.pad(tail, ((0, 0), (0, width - slots)))])
                    pieces.append(piece)
            return pieces
    else:
        valid = [True] * group
        join = split = lambda blocks, _: list(blocks)
    entered = join(entering_there, valid)
    if each > 1:
        graded = join([pick(upstream_there, relative[k], 0) for k in range(group)], valid)
        graded = jnp.stack([graded[-k % WAYS] for k in range(WAYS)])
        turn_vec = jnp.zeros((1,), int32)
    else:
        graded, turn_vec = upstream_there, place_vec
    produced, returned, earlier = [], [None] * WAYS, ()
    acts, pres = [], []
    for ids in SETS:
        out, backs, act, pre = expert_call(
            counts, turn_vec, ids, earlier, produced, [entered[k] for k in ids], graded, wide, narrow, acts
        )
        produced, earlier = [out], earlier + ids
        for at, k in enumerate(ids):
            returned[k] = backs[at]
        acts.append(act)
        pres.append(pre)
    returned_home = exchange(split(returned, True), -1)
    ordered = [k for ids in SETS for k in ids]
    arrange = lambda chunks: [chunks[k] for k in ordered]
    depth = rows + 128 if each == 1 else spots
    keep_wide, send_wide, keep_narrow, send_narrow = weight_calls(
        counts, spot_vec, turn_vec, SETS, arrange(entered), graded, acts, pres, dp_size, depth, returned_home[2]
    )
    half, block = dp_size // 2, width // dp_size
    weight_parts = kernel_call(
        weight_first_kernel,
        (width * hidden, 6 * width * hidden),
        in_specs=[pl.BlockSpec()] * 4,
        out_shape=[sd((block, 2 * hidden), BF)] * half,
    )(keep_wide, swap(send_wide, "dp", 1), keep_narrow, swap(send_narrow, "dp", 1))

    head_rows = jnp.arange(16)[:, None] == jnp.arange(width)[None, :] // HEAD_DIM
    (produced,) = produced
    if each > 1:
        pieces = jnp.stack(split([produced[-k % WAYS] for k in range(WAYS)], False))
        produced = pieces[relative]
    anywhere = pl.BlockSpec(memory_space=pl.ANY)
    weight, residual_grad, attended_grad, delta, outer_part, extra_part, tiny, produced_sent = kernel_call(
        partial(home_kernel, group, slots, rows, group, width // (dp_size * group)),
        (4 * rows * width * width + 2 * rows * spots * width, 30 * rows * width),
        weight_parts[0],
        grid=(seqs,),
        in_specs=[smem, whole((experts_padded, 1)), line, line, line, row_block, row_block, row_block,
                  pl.BlockSpec((route, length), lambda s: (0, s)), table_spec, whole((128, width)), vec_spec, vec_spec,
                  weight_spec, whole((16, width))]
        + [tailed_spec] * group + [anywhere],
        out_specs=[line, row_block, row_block, heads_block, weight_spec, whole((width, 128)),
                   whole((experts_padded + 8, 128)), anywhere],
        out_shape=[sd((1, rows), F32), sd((rows, width), F32), sd((rows, width), BF), sd((16, rows), F32),
                   sd((width, width), BF), sd((width, 128), BF), sd((experts_padded + 8, 128), F32),
                   sd((group, slots, width), BF)],
        input_output_aliases={15 + group: 7},
        scratch_shapes=[pltpu.VMEM((spots, width), BF), pltpu.VMEM((width, width), F32),
                        pltpu.VMEM((128, width), F32), pltpu.VMEM((experts_padded, 128), F32)],
    )(
        learned_sharpness, prior, chosen, rank, pos, residual, upstream_output_sensitivity, attended,
        projected, table, jnp.concatenate([router, jnp.zeros((128 - route, width), F32)]), gain_two, shift_two,
        mixer_result_matrix, head_rows.astype(BF), *returned_home, produced,
    )
    produced_home = lax.all_to_all(produced_sent, "expert", 0, 0, tiled=True)

    pieces, start = [], 0
    for cut in CUTS:
        early = start == 0
        part = pl.BlockSpec((length, cut), lambda s, at=start // cut: (s, at))
        own = pl.BlockSpec((length, cut), lambda s: (s, 0))
        more = [outer_part, extra_part] if early else []
        pack = [sd((half, block, 3 * cut + width + 128), BF)] * 2 if early else []
        *grads, = kernel_call(
            partial(score_back_kernel, cut // 128, start // HEAD_DIM, early),
            (8 * rows * length * cut * 4 + 6 * rows * width * cut, 20 * rows * cut),
            [] if early else [pieces, hidden_grad],
            grid=(seqs,),
            in_specs=[smem, label_spec] + [part] * 4 + [heads_block] * 2 + [turned_block]
            + [whole(array.shape) for array in more],
            out_specs=[own] * 3 + [whole(array.shape) for array in pack],
            out_shape=[sd((rows, cut), BF)] * 3 + pack,
            scratch_shapes=[pltpu.VMEM((length, length), F32)] + [pltpu.VMEM((width, 3 * cut), F32)] * early,
        )(spot_vec, labels, queries, keys, values, attended_grad, lse, delta, turned, *more)
        pieces.append(grads[:3])
        if early:
            keep, send = grads[3:]
            hidden_grad, return_grad = kernel_call(
                partial(weight_last_kernel, hidden // dp_size),
                (8 * block * hidden, 30 * block * hidden),
                pieces,
                in_specs=[pl.BlockSpec()] * half,
                out_shape=[sd((block, hidden), F32), sd((hidden // dp_size, width), F32)],
            )(weight_parts[0], *[swap(weight_parts[k], "dp", 2 * k) for k in range(1, half)])
        start += cut
    first, last = CUTS
    exact = 3 * first + width
    early = first_sum(keep, send, exact, pieces[1])
    pack = sd((half, block, 3 * last + 128), BF)
    tokens_grad, keep, send = kernel_call(
        partial(tokens_kernel, len(CUTS)),
        (6 * rows * width * (width + last), 16 * rows * width),
        early,
        grid=(seqs,),
        in_specs=[smem, turned_block, row_block, row_block] + [weight_spec] * 3 + [vec_spec] * 2
        + [pl.BlockSpec((length, cut), lambda s: (s, 0)) for cut in CUTS for _ in range(3)],
        out_specs=[row_block] + [whole(pack.shape)] * 2,
        out_shape=[sd((rows, width), BF)] + [pack] * 2,
        scratch_shapes=[pltpu.VMEM((128, width), F32), pltpu.VMEM((3, length, width), BF),
                        pltpu.VMEM((width, 3 * last), F32), pltpu.VMEM((width, 128), BF)],
    )(spot_vec, turned, layer_inputs_matrix, residual_grad, asker_matrix, lookup_label_matrix, content_matrix,
      gain_one, shift_one, *[piece for group_pieces in pieces for piece in group_pieces])
    early = second_sum(early, place_vec, exact, tokens_grad)
    late = first_sum(keep, send, None, early)
    layer_output = kernel_call(
        output_kernel,
        (2 * rows * spots * width, 12 * rows * width),
        late,
        grid=(seqs,),
        in_specs=[smem, row_block, line, line, whole((group, slots, width))],
        out_specs=row_block,
        out_shape=sd((rows, width), BF),
        scratch_shapes=[pltpu.VMEM((spots, width), BF)],
    )(place_vec, residual, weight, pos, produced_home)
    early = third_sum(early, exact, layer_output)
    late = third_sum(second_sum(late, place_vec, None, early))

    joined = lambda part: jnp.concatenate(
        [early[:, part * first : (part + 1) * first], late[:, part * last : (part + 1) * last]], axis=1
    )
    extra = early[:, exact : exact + 128]
    if group <= 8:
        table_grad, sharp = extra[:route, EXACT : EXACT + group].T, extra[0, EXACT + experts_padded].reshape(1)
    else:
        tiny = small_sum(tiny)
        table_grad, sharp = tiny[:group, :route], tiny[experts_padded, :1]
    return (
        layer_output,
        tokens_grad,
        late[:, 3 * last],
        late[:, 3 * last + 1],
        joined(0),
        joined(1),
        joined(2),
        early[:, 3 * first : exact],
        extra[:, route],
        extra[:, route + 1],
        extra[:, :route],
        table_grad,
        sharp,
        hidden_grad[None],
        return_grad[None],
    )


def solution(mesh):
    placed = (
        P(("dp", "expert"), None),
        P(("dp", "expert"), None),
        P(),
        P(),
        P(),
        P(),
        P(),
        P(),
        P(),
        P(),
        P(),
        P(),
        P(),
        P("expert", None, None),
        P("expert", None, None),
        P(("dp", "expert"), None),
        P(("dp", "expert"), None),
        P(("dp", "expert"), None),
    )
    return jax.shard_map(
        body,
        mesh=mesh,
        in_specs=placed,
        out_specs=(
            P(("dp", "expert"), None),
            P(("dp", "expert"), None),
            P(("dp", "expert")),
            P(("dp", "expert")),
            P(("dp", "expert"), None),
            P(("dp", "expert"), None),
            P(("dp", "expert"), None),
            P(("dp", "expert"), None),
            P(("dp", "expert")),
            P(("dp", "expert")),
            P(("dp", "expert"), None),
            P(),
            P(),
            P("expert", "dp", None),
            P("expert", "dp", None),
        ),
        check_vma=False,
    )
```

time: 1000 us -> 376 us (0.38)
  matrix products: 305 us -> 0 us
  waiting for transfers between devices: 346 us -> 89.5 us
  Pallas kernels: 0 us -> 210 us
  blocking collectives: 162 us -> 0 us
  local copies, waits for them, and re-layouts: 92.5 us -> 25.6 us
  other arithmetic: 61.4 us -> 3.18 us
  starting transfers between devices: 9.21 us -> 42.2 us
  between operations: 18 us -> 1.87 us
    dot_general x31 -> x0, matrix products: 305 us -> none  [the longest x1 50.8 us: body(): jnp.einsum('nemd,efd->nemf', grouped_grad, specialist_narrowing_matrix, p...]
    reduce_scatter x6 -> x0, waiting for transfers between devices: 255 us -> none  [the longest x1 105 us: body(): lax.psum_scatter(query_full, ('dp', 'expert'), scatter_dimension=0, tiled...]
    pallas_call x0 -> x19, Pallas kernels: none -> 210 us  [kernel_call(): return lambda *args: call(*args, *deps)]
    all_to_all x2 -> x0, blocking collectives: 113 us -> none  [the longest x1 56.9 us: body(): lax.all_to_all(grad_out, 'expert', split_axis=0, concat_axis=0, tiled=True)]
    unnamed x2 -> x0, blocking collectives: 49.5 us -> none
    all_to_all x2, waiting for transfers between devices: 90.3 us -> 43.4 us  [the longest x1 43.4 us: body(): upstream_there = lax.all_to_all(upstream_sent, 'expert', 0, 0, tiled=True)]
    ppermute x0 -> x25, waiting for transfers between devices: none -> 46.1 us  [the longest x12 28.3 us: shift(): lax.ppermute(values, axis, [(i, (i + step) % size) for i in range(size)])]
    convert_element_type x8 -> x3, other arithmetic: 33 us -> 0.63 us  [the longest x1 0.62 us: body(): head_rows.astype(BF)]
  transfers between devices with their start and end apart: 8 -> 27, of which waited for: 5 -> 7; matrix products, arithmetic and copies ran while one was open for 22% -> 4% of each run, Pallas kernels for 0% -> 54%
where the time goes in v2:
time: 376 us; the launch traced here: 373 us
  Pallas kernels  210 us (56%)
  waiting for transfers between devices  89.5 us (24%)
  starting transfers between devices  42.2 us (11%)
  local copies, waits for them, and re-layouts  25.6 us (7%)
    pallas_call x19, Pallas kernels, kernel_call(): return lambda *args: call(*args, *deps)  210 us
    all_to_all x1, waiting for transfers between devices, body(): upstream_there = lax.all_to_all(upstream_sent, 'expert', 0, 0, tiled=True)  43.4 us
    ppermute x12, waiting for transfers between devices, shift(): lax.ppermute(values, axis, [(i, (i + step) % size) for i in range(size)])  28.3 us
    ppermute x12, starting transfers between devices, shift(): lax.ppermute(values, axis, [(i, (i + step) % size) for i in range(size)])  18.9 us
    ppermute x13, waiting for transfers between devices, swap(): return lax.ppermute(values, axis, [(i, i ^ mask) for i in range(size)])  17.7 us
    unnamed x66, local copies, waits for them, and re-layouts  13.1 us
    ppermute x13, starting transfers between devices, swap(): return lax.ppermute(values, axis, [(i, i ^ mask) for i in range(size)])  12.9 us
  transfers between devices with their start and end apart: 27, of which 7 were waited for; matrix products, arithmetic and copies ran while one was open for 4% of the time, Pallas kernels for 54%

profile of v2, /device:TPU:0, one launch (start us, length us, event | category | flops | bytes accessed | tf_op | source)
XLA Modules:
  0.0 372.6 jit_solution(16899895132167960195)
XLA Ops:
  0.7 6.5 %shard_map.289 = (s32[1,1024]{1,0:T(1,128)}, s32[1,1024]{1,0:T(1,128)}, bf16[4,400,768]{2,1,0:T(8,128)(2,1)}) custom-call(s32[1]{0:T(128)} %bitcast.refs_0_.refs_1_.refs_2_, s32[1,1024]{1,0:T(1,128)} %refs_1_.1, s32[1,1024]{1,0:T(1,128)} %bitcast.23, bf16[1024,768]{1,0:T(8,128)(2,1)} %refs_6_.4), custom_call_target="tpu_custom_call" | custom-call | flops 2415919104 | bytes 6291456 | tf_op jit(solution)/shard_map/pallas_call | solution.py:60
  7.2 6.6 %all-to-all-start = ((bf16[4,400,768]{2,1,0:T(8,128)(2,1)}), bf16[4,400,768]{2,1,0:T(8,128)(2,1)S(1)}, u32[]{:S(2)}, u32[]{:S(2)}) async-start(bf16[4,400,768]{2,1,0:T(8,128)(2,1)} %get-tuple-element.98), calls=%async_computation | async-start | bytes 4915200 | tf_op jit(solution)/shard_map/all_to_all | solution.py:856
  18.1 28.8 %shard_map.290 = (bf16[768,1024]{1,0:T(8,128)(2,1)}, bf16[1024,768]{1,0:T(8,128)(2,1)}, bf16[1024,768]{1,0:T(8,128)(2,1)}, bf16[1024,768]{1,0:T(8,128)(2,1)}, bf...) custom-call(bf16[1024,768]{1,0:T(8,128)(2,1)} %refs_2_.1, ...), custom_call_target="tpu_custom_call" | custom-call | flops 12482248704 | bytes 15728640 | tf_op jit(solution)/shard_map/pallas_call | solution.py:60
  46.8 3.0 collective-permute-start
  49.8 1.5 collective-permute-start.1
  51.3 2.3 collective-permute-start.2
  53.7 43.4 %all-to-all-done.refs_2_.refs_3_ = bf16[4,400,768]{2,1,0:T(8,128)(2,1)S(1)} async-done(((bf16[4,400,768]{2,1,0:T(8,128)(2,1)}), bf16[4,400,768]{2,1,0:T(8,128)(2,1)S(1)}, u32[]{:S(2)}, u32[]{:S(2)}) %all-to-all-start) | async-done | bytes 2457632 | tf_op jit(solution)/shard_map/all_to_all | solution.py:856
  97.3 1.0 select_reduce_fusion.refs_0_
  98.3 11.9 %collective-permute-done.refs_4_.refs_3_.refs_5_ = bf16[400,768]{1,0:T(8,128)(2,1)S(1)} collective-permute-done((bf16[400,768]{1,0:T(8,128)(2,1)}, bf16[400,768]{1,0:T(8,128)(2,1)S(1)}, u32[]{:S(2)}, u32[]{:S(2)}) %collective-permute-start) | collective-permute-done | bytes 614432 | tf_op jit(solution)/shard_map/ppermute | solution.py:715
  111.1 23.5 %shard_map.291 = (bf16[4,384,768]{2,1,0:T(8,128)(2,1)}, bf16[400,768]{1,0:T(8,128)(2,1)}, bf16[400,768]{1,0:T(8,128)(2,1)}, bf16[768,3072]{1,0:T(8,128)(2,1)}, bf16[768,3072]{1,0:T(8,128)(2,1)}) custom-call(s32[4]{0:T(128)} %select_reduce_fusion.refs_0_, s32[1]{0:T(128)} %bitcast.refs_0_.refs_1_.refs_2_, bf16[4,400,768]{2,1,0:T(8,128)(2,1)} %copy-done, ...), custom_call_target="tpu_custom_call" | custom-call | flops 10871635968 | bytes 18874368 | tf_op jit(solution)/shard_map/pallas_call | solution.py:60
  134.6 24.1 %shard_map.292 = (bf16[4,384,768]{2,1,0:T(8,128)(2,1)}, bf16[400,768]{1,0:T(8,128)(2,1)}, bf16[400,768]{1,0:T(8,128)(2,1)}, bf16[768,3072]{1,0:T(8,128)(2,1)}, bf16[768,3072]{1,0:T(8,128)(2,1)}) custom-call(s32[4]{0:T(128)} %select_reduce_fusion.refs_0_, s32[1]{0:T(128)} %bitcast.refs_0_.refs_1_.refs_2_, bf16[4,400,768]{2,1,0:T(8,128)(2,1)} %copy-done, ...), custom_call_target="tpu_custom_call" | custom-call | flops 10871635968 | bytes 18874368 | tf_op jit(solution)/shard_map/pallas_call | solution.py:60
  158.7 13.0 %shard_map.293 = (bf16[4,96,3072]{2,1,0:T(8,128)(2,1)}, bf16[4,96,3072]{2,1,0:T(8,128)(2,1)}) custom-call(s32[4]{0:T(128)} %select_reduce_fusion.refs_0_, s32[1]{0:T(128)} %bitcast.7.refs_1_.refs_0_, bf16[400,768]{1,0:T(8,128)(2,1)} %get-tuple-element.102.refs_3_.refs_2_.refs_4_, bf16[400,768]{1,0:T(8,128)(2,1)} %copy-done.27, ...), custom_call_target="tpu_custom_call" | custom-call | flops 5435817984 | bytes 14155776 | tf_op jit(solution)/shard_map/pallas_call | solution.py:60
  172.5 15.1 %shard_map.294 = (bf16[4,768,384]{2,1,0:T(8,128)(2,1)}, bf16[4,768,384]{2,1,0:T(8,128)(2,1)}) custom-call(s32[4]{0:T(128)} %select_reduce_fusion.refs_0_, s32[1]{0:T(128)} %bitcast.7.refs_1_.refs_0_, s32[1]{0:T(128)} %bitcast.refs_0_.refs_1_.refs_2_, bf16[4,400,768]{2,1,0:T(8,128)(2,1)} %copy-done, ...), custom_call_target="tpu_custom_call" | custom-call | flops 5435817984 | bytes 14155776 | tf_op jit(solution)/shard_map/pallas_call | solution.py:60
  188.2 2.4 collective-permute-start.5
  192.7 1.3 copy-done.2
  194.0 6.3 %shard_map.295 = (bf16[96,6144]{1,0:T(8,128)(2,1)}, bf16[96,6144]{1,0:T(8,128)(2,1)}, bf16[96,6144]{1,0:T(8,128)(2,1)}, bf16[96,6144]{1,0:T(8,128)(2,1)}) custom-call(bf16[4,96,3072]{2,1,0:T(8,128)(2,1)} %get-tuple-element.115.refs_11_.refs_0_, bf16[4,96,3072]{2,1,0:T(8,128)(2,1)} %copy-done.2, bf16[4,768,384]{2,1,0:T(8,128)(2,1)} %get-tuple-element.118.refs_2_, ...), custom_call_target="tpu_custom_call" | custom-call | flops 2359296 | bytes 14155776 | tf_op jit(solution)/shard_map/pallas_call | solution.py:60
  200.3 2.1 collective-permute-start.10
  203.8 14.4 %collective-permute-done.3.refs_16_ = bf16[400,768]{1,0:T(8,128)(2,1)} collective-permute-done((bf16[400,768]{1,0:T(8,128)(2,1)}, bf16[400,768]{1,0:T(8,128)(2,1)}, u32[]{:S(2)}, u32[]{:S(2)}) %collective-permute-start.3) | collective-permute-done | bytes 614432 | tf_op jit(solution)/shard_map/ppermute | solution.py:715
  218.2 18.6 %shard_map.296 = (f32[1,1024]{1,0:T(1,128)}, f32[1024,768]{1,0:T(8,128)}, bf16[1024,768]{1,0:T(8,128)(2,1)}, f32[16,1024]{1,0:T(8,128)}, bf16[768,768]{1,0:T(8,1...) custom-call(f32[1]{0:T(128)S(6)} %copy.44.refs_12_.refs_0_, ...), custom_call_target="tpu_custom_call", output_to_operand_aliasing={{7}: (19, {})} | custom-call | flops 4831838208 | bytes 23592960 | tf_op jit(solution)/shard_map/pallas_call | solution.py:60
  236.8 3.8 %all-to-all-start.1 = ((bf16[4,384,768]{2,1,0:T(8,128)(2,1)}), bf16[4,384,768]{2,1,0:T(8,128)(2,1)S(1)}, u32[]{:S(2)}, u32[]{:S(2)}) async-start(bf16[4,384,768]{2,1,0:T(8,128)(2,1)} %get-tuple-element.122), calls=%async_computation.1 | async-start | bytes 4718592 | tf_op jit(solution)/shard_map/all_to_all | solution.py:973
  240.6 18.3 %shard_map.297 = (bf16[1024,384]{1,0:T(8,128)(2,1)}, bf16[1024,384]{1,0:T(8,128)(2,1)}, bf16[1024,384]{1,0:T(8,128)(2,1)}, bf16[4,96,2048]{2,1,0:T(8,128)(2,1)}, bf16[4,96,2048]{2,1,0:T(8,128)(2,1)}) custom-call(s32[1]{0:T(128)} %bitcast.7.refs_1_.refs_0_, s32[2,1,512]{2,1,0:T(1,128)} %reshape.153.refs_1_, bf16[1024,768]{1,0:T(8,128)(2,1)} %get-tuple-element.125.refs_2_, ...), custom_call_target="tpu_custom_call" | custom-call | flops 8254390272 | bytes 7864320 | tf_op jit(solution)/shard_map/pallas_call | solution.py:60
  259.0 1.0 copy-done.5
  260.0 4.6 %shard_map.298 = (f32[96,3072]{1,0:T(8,128)}, f32[384,768]{1,0:T(8,128)}) custom-call(bf16[96,6144]{1,0:T(8,128)(2,1)} %get-tuple-element.120.refs_20_.refs_0_, bf16[96,6144]{1,0:T(8,128)(2,1)} %collective-permute-done.8.refs_1_, bf16[96,6144]{1,0:T(8,128)(2,1)} %collective-permute-done.9.refs_2_, bf16[96,6144]{1,0:T(8,128)(2,1)} %copy-done.5, ...), custom_call_target="tpu_custom_call" | custom-call | flops 2359296 | bytes 8847360 | tf_op jit(solution)/shard_map/pallas_call | solution.py:60
  264.5 11.9 %shard_map.299 = (bf16[1024,384]{1,0:T(8,128)(2,1)}, bf16[1024,384]{1,0:T(8,128)(2,1)}, bf16[1024,384]{1,0:T(8,128)(2,1)}) custom-call(s32[1]{0:T(128)} %bitcast.7.refs_1_.refs_0_, s32[2,1,512]{2,1,0:T(1,128)} %reshape.153.refs_1_, bf16[1024,768]{1,0:T(8,128)(2,1)} %get-tuple-element.125.refs_2_, bf16[1024,768]{1,0:T(8,128)(2,1)} %get-tuple-element.126.refs_3_, ...), custom_call_target="tpu_custom_call" | custom-call | flops 8254390272 | bytes 7864320 | tf_op jit(solution)/shard_map/pallas_call | solution.py:60
  276.5 1.1 copy-done.4
  277.6 3.6 shard_map.300
  281.2 18.5 %shard_map.301 = (bf16[1024,768]{1,0:T(8,128)(2,1)}, bf16[4,96,1280]{2,1,0:T(8,128)(2,1)}, bf16[4,96,1280]{2,1,0:T(8,128)(2,1)}) custom-call(s32[1]{0:T(128)} %bitcast.7.refs_1_.refs_0_, bf16[768,1024]{1,0:T(8,128)(2,1)} %get-tuple-element.123.refs_8_.refs_1_, bf16[1024,768]{1,0:T(8,128)(2,1)} %refs_2_.1, f32[1024,768]{1,0:T(8,128)} %get-tuple-element.124.refs_3_, ...), custom_call_target="tpu_custom_call" | custom-call | flops 5435817984 | bytes 12582912 | tf_op jit(solution)/shard_map/pallas_call | solution.py:60
  300.3 3.1 collective-permute-start.13
  303.4 1.5 collective-permute-start.14
  305.0 8.3 %collective-permute-done.13.refs_2_ = bf16[96,2048]{1,0:T(8,128)(2,1)S(1)} collective-permute-done((bf16[96,2048]{1,0:T(8,128)(2,1)S(1)}, bf16[96,2048]{1,0:T(8,128)(2,1)S(1)}, u32[]{:S(2)}, u32[]{:S(2)}) %collective-permute-start.13) | collective-permute-done | bytes 393248 | tf_op jit(solution)/shard_map/ppermute | solution.py:710
  313.3 9.3 %collective-permute-done.14.refs_3_ = bf16[96,2048]{1,0:T(8,128)(2,1)S(1)} collective-permute-done((bf16[96,2048]{1,0:T(8,128)(2,1)S(1)}, bf16[96,2048]{1,0:T(8,128)(2,1)S(1)}, u32[]{:S(2)}, u32[]{:S(2)}) %collective-permute-start.14) | collective-permute-done | bytes 393248 | tf_op jit(solution)/shard_map/ppermute | solution.py:710
  323.6 2.6 shard_map.302
  326.2 2.0 collective-permute-start.19
  328.2 2.4 collective-permute-start.20
  330.5 1.5 collective-permute-start.21
  332.9 2.5 shard_map.303
  335.4 1.1 collective-permute-start.16
  337.5 1.4 copy-done.1
  338.9 6.6 %shard_map.304.refs_4_ = bf16[1024,768]{1,0:T(8,128)(2,1)} custom-call(s32[1]{0:T(128)} %bitcast.refs_0_.refs_1_.refs_2_, f32[1024,768]{1,0:T(8,128)} %get-tuple-element.97.refs_5_.refs_1_, f32[1,1024]{1,0:T(1,128)} %get-tuple-element.121.refs_2_, s32[1,1024]{1,0:T(1,128)} %get-tuple-element.96.refs_14_.refs_4_.refs_3_, bf16[4,384,768]{2,1,0:T(8,128)(2,1)} %copy-done.1, ...), custom_call_target="tpu_custom_call" | custom-call | flops 2415919104 | bytes 9437184 | tf_op jit(solution)/shard_map/pallas_call | solution.py:60
  345.6 1.5 collective-permute-start.18
  348.4 1.9 shard_map.305.refs_5_
  351.1 1.5 slice.101
  352.7 1.3 slice.106
  356.2 2.2 shard_map.306
  359.6 2.7 collective-permute-start.24
  365.1 1.3 collective-permute-done.23.refs_2_
  367.0 1.7 shard_map.307
  369.5 1.5 slice_reduce_fusion.2
  (121 shorter events, 24.2 us)
Async XLA Ops:
  7.1 6.7 %copy-start.24 = (s32[2,512]{1,0:T(2,128)S(1)}, s32[2,512]{1,0:T(2,128)}, u32[]{:S(2)}) copy-start(s32[2,512]{1,0:T(2,128)} %param.35) | copy-start | bytes 12292
  7.1 7.3 %copy-start.20 = (f32[768]{0:T(1024)S(1)}, f32[768]{0:T(1024)}, u32[]{:S(2)}) copy-start(f32[768]{0:T(1024)} %param.22) | copy-start | bytes 9220
  7.1 7.9 %copy-start.21 = (f32[768]{0:T(1024)S(1)}, f32[768]{0:T(1024)}, u32[]{:S(2)}) copy-start(f32[768]{0:T(1024)} %param.23) | copy-start | bytes 9220
  7.1 8.5 %copy-start.22 = (f32[768]{0:T(1024)S(1)}, f32[768]{0:T(1024)}, u32[]{:S(2)}) copy-start(f32[768]{0:T(1024)} %param.28) | copy-start | bytes 9220
  7.2 9.1 %copy-start.23 = (f32[768]{0:T(1024)S(1)}, f32[768]{0:T(1024)}, u32[]{:S(2)}) copy-start(f32[768]{0:T(1024)} %param.29) | copy-start | bytes 9220
  7.2 10.3 %copy-start.25 = (f32[4,16]{1,0:T(4,128)S(1)}, f32[4,16]{1,0:T(4,128)}, u32[]{:S(2)}) copy-start(f32[4,16]{1,0:T(4,128)} %param.31) | copy-start | bytes 772
  7.2 89.9 %all-to-all-start = ((bf16[4,400,768]{2,1,0:T(8,128)(2,1)}), bf16[4,400,768]{2,1,0:T(8,128)(2,1)S(1)}, u32[]{:S(2)}, u32[]{:S(2)}) async-start(bf16[4,400,768]{2,1,0:T(8,128)(2,1)} %get-tuple-element.98), calls=%async_computation | async-start | bytes 4915200 | tf_op jit(solution)/shard_map/all_to_all | solution.py:856
  46.8 63.4 %collective-permute-start = (bf16[400,768]{1,0:T(8,128)(2,1)}, bf16[400,768]{1,0:T(8,128)(2,1)S(1)}, u32[]{:S(2)}, u32[]{:S(2)}) collective-permute-start(bf16[400,768]{1,0:T(8,128)(2,1)} %get-tuple-element.103), channel_id=1, source_target_pairs={{0,2},{1,3},{2,0},{3,1},{4,6},{5,7},{6,4},{7,5},{8,10},{9,11},{10,... | collective-permute-start | bytes 1843208 | tf_op jit(solution)/shard_map/ppermute | solution.py:715
  49.8 84.8 %collective-permute-start.1 = (bf16[400,768]{1,0:T(8,128)(2,1)}, bf16[400,768]{1,0:T(8,128)(2,1)}, u32[]{:S(2)}, u32[]{:S(2)}) collective-permute-start(bf16[400,768]{1,0:T(8,128)(2,1)} %get-tuple-element.105), channel_id=1, source_target_pairs={{0,1},{1,2},{2,3},{3,0},{4,5},{5,6},{6,7},{7,4},{8,9},{9,10},{10,1... | collective-permute-start | bytes 1843208 | tf_op jit(solution)/shard_map/ppermute | solution.py:715
  51.3 83.3 %collective-permute-start.2 = (bf16[400,768]{1,0:T(8,128)(2,1)}, bf16[400,768]{1,0:T(8,128)(2,1)}, u32[]{:S(2)}, u32[]{:S(2)}) collective-permute-start(bf16[400,768]{1,0:T(8,128)(2,1)} %get-tuple-element.106), channel_id=1, source_target_pairs={{0,3},{1,0},{2,1},{3,2},{4,7},{5,4},{6,5},{7,6},{8,11},{9,8},{10,9... | collective-permute-start | bytes 1843208 | tf_op jit(solution)/shard_map/ppermute | solution.py:715
  97.1 13.2 %copy-start = (bf16[4,400,768]{2,1,0:T(8,128)(2,1)}, bf16[4,400,768]{2,1,0:T(8,128)(2,1)S(1)}, u32[]{:S(2)}) copy-start(bf16[4,400,768]{2,1,0:T(8,128)(2,1)S(1)} %all-to-all-done.refs_2_.refs_3_) | copy-start | bytes 7372804
  134.6 37.1 %collective-permute-start.4 = (bf16[400,768]{1,0:T(8,128)(2,1)}, bf16[400,768]{1,0:T(8,128)(2,1)S(1)}, u32[]{:S(2)}, u32[]{:S(2)}) collective-permute-start(bf16[400,768]{1,0:T(8,128)(2,1)} %get-tuple-element.110), channel_id=1, source_target_pairs={{0,2},{1,3},{2,0},{3,1},{4,6},{5,7},{6,4},{7,5},{8,10},{9,11},{10,... | collective-permute-start | bytes 1843208 | tf_op jit(solution)/shard_map/ppermute | solution.py:715
  171.7 21.0 %collective-permute-start.6 = (bf16[4,96,3072]{2,1,0:T(8,128)(2,1)}, bf16[4,96,3072]{2,1,0:T(8,128)(2,1)S(1)}, u32[]{:S(2)}, u32[]{:S(2)}) collective-permute-start(bf16[4,96,3072]{2,1,0:T(8,128)(2,1)} %get-tuple-element.116.refs_12_), channel_id=1, source_target_pairs={{0,4},{4,0},{8,12},{12,8},{16,20},{20,16},{24,28},{28,24},{1,5},{5... | collective-permute-start | bytes 7077896 | tf_op jit(solution)/shard_map/ppermute | solution.py:710
  172.5 18.1 %copy-start.19 = (f32[768,16]{0,1:T(8,128)S(1)}, f32[768,16]{0,1:T(8,128)}, u32[]{:S(2)}) copy-start(f32[768,16]{0,1:T(8,128)} %param.30) | copy-start | bytes 147460
  187.6 5.0 %collective-permute-start.7 = (bf16[4,768,384]{2,1,0:T(8,128)(2,1)}, bf16[4,768,384]{2,1,0:T(8,128)(2,1)}, u32[]{:S(2)}, u32[]{:S(2)}) collective-permute-start(bf16[4,768,384]{2,1,0:T(8,128)(2,1)} %get-tuple-element.119), channel_id=1, source_target_pairs={{0,4},{4,0},{8,12},{12,8},{16,20},{20,16},{24,28},{28,24},{1,5},{5... | collective-permute-start | bytes 7077896 | tf_op jit(solution)/shard_map/ppermute | solution.py:710
  188.2 30.0 %collective-permute-start.3 = (bf16[400,768]{1,0:T(8,128)(2,1)}, bf16[400,768]{1,0:T(8,128)(2,1)}, u32[]{:S(2)}, u32[]{:S(2)}) collective-permute-start(bf16[400,768]{1,0:T(8,128)(2,1)} %get-tuple-element.109), channel_id=1, source_target_pairs={{0,3},{1,0},{2,1},{3,2},{4,7},{5,4},{6,5},{7,6},{8,11},{9,8},{10,9... | collective-permute-start | bytes 1843208 | tf_op jit(solution)/shard_map/ppermute | solution.py:715
  188.2 30.0 %collective-permute-start.5 = (bf16[400,768]{1,0:T(8,128)(2,1)}, bf16[400,768]{1,0:T(8,128)(2,1)}, u32[]{:S(2)}, u32[]{:S(2)}) collective-permute-start(bf16[400,768]{1,0:T(8,128)(2,1)} %get-tuple-element.111), channel_id=1, source_target_pairs={{0,1},{1,2},{2,3},{3,0},{4,5},{5,6},{6,7},{7,4},{8,9},{9,10},{10,1... | collective-permute-start | bytes 1843208 | tf_op jit(solution)/shard_map/ppermute | solution.py:715
  192.7 1.4 copy-start.2
  200.3 58.6 %collective-permute-start.10 = (bf16[96,6144]{1,0:T(8,128)(2,1)}, bf16[96,6144]{1,0:T(8,128)(2,1)S(1)}, u32[]{:S(2)}, u32[]{:S(2)}) collective-permute-start(bf16[96,6144]{1,0:T(8,128)(2,1)} %get-tuple-element.138), channel_id=1, source_target_pairs={{0,24},{4,28},{8,16},{12,20},{16,8},{20,12},{24,0},{28,4},{1,25},{... | collective-permute-start | bytes 3538952 | tf_op jit(solution)/shard_map/ppermute | solution.py:710
  202.4 56.6 %collective-permute-start.8 = (bf16[96,6144]{1,0:T(8,128)(2,1)}, bf16[96,6144]{1,0:T(8,128)(2,1)}, u32[]{:S(2)}, u32[]{:S(2)}) collective-permute-start(bf16[96,6144]{1,0:T(8,128)(2,1)} %get-tuple-element.136), channel_id=1, source_target_pairs={{0,8},{4,12},{8,0},{12,4},{16,24},{20,28},{24,16},{28,20},{1,9},{5... | collective-permute-start | bytes 3538952 | tf_op jit(solution)/shard_map/ppermute | solution.py:710
  202.9 56.1 %collective-permute-start.9 = (bf16[96,6144]{1,0:T(8,128)(2,1)}, bf16[96,6144]{1,0:T(8,128)(2,1)}, u32[]{:S(2)}, u32[]{:S(2)}) collective-permute-start(bf16[96,6144]{1,0:T(8,128)(2,1)} %get-tuple-element.137), channel_id=1, source_target_pairs={{0,16},{4,20},{8,24},{12,28},{16,0},{20,4},{24,8},{28,12},{1,17},{... | collective-permute-start | bytes 3538952 | tf_op jit(solution)/shard_map/ppermute | solution.py:710
  236.8 100.7 %all-to-all-start.1 = ((bf16[4,384,768]{2,1,0:T(8,128)(2,1)}), bf16[4,384,768]{2,1,0:T(8,128)(2,1)S(1)}, u32[]{:S(2)}, u32[]{:S(2)}) async-start(bf16[4,384,768]{2,1,0:T(8,128)(2,1)} %get-tuple-element.122), calls=%async_computation.1 | async-start | bytes 4718592 | tf_op jit(solution)/shard_map/all_to_all | solution.py:973
  258.9 17.6 %collective-permute-start.11 = (bf16[4,96,2048]{2,1,0:T(8,128)(2,1)}, bf16[4,96,2048]{2,1,0:T(8,128)(2,1)S(1)}, u32[]{:S(2)}, u32[]{:S(2)}) collective-permute-start(bf16[4,96,2048]{2,1,0:T(8,128)(2,1)} %get-tuple-element.144), channel_id=1, source_target_pairs={{0,4},{4,0},{8,12},{12,8},{16,20},{20,16},{24,28},{28,24},{1,5},{5... | collective-permute-start | bytes 4718600 | tf_op jit(solution)/shard_map/ppermute | solution.py:710
  259.0 1.0 copy-start.5
  276.4 1.1 copy-start.4
  281.2 19.1 %copy-start.30 = (bf16[96,2048]{1,0:T(8,128)(2,1)S(1)}, bf16[96,2048]{1,0:T(8,128)(2,1)}, u32[]{:S(2)}) copy-start(bf16[96,2048]{1,0:T(8,128)(2,1)} %get-tuple-element.146.refs_16_) | copy-start | bytes 1179652
  281.2 22.2 %copy-start.29 = (bf16[96,2048]{1,0:T(8,128)(2,1)S(1)}, bf16[96,2048]{1,0:T(8,128)(2,1)}, u32[]{:S(2)}) copy-start(bf16[96,2048]{1,0:T(8,128)(2,1)} %get-tuple-element.147.refs_17_) | copy-start | bytes 1179652
  281.2 23.7 %copy-start.28 = (bf16[96,2048]{1,0:T(8,128)(2,1)S(1)}, bf16[96,2048]{1,0:T(8,128)(2,1)}, u32[]{:S(2)}) copy-start(bf16[96,2048]{1,0:T(8,128)(2,1)} %get-tuple-element.148.refs_18_) | copy-start | bytes 1179652
  299.7 32.3 %collective-permute-start.12 = (bf16[4,96,1280]{2,1,0:T(8,128)(2,1)}, bf16[4,96,1280]{2,1,0:T(8,128)(2,1)S(1)}, u32[]{:S(2)}, u32[]{:S(2)}) collective-permute-start(bf16[4,96,1280]{2,1,0:T(8,128)(2,1)} %get-tuple-element.150), channel_id=1, source_target_pairs={{0,4},{4,0},{8,12},{12,8},{16,20},{20,16},{24,28},{28,24},{1,5},{5... | collective-permute-start | bytes 2949128 | tf_op jit(solution)/shard_map/ppermute | solution.py:710
  300.3 13.1 %collective-permute-start.13 = (bf16[96,2048]{1,0:T(8,128)(2,1)S(1)}, bf16[96,2048]{1,0:T(8,128)(2,1)S(1)}, u32[]{:S(2)}, u32[]{:S(2)}) collective-permute-start(bf16[96,2048]{1,0:T(8,128)(2,1)S(1)} %copy-done.30), channel_id=1, source_target_pairs={{0,8},{4,12},{8,0},{12,4},{16,24},{20,28},{24,16},{28,20},{1,9},{5... | collective-permute-start | bytes 1179656 | tf_op jit(solution)/shard_map/ppermute | solution.py:710
  303.4 19.3 %collective-permute-start.14 = (bf16[96,2048]{1,0:T(8,128)(2,1)S(1)}, bf16[96,2048]{1,0:T(8,128)(2,1)S(1)}, u32[]{:S(2)}, u32[]{:S(2)}) collective-permute-start(bf16[96,2048]{1,0:T(8,128)(2,1)S(1)} %copy-done.29), channel_id=1, source_target_pairs={{0,16},{4,20},{8,24},{12,28},{16,0},{20,4},{24,8},{28,12},{1,17},{... | collective-permute-start | bytes 1179656 | tf_op jit(solution)/shard_map/ppermute | solution.py:710
  305.0 17.7 %collective-permute-start.15 = (bf16[96,2048]{1,0:T(8,128)(2,1)S(1)}, bf16[96,2048]{1,0:T(8,128)(2,1)S(1)}, u32[]{:S(2)}, u32[]{:S(2)}) collective-permute-start(bf16[96,2048]{1,0:T(8,128)(2,1)S(1)} %copy-done.28), channel_id=1, source_target_pairs={{0,24},{4,28},{8,16},{12,20},{16,8},{20,12},{24,0},{28,4},{1,25},{... | collective-permute-start | bytes 1179656 | tf_op jit(solution)/shard_map/ppermute | solution.py:710
  313.3 9.4 %copy-start.7 = (bf16[96,2048]{1,0:T(8,128)(2,1)}, bf16[96,2048]{1,0:T(8,128)(2,1)S(1)}, u32[]{:S(2)}) copy-start(bf16[96,2048]{1,0:T(8,128)(2,1)S(1)} %collective-permute-done.13.refs_2_) | copy-start | bytes 1179652
  326.2 19.4 %collective-permute-start.19 = (bf16[32,2048]{1,0:T(8,128)(2,1)}, bf16[32,2048]{1,0:T(8,128)(2,1)S(1)}, u32[]{:S(2)}, u32[]{:S(2)}) collective-permute-start(bf16[32,2048]{1,0:T(8,128)(2,1)} %get-tuple-element.153.refs_3_), channel_id=1, source_target_pairs={{0,1},{1,2},{2,3},{3,0},{4,5},{5,6},{6,7},{7,4},{8,9},{9,10},{10,1... | collective-permute-start | bytes 393224 | tf_op jit(solution)/shard_map/ppermute | solution.py:715
  328.2 18.9 %collective-permute-start.20 = (bf16[32,2048]{1,0:T(8,128)(2,1)}, bf16[32,2048]{1,0:T(8,128)(2,1)S(1)}, u32[]{:S(2)}, u32[]{:S(2)}) collective-permute-start(bf16[32,2048]{1,0:T(8,128)(2,1)} %get-tuple-element.154.refs_4_), channel_id=1, source_target_pairs={{0,2},{1,3},{2,0},{3,1},{4,6},{5,7},{6,4},{7,5},{8,10},{9,11},{10,... | collective-permute-start | bytes 393224 | tf_op jit(solution)/shard_map/ppermute | solution.py:715
  330.5 16.5 %collective-permute-start.21 = (bf16[32,2048]{1,0:T(8,128)(2,1)}, bf16[32,2048]{1,0:T(8,128)(2,1)S(1)}, u32[]{:S(2)}, u32[]{:S(2)}) collective-permute-start(bf16[32,2048]{1,0:T(8,128)(2,1)} %get-tuple-element.155.refs_5_), channel_id=1, source_target_pairs={{0,3},{1,0},{2,1},{3,2},{4,7},{5,4},{6,5},{7,6},{8,11},{9,8},{10,9... | collective-permute-start | bytes 393224 | tf_op jit(solution)/shard_map/ppermute | solution.py:715
  335.4 19.3 %collective-permute-start.16 = (bf16[96,1280]{1,0:T(8,128)(2,1)}, bf16[96,1280]{1,0:T(8,128)(2,1)S(1)}, u32[]{:S(2)}, u32[]{:S(2)}) collective-permute-start(bf16[96,1280]{1,0:T(8,128)(2,1)} %get-tuple-element.157.refs_6_), channel_id=1, source_target_pairs={{0,8},{4,12},{8,0},{12,4},{16,24},{20,28},{24,16},{28,20},{1,9},{5... | collective-permute-start | bytes 737288 | tf_op jit(solution)/shard_map/ppermute | solution.py:710
  336.5 18.2 %collective-permute-start.17 = (bf16[96,1280]{1,0:T(8,128)(2,1)}, bf16[96,1280]{1,0:T(8,128)(2,1)S(1)}, u32[]{:S(2)}, u32[]{:S(2)}) collective-permute-start(bf16[96,1280]{1,0:T(8,128)(2,1)} %get-tuple-element.158.refs_7_), channel_id=1, source_target_pairs={{0,16},{4,20},{8,24},{12,28},{16,0},{20,4},{24,8},{28,12},{1,17},{... | collective-permute-start | bytes 737288 | tf_op jit(solution)/shard_map/ppermute | solution.py:710
  337.5 1.4 copy-start.1
  338.9 6.6 %copy-start.31 = (bf16[96,1280]{1,0:T(8,128)(2,1)S(1)}, bf16[96,1280]{1,0:T(8,128)(2,1)}, u32[]{:S(2)}) copy-start(bf16[96,1280]{1,0:T(8,128)(2,1)} %get-tuple-element.159.refs_8_) | copy-start | bytes 737284
  345.5 1.5 copy-start.13
  345.6 9.2 %collective-permute-start.18 = (bf16[96,1280]{1,0:T(8,128)(2,1)S(1)}, bf16[96,1280]{1,0:T(8,128)(2,1)S(1)}, u32[]{:S(2)}, u32[]{:S(2)}) collective-permute-start(bf16[96,1280]{1,0:T(8,128)(2,1)S(1)} %copy-done.31), channel_id=1, source_target_pairs={{0,24},{4,28},{8,16},{12,20},{16,8},{20,12},{24,0},{28,4},{1,25},{... | collective-permute-start | bytes 737288 | tf_op jit(solution)/shard_map/ppermute | solution.py:710
  350.2 12.1 %slice-start = ((f32[24,2048]{1,0:T(8,128)}), f32[24,16]{1,0:T(8,128)S(1)}, s32[]{:S(2)}) async-start(f32[24,2048]{1,0:T(8,128)} %shard_map.305.refs_5_), calls=%async_computation.2 | async-start | bytes 24576 | tf_op jit(solution)/shard_map/slice | solution.py:1056
  350.2 13.4 %copy-start.3 = (f32[24,2048]{1,0:T(8,128)S(1)}, f32[24,2048]{1,0:T(8,128)}, u32[]{:S(2)}) copy-start(f32[24,2048]{1,0:T(8,128)} %shard_map.305.refs_5_) | copy-start | bytes 589828
  358.5 6.6 %collective-permute-start.22 = (bf16[32,1280]{1,0:T(8,128)(2,1)}, bf16[32,1280]{1,0:T(8,128)(2,1)S(1)}, u32[]{:S(2)}, u32[]{:S(2)}) collective-permute-start(bf16[32,1280]{1,0:T(8,128)(2,1)} %get-tuple-element.161), channel_id=1, source_target_pairs={{0,1},{1,2},{2,3},{3,0},{4,5},{5,6},{6,7},{7,4},{8,9},{9,10},{10,1... | collective-permute-start | bytes 245768 | tf_op jit(solution)/shard_map/ppermute | solution.py:715
  359.0 7.3 %collective-permute-start.23 = (bf16[32,1280]{1,0:T(8,128)(2,1)}, bf16[32,1280]{1,0:T(8,128)(2,1)S(1)}, u32[]{:S(2)}, u32[]{:S(2)}) collective-permute-start(bf16[32,1280]{1,0:T(8,128)(2,1)} %get-tuple-element.162), channel_id=1, source_target_pairs={{0,2},{1,3},{2,0},{3,1},{4,6},{5,7},{6,4},{7,5},{8,10},{9,11},{10,... | collective-permute-start | bytes 245768 | tf_op jit(solution)/shard_map/ppermute | solution.py:715
  359.6 6.8 %collective-permute-start.24 = (bf16[32,1280]{1,0:T(8,128)(2,1)}, bf16[32,1280]{1,0:T(8,128)(2,1)S(1)}, u32[]{:S(2)}, u32[]{:S(2)}) collective-permute-start(bf16[32,1280]{1,0:T(8,128)(2,1)} %get-tuple-element.163), channel_id=1, source_target_pairs={{0,3},{1,0},{2,1},{3,2},{4,7},{5,4},{6,5},{7,6},{8,11},{9,8},{10,9... | collective-permute-start | bytes 245768 | tf_op jit(solution)/shard_map/ppermute | solution.py:715
  365.1 1.3 copy-start.16
  (12 other events, 9.0 us)

commit v3 on v2

v3 whole, which is shorter than its diff:
```python
from functools import partial

import jax
import jax.numpy as jnp
from jax import lax
from jax.experimental import pallas as pl
from jax.experimental.pallas import tpu as pltpu
from jax.sharding import PartitionSpec as P

HEAD_DIM = 64
EPSILON = 1e-05
MASKED = -1e30
BF = jnp.bfloat16
F32 = jnp.float32
TAIL = 16
ROUTE_VMEM = 24
ATTEND_VMEM = 54
HOME_VMEM = 18
SCORE_VMEM = 12
TOKENS_VMEM = 18
OUTPUT_VMEM = 10
WIDE_VMEM = 36
NARROW_VMEM = 36
SUM1_VMEM = 8
SUM2_VMEM = 8
SUM3_VMEM = 10
SUM4_VMEM = 8
SUM5_VMEM = 8
SUM6_VMEM = 8
EXPERT_VMEM = (36, 50)
NN = (((1,), (0,)), ((), ()))
NT = (((1,), (1,)), ((), ()))
TN = (((0,), (0,)), ((), ()))


def mxu(left, right, dims=NN):
    return lax.dot_general(left, right, dims, preferred_element_type=F32)


def split_high(values):
    high = values.astype(BF)
    low = (values - high.astype(F32)).astype(BF)
    return high, low


def mxu_wide(left, right, dims=NN):
    left_high, left_low = split_high(left)
    right_high, right_low = split_high(right)
    return (
        mxu(left_high, right_high, dims)
        + mxu(left_high, right_low, dims)
        + mxu(left_low, right_high, dims)
    )


def kernel_call(body, weight, deps=(), vmem=56, **kwargs):
    deps = jax.tree.leaves(deps)
    inputs, outputs = len(kwargs["in_specs"]), len(kwargs["out_shape"])
    first = inputs + len(deps)
    any_spec = pl.BlockSpec(memory_space=pl.ANY)
    kwargs["in_specs"] = list(kwargs["in_specs"]) + [any_spec] * len(deps)
    kwargs["out_shape"] = list(kwargs["out_shape"]) + [jax.ShapeDtypeStruct((8, 128), F32)]
    if "out_specs" in kwargs:
        done_spec = whole((8, 128)) if "grid" in kwargs else pl.BlockSpec(memory_space=pltpu.VMEM)
        kwargs["out_specs"] = list(kwargs["out_specs"]) + [done_spec]

    def run(*refs):
        refs[first + outputs][...] = jnp.zeros((8, 128), F32)
        body(*refs[:inputs], *refs[first : first + outputs], *refs[first + outputs + 1 :])

    call = pl.pallas_call(
        run,
        compiler_params=pltpu.CompilerParams(
            vmem_limit_bytes=vmem * 2**20,
            dimension_semantics=("arbitrary",) * len(kwargs.get("grid", ())),
        ),
        cost_estimate=pl.CostEstimate(flops=int(weight * 2**30), bytes_accessed=0, transcendentals=0),
        **kwargs,
    )

    def made(*args):
        *outs, done = call(*args, *deps)
        return outs, done

    return made


def hbm(array):
    return pltpu.with_memory_space_constraint(array, pltpu.HBM)


def whole(shape):
    return pl.BlockSpec(shape, lambda *_: (0,) * len(shape))


def route_kernel(slots, place_ref, order_ref, chosen_ref, rows_ref, pos_ref, rank_ref, sent_ref):
    group = sent_ref.shape[0]
    order = order_ref[...].astype(F32)
    count = order.shape[1]
    chosen = chosen_ref[...]
    chosen_wide = jnp.transpose(jnp.broadcast_to(chosen.astype(F32), (128, count)))
    order_col = jnp.transpose(jnp.broadcast_to(order, (128, count)))[:, :1]
    before = (order_col < order) & (chosen_wide[:, :1] == chosen.astype(F32))
    rank = jnp.sum(before.astype(F32), axis=0, keepdims=True).astype(jnp.int32)
    place = place_ref[0]
    pos = jnp.where(chosen >= place, chosen - place, chosen - place + group) * slots + rank
    pos_ref[...] = pos
    rank_ref[...] = rank
    lanes = lax.broadcasted_iota(jnp.int32, (count, 128), 1).astype(F32)
    rows = rows_ref[...]
    tally = jnp.sum((chosen_wide == lanes).astype(F32), axis=0, keepdims=True)
    upper = jnp.floor(tally * (1.0 / 256.0))
    place_row = lax.broadcasted_iota(jnp.int32, (TAIL, 128), 0)
    tail = jnp.where(place_row == 0, upper, jnp.where(place_row == 1, tally - 256.0 * upper, 0.0))
    tail = jnp.concatenate([tail, jnp.zeros((TAIL, rows.shape[1] - 128), F32)], axis=1).astype(BF)
    for k in range(group):
        spots = lax.broadcasted_iota(jnp.int32, (slots, count), 0) + k * slots
        sent_ref[k, :slots, :] = mxu((spots == chosen * slots + rank).astype(F32).astype(BF), rows).astype(BF)
        sent_ref[k, slots:, :] = tail


def norm_of(values, gain, shift):
    centered = values - jnp.mean(values, axis=-1, keepdims=True)
    scale = lax.rsqrt(jnp.mean(centered * centered, axis=-1, keepdims=True) + EPSILON)
    unit = centered * scale
    return unit, scale, unit * gain + shift


def router_of(projected, table, temper):
    scale = lax.rsqrt(jnp.sum(projected * projected, axis=0, keepdims=True) + 1.0)
    unit = projected * scale
    table_scale = lax.rsqrt(jnp.sum(table * table, axis=1, keepdims=True) + 1.0)
    unit_table = table * table_scale
    logits = lax.dot_general(
        unit_table, unit, NN, precision=lax.Precision.HIGHEST, preferred_element_type=F32
    ) / temper
    return scale, unit, table_scale, unit_table, logits


def softmax_rows(logits, experts):
    valid = lax.broadcasted_iota(jnp.int32, logits.shape, 0) < experts
    logits = jnp.where(valid, logits, MASKED)
    weights = jnp.exp(logits - jnp.max(logits, axis=0, keepdims=True))
    return weights / jnp.sum(weights, axis=0, keepdims=True)


def same_label(labels):
    labels = labels.astype(F32)
    column = jnp.transpose(jnp.broadcast_to(labels, (128, labels.shape[1])))[:, :1]
    return jnp.where(column == labels, 0.0, MASKED)


def attend_kernel(experts, slots, x_ref, label_ref, gain_one_ref, shift_one_ref, wq_ref,
                  wk_ref, wv_ref, wo_ref, gain_two_ref, shift_two_ref, router_ref, table_ref, temper_ref,
                  chosen_ref, pos_ref, turned_ref, q_ref, k_ref, v_ref, att_ref, lse_ref, residual_ref,
                  projected_ref, *rest):
    sent_refs, bias_ref, lse_cols_ref = rest[:-2], rest[-2], rest[-1]
    step = pl.program_id(0)
    x = x_ref[...].astype(F32)
    rows, width = x.shape
    normed = norm_of(x, gain_one_ref[...], shift_one_ref[...])[2].astype(BF)
    turned_ref[...] = jnp.transpose(normed)
    q_ref[...] = (mxu(normed, wq_ref[...]).astype(BF).astype(F32) * HEAD_DIM ** (-0.5)).astype(BF)
    k_ref[...] = mxu(normed, wk_ref[...]).astype(BF)
    v_ref[...] = mxu(normed, wv_ref[...]).astype(BF)
    bias_ref[...] = same_label(label_ref[0])
    lane = lax.broadcasted_iota(jnp.int32, (rows, 128), 1)
    low_lanes = lane < HEAD_DIM
    lse_cols = jnp.zeros((rows, 128), F32)
    for pair in range(width // 128):
        columns = slice(pair * 128, pair * 128 + 128)
        q_pair, k_pair, v_pair = q_ref[:, columns], k_ref[:, columns], v_ref[:, columns]
        outs = []
        for half in range(2):
            own = low_lanes if half == 0 else jnp.logical_not(low_lanes)
            q_own = jnp.where(own, q_pair.astype(F32), 0.0).astype(BF)
            scores = mxu(q_own, k_pair, NT) + bias_ref[...]
            largest = jnp.max(scores, axis=-1, keepdims=True)
            weights = jnp.exp(scores - largest)
            total = jnp.sum(weights, axis=-1, keepdims=True)
            outs.append(mxu(weights.astype(BF), v_pair) * (1.0 / total))
            lse_cols = jnp.where(lane == pair * 2 + half, largest + jnp.log(total), lse_cols)
        att_ref[:, columns] = jnp.where(low_lanes, outs[0], outs[1]).astype(BF)
    lse_cols_ref[...] = lse_cols
    lse_ref[...] = jnp.transpose(lse_cols_ref[...])[: lse_ref.shape[0]]
    residual = x + mxu(att_ref[...], wo_ref[...])
    residual_ref[...] = residual
    normed_two = norm_of(residual, gain_two_ref[...], shift_two_ref[...])[2]
    projected = lax.dot_general(
        router_ref[...], normed_two, NT, precision=lax.Precision.HIGHEST, preferred_element_type=F32
    )
    projected_ref[...] = projected
    logits = router_of(projected, table_ref[...], temper_ref[0])[4]
    routed = softmax_rows(logits, experts)
    selected = chosen_ref[...] == lax.broadcasted_iota(jnp.int32, logits.shape, 0)
    gate = jnp.sum(jnp.where(selected, routed, 0.0), axis=0, keepdims=True)
    high = gate.astype(BF).astype(F32)
    mid = (gate - high).astype(BF).astype(F32)
    low = gate - high - mid
    place = lax.broadcasted_iota(jnp.int32, (TAIL, rows), 0)
    pieces = jnp.where(place == 0, high, jnp.where(place == 1, mid, jnp.where(place == 2, low, 0.0)))
    pieces = pieces.astype(BF)
    entering = normed_two.astype(BF)
    pos = pos_ref[...]
    for k in range(len(sent_refs)):
        spots = lax.broadcasted_iota(jnp.int32, (slots, rows), 0) + k * slots
        here = (spots == pos).astype(F32).astype(BF)
        sent = mxu(here, entering)
        gates = mxu(pieces, here, NT)
        tail = jnp.concatenate([gates, jnp.zeros((TAIL, width - slots), F32)], axis=1)

        @pl.when(step == 0)
        def _():
            sent_refs[k][:slots, :] = sent.astype(BF)
            sent_refs[k][slots:, :] = tail.astype(BF)

        @pl.when(step > 0)
        def _():
            sent_refs[k][:slots, :] = (sent_refs[k][:slots, :].astype(F32) + sent).astype(BF)
            sent_refs[k][slots:, :] = (sent_refs[k][slots:, :].astype(F32) + tail).astype(BF)


def gelu_parts(values):
    share = 0.5 * lax.erf(values * 0.5**0.5) + 0.5
    return share, jnp.exp(values * values * (-0.5)) * (2.0 * 3.141592653589793) ** (-0.5)


def pack_offsets(counts_ref, ids):
    offsets, total = [], 0
    for k in ids:
        offsets.append(pl.multiple_of(total, 16))
        total = total + (counts_ref[k] + 15) // 16 * 16
    return offsets, total


def source_of(place_ref, k, group):
    return lax.rem(place_ref[0] - k + group, group)


def expert_kernel(ids, past, block, counts_ref, place_ref, u_ref, *refs):
    chunks = len(ids)
    x_refs = refs[:chunks]
    wide_ref, narrow_ref = refs[chunks : chunks + 2]
    rest = refs[chunks + 2 + past :]
    out_ref, back_refs = rest[0], rest[1 : 1 + chunks]
    act_ref, pre_ref, xs, us, out_sum, back_sum, sums, outs, sent = rest[1 + chunks :]
    step, steps = pl.program_id(0), pl.num_programs(0)
    rows = x_refs[0].shape[0] - TAIL
    offsets, total = pack_offsets(counts_ref, ids)

    @pl.when(step == 0)
    def _():
        xs[...] = jnp.zeros_like(xs)
        us[...] = jnp.zeros_like(us)
        out_sum[...] = jnp.zeros_like(out_sum)
        back_sum[...] = jnp.zeros_like(back_sum)
        for k in range(chunks):
            xs[pl.ds(offsets[k], rows), :] = x_refs[k][:rows, :]
            us[pl.ds(offsets[k], rows), :] = u_ref[source_of(place_ref, ids[k], u_ref.shape[0]), :rows, :]

    def one(i, carry):
        here = pl.ds(pl.multiple_of(i * block, block), block)
        wide, narrow = wide_ref[...], narrow_ref[...]
        hidden = mxu(xs[here, :], wide)
        grad = mxu(us[here, :], narrow, NT)
        share, density = gelu_parts(hidden)
        act = (hidden * share).astype(BF)
        act_ref[here, :] = act
        pre = (grad * (share + hidden * density)).astype(BF)
        pre_ref[here, :] = pre
        out_sum[here, :] += mxu(act, narrow)
        back_sum[here, :] += mxu(pre, wide, NT)
        return carry

    blocks = (total + block - 1) // block
    lax.fori_loop(0, blocks, one, 0)

    def none(i, carry):
        here = pl.ds(pl.multiple_of(i * block, block), block)
        act_ref[here, :] = jnp.zeros((block, act_ref.shape[1]), BF)
        pre_ref[here, :] = jnp.zeros((block, pre_ref.shape[1]), BF)
        return carry

    lax.fori_loop(blocks, act_ref.shape[0] // block, none, 0)

    @pl.when(step == steps - 1)
    def _():
        out = out_sum[...].astype(BF).astype(F32)
        gates = jnp.sum(out * us[...].astype(F32), axis=1, keepdims=True)
        sums[...] = jnp.broadcast_to(gates, sums.shape)
        moves = []
        for k in range(chunks):
            here = pl.ds(offsets[k], rows)
            outs[k] = out_sum[here, :].astype(BF)
            moves.append(
                pltpu.make_async_copy(
                    outs.at[k], out_ref.at[source_of(place_ref, ids[k], u_ref.shape[0])], sent.at[k]
                )
            )
            moves[k].start()
            back_refs[k][:rows, :] = back_sum[here, :].astype(BF)
            gate = jnp.transpose(sums[here, :])[:1]
            high = gate.astype(BF).astype(F32)
            mid = (gate - high).astype(BF).astype(F32)
            place = lax.broadcasted_iota(jnp.int32, (TAIL, rows), 0)
            tail = jnp.where(place == 0, high, jnp.where(place == 1, mid, jnp.where(place == 2, gate - high - mid, 0.0)))
            tail = jnp.concatenate([tail, jnp.zeros((TAIL, out.shape[1] - rows), F32)], axis=1)
            back_refs[k][rows:, :] = tail.astype(BF)
        for move in moves:
            move.wait()


def expert_call(counts, place, ids, past, xs, us, wide, narrow, deps, block=384, parts=4):
    chunks, (tailed, width), hidden = len(xs), xs[0].shape, wide.shape[1]
    rows = tailed - TAIL
    cut, most = hidden // parts, chunks * rows
    sd = jax.ShapeDtypeStruct
    smem, anywhere = (pl.BlockSpec(memory_space=space) for space in (pltpu.SMEM, pl.ANY))
    chunk, every = whole((tailed, width)), (us.shape[0], rows, width)
    inner = pl.BlockSpec((most, cut), lambda f: (0, f))
    outs, done = kernel_call(
        partial(expert_kernel, ids, len(past), block),
        10,
        deps,
        vmem=EXPERT_VMEM[len(ids) - 1],
        grid=(parts,),
        in_specs=[smem] * 2 + [whole(us.shape)] + [chunk] * chunks
        + [pl.BlockSpec((width, cut), lambda f: (0, f)), pl.BlockSpec((cut, width), lambda f: (f, 0))]
        + [anywhere] * len(past),
        out_specs=[anywhere] + [chunk] * chunks + [inner, inner],
        out_shape=[pltpu.HBM(every, BF)] + [sd((tailed, width), BF)] * chunks + [pltpu.HBM((most, hidden), BF)] * 2,
        input_output_aliases={5 + chunks: 0} if past else {},
        scratch_shapes=[pltpu.VMEM((most, width), BF)] * 2
        + [pltpu.VMEM((most, width), F32)] * 2 + [pltpu.VMEM((most, 128), F32)]
        + [pltpu.VMEM((chunks, rows, width), BF), pltpu.SemaphoreType.DMA((chunks,))],
    )(counts, place, us, *xs, hbm(wide), hbm(narrow), *map(hbm, past))
    return outs[0], outs[1 : 1 + chunks], outs[-2], outs[-1], done


def pack_weighed(ids, counts_ref, x_refs, rows_of, depth, packed_ref, turned_ref):
    rows = x_refs[0].shape[0] - TAIL
    offsets, _ = pack_offsets(counts_ref, ids)
    packed_ref[...] = jnp.zeros_like(packed_ref)
    lanes = lax.broadcasted_iota(jnp.int32, (128, rows), 1)
    for k in range(len(ids)):
        gates = jnp.sum(x_refs[k][rows:, :rows].astype(F32), axis=0, keepdims=True)
        gates = jnp.where(lanes < counts_ref[ids[k]], gates, 0.0)
        gates = jnp.transpose(gates)[:, :1]
        packed_ref[pl.ds(offsets[k], rows), :] = (rows_of(k).astype(F32) * gates).astype(BF)
    turned_ref[...] = jnp.transpose(packed_ref[:depth])


def pack_units(sets, counts_ref, part_refs, packed_ref):
    offsets, _ = pack_offsets(counts_ref, sum(sets, ()))
    first = 0
    for part, part_ref in zip(sets, part_refs):
        packed_ref[pl.ds(offsets[first], part_ref.shape[0]), :] = part_ref[...]
        first += len(part)


def wide_kernel(sets, depth, counts_ref, spot_ref, *refs):
    ids = sum(sets, ())
    x_refs, pre_refs = refs[: len(ids)], refs[len(ids) : len(ids) + len(sets)]
    keep_ref, send_ref, packed, turned, pres = refs[len(ids) + len(sets) :]
    rows = x_refs[0].shape[0] - TAIL

    @pl.when(pl.program_id(0) == 0)
    def _():
        pres[...] = jnp.zeros_like(pres)
        pack_weighed(ids, counts_ref, x_refs, lambda k: x_refs[k][:rows, :], depth, packed, turned)

    pack_units(sets, counts_ref, pre_refs, pres)
    put_halves(spot_ref[0], keep_ref, [send_ref], slice(None), mxu(turned[...], pres[:depth]).astype(BF))


def narrow_kernel(sets, depth, counts_ref, spot_ref, place_ref, u_ref, *refs):
    ids = sum(sets, ())
    x_refs, act_refs = refs[: len(ids)], refs[len(ids) : len(ids) + len(sets)]
    keep_ref, send_ref, packed, turned, acts = refs[len(ids) + len(sets) :]
    rows = x_refs[0].shape[0] - TAIL
    step = pl.program_id(0)

    @pl.when(step == 0)
    def _():
        acts[...] = jnp.zeros_like(acts)
        rows_of = lambda k: u_ref[source_of(place_ref, ids[k], u_ref.shape[0]), :rows, :]
        pack_weighed(ids, counts_ref, x_refs, rows_of, depth, packed, turned)

    pack_units(sets, counts_ref, act_refs, acts)
    narrow = mxu(turned[...], acts[:depth]).astype(BF)
    spot = spot_ref[0]
    cut = keep_ref.shape[2]
    count = narrow.shape[1] // cut
    for k in range(count):
        part = narrow[:, k * cut : (k + 1) * cut]
        at = (step * count + k) // 2 ^ (spot // 2)

        @pl.when(spot % 2 == k % 2)
        def _():
            keep_ref[at] = part

        @pl.when(spot % 2 != k % 2)
        def _():
            send_ref[at] = part


def weight_calls(counts, spot, place, sets, xs, us, acts, pres, blocks, depth, deps, parts=4):
    chunks, (tailed, width), hidden = len(xs), xs[0].shape, acts[0].shape[1]
    half = blocks // 2
    cut, most = hidden // parts, chunks * (tailed - TAIL)
    smem = pl.BlockSpec(memory_space=pltpu.SMEM)
    inner = [pl.BlockSpec((act.shape[0], cut), lambda f: (0, f)) for act in acts]
    common = dict(
        grid=(parts,),
        scratch_shapes=[pltpu.VMEM((most, width), BF), pltpu.VMEM((width, depth), BF), pltpu.VMEM((most, cut), BF)],
    )
    chunk_specs = [whole((tailed, width))] * chunks
    wide, wide_done = kernel_call(
        partial(wide_kernel, sets, depth),
        5,
        vmem=WIDE_VMEM,
        in_specs=[smem] * 2 + chunk_specs + inner,
        out_specs=[pl.BlockSpec((half, width // blocks, cut), lambda f: (0, 0, f))] * 2,
        out_shape=[jax.ShapeDtypeStruct((half, width // blocks, hidden), BF)] * 2,
        **common,
    )(counts, spot, *xs, *map(hbm, pres))
    narrow, _ = kernel_call(
        partial(narrow_kernel, sets, depth),
        1,
        [deps, wide_done],
        vmem=NARROW_VMEM,
        in_specs=[smem] * 3 + [whole(us.shape)] + chunk_specs + inner,
        out_specs=[whole((half, width, hidden // blocks))] * 2,
        out_shape=[jax.ShapeDtypeStruct((half, width, hidden // blocks), BF)] * 2,
        **common,
    )(counts, spot, place, us, *xs, *map(hbm, acts))
    return *wide, *narrow


def weight_first_kernel(keep_wide, came_wide, keep_narrow, came_narrow, own_ref, x_keep, x_send, y_keep, y_send):
    rows, hidden = keep_wide.shape[1:]
    cut = keep_narrow.shape[2]
    for k in range(4):
        wide = (keep_wide[k].astype(F32) + came_wide[k].astype(F32)).astype(BF)
        if k == 0:
            own_ref[:, :hidden] = wide
        elif k == 2:
            x_keep[...] = wide
        else:
            x_send[k // 2] = wide
        for slab in range(keep_narrow.shape[1] // rows):
            here = slice(slab * rows, (slab + 1) * rows)
            columns = slice(slab * cut, (slab + 1) * cut)
            total = (keep_narrow[k, here, :].astype(F32) + came_narrow[k, here, :].astype(F32)).astype(BF)
            if k == 0:
                own_ref[:, hidden + slab * cut : hidden + (slab + 1) * cut] = total
            elif k == 1:
                y_keep[:, columns] = total
            else:
                y_send[k - 2, :, columns] = total


def weight_second_kernel(own_ref, x_keep, x_came, y_keep, y_came, sum_ref, x_send, y_send):
    hidden = x_keep.shape[1]
    sum_ref[:, :hidden] = own_ref[:, :hidden].astype(F32) + x_came[0].astype(F32)
    sum_ref[:, hidden:] = own_ref[:, hidden:].astype(F32) + y_came[0].astype(F32)
    x_send[...] = (x_keep[...].astype(F32) + x_came[1].astype(F32)).astype(BF)
    y_send[...] = (y_keep[...].astype(F32) + y_came[1].astype(F32)).astype(BF)


def weight_last_kernel(sum_ref, x_came, y_came, wide_ref, narrow_ref):
    rows, hidden = wide_ref.shape
    cut = narrow_ref.shape[0]
    wide_ref[...] = sum_ref[:, :hidden] + x_came[...].astype(F32)
    for slab in range(narrow_ref.shape[1] // rows):
        columns = slice(slab * cut, (slab + 1) * cut)
        piece = sum_ref[:, hidden + slab * cut : hidden + (slab + 1) * cut] + y_came[:, columns].astype(F32)
        narrow_ref[:, slab * rows : (slab + 1) * rows] = jnp.transpose(piece)


def as_column(row):
    return jnp.transpose(jnp.broadcast_to(row, (128, row.shape[1])))[:, :1]


def put_halves(spot, keep_ref, send_refs, columns, values):
    half, rows = keep_ref.shape[:2]
    held = half // len(send_refs)
    for block in range(2 * half):
        part = values[block * rows : (block + 1) * rows]
        at = (block // 2) ^ (spot // 2)

        @pl.when(spot % 2 == block % 2)
        def _():
            keep_ref[at, :, columns] = part

        for k, send_ref in enumerate(send_refs):

            @pl.when((spot % 2 != block % 2) & (at // held == k))
            def _():
                send_ref[at % held, :, columns] = part


EXACT = 32


def split_exact(values):
    lane = lax.broadcasted_iota(jnp.int32, values.shape, 1)
    high = values.astype(BF).astype(F32)
    mid = (values - high).astype(BF).astype(F32)
    low = values - high - mid
    band = (lane - EXACT) // 16
    mid, low = pltpu.roll(mid, 16, 1), pltpu.roll(low, 32, 1)
    return jnp.where(band == 0, high, jnp.where(band == 1, mid, jnp.where(band == 2, low, values)))


def join_exact(values):
    lane = lax.broadcasted_iota(jnp.int32, values.shape, 1)
    total = values + pltpu.roll(values, 128 - 16, 1) + pltpu.roll(values, 128 - 32, 1)
    return jnp.where((lane >= EXACT) & (lane < EXACT + 16), total, values)


def home_kernel(experts, slots, capacity, chunks, extra_rows, temper_ref, prior_ref, chosen_ref, rank_ref, pos_ref,
                residual_ref, upstream_ref, att_ref, projected_ref, table_ref, router_ref, gain_ref, shift_ref,
                wo_ref, *refs):
    back_refs = refs[:chunks]
    (weight_ref, grad_ref, att_grad_ref, delta_ref, outer_ref, extra_ref, tiny_ref, spots_ref, extra_sum) = refs[
        chunks:
    ]
    rows, width = residual_ref.shape
    route = projected_ref.shape[0]
    for k in range(chunks):
        spots_ref[k * slots : (k + 1) * slots, :] = back_refs[k][:slots, :]
    temper = temper_ref[0]
    table = table_ref[...]
    projected = projected_ref[...]
    scale, unit, table_scale, unit_table, logits = router_of(projected, table, temper)
    routed = softmax_rows(logits, experts)
    chosen = chosen_ref[...]
    selected = chosen == lax.broadcasted_iota(jnp.int32, logits.shape, 0)
    before = sum(jnp.where(chosen == expert, prior_ref[expert], 0) for expert in range(experts))
    kept = (before + rank_ref[...] < capacity).astype(F32)
    gate = jnp.sum(jnp.where(selected, routed, 0.0), axis=0, keepdims=True)
    weight = gate * kept
    weight_ref[...] = weight
    pos = pos_ref[...]
    gate_grad = jnp.zeros((1, rows), F32)
    for k in range(chunks):
        here = (lax.broadcasted_iota(jnp.int32, (slots, rows), 0) + k * slots == pos).astype(F32).astype(BF)
        gate_grad += jnp.sum(mxu(back_refs[k][slots:, :slots], here), axis=0, keepdims=True)
    gate_grad = gate_grad * kept
    logit_grad = gate_grad * routed * (selected.astype(F32) - gate)
    highest = dict(precision=lax.Precision.HIGHEST, preferred_element_type=F32)
    unit_grad = lax.dot_general(unit_table, logit_grad, TN, **highest) / temper
    table_grad = lax.dot_general(logit_grad, unit, NT, **highest) / temper
    sharp = -jnp.sum(logit_grad * logits, keepdims=True) / temper
    projected_grad = scale * unit_grad - scale * scale * scale * projected * jnp.sum(
        projected * unit_grad, axis=0, keepdims=True
    )
    padded = jnp.concatenate([projected_grad, jnp.zeros((128 - route, rows), F32)], axis=0)
    router = jnp.concatenate([router_ref[...], jnp.zeros((128 - route, width), F32)], axis=0)
    column = pos.astype(F32)
    both = jnp.transpose(jnp.concatenate([column, weight, jnp.zeros((126, rows), F32)], axis=0))
    routed_grad = jnp.transpose(padded)
    head_lane = lax.broadcasted_iota(jnp.int32, (width, 128), 1)
    heads = (lax.broadcasted_iota(jnp.int32, (width, 128), 0) // HEAD_DIM == head_lane).astype(F32).astype(BF)
    gain, shift = gain_ref[...], shift_ref[...]
    pos_column, weight_column = both[:, :1].astype(jnp.int32), both[:, 1:2]
    lanes = lax.broadcasted_iota(jnp.int32, (rows, spots_ref.shape[0]), 1)
    home = mxu((lanes == pos_column).astype(F32).astype(BF), spots_ref[...])
    y_grad = home * weight_column + mxu_wide(routed_grad, router)
    unit_two, norm_scale, normed_two = norm_of(residual_ref[...], gain, shift)
    inner = y_grad * gain
    two_part = norm_scale * (
        inner
        - jnp.mean(inner, axis=-1, keepdims=True)
        - unit_two * jnp.mean(inner * unit_two, axis=-1, keepdims=True)
    )
    residual_grad = upstream_ref[...].astype(F32) + two_part
    grad_ref[...] = residual_grad
    branch = residual_grad.astype(BF)
    att_grad = mxu(branch, wo_ref[...], NT).astype(BF)
    att_grad_ref[...] = att_grad
    product_high, product_low = split_high(att_grad.astype(F32) * att_ref[...].astype(F32))
    delta = mxu(product_high, heads) + mxu(product_low, heads)
    delta_ref[...] = jnp.transpose(delta)[: delta_ref.shape[0]]
    outer_ref[...] = mxu(jnp.transpose(att_ref[...]), branch).astype(BF)
    extra_sum[...] = jnp.zeros_like(extra_sum)
    extra_sum[:route, :] = mxu_wide(projected_grad, normed_two)
    extra_sum[route : route + 1, :] = jnp.sum(y_grad * unit_two, axis=0, keepdims=True)
    extra_sum[route + 1 : route + 2, :] = jnp.sum(y_grad, axis=0, keepdims=True)
    wide_table = jnp.concatenate([table, jnp.zeros((table.shape[0], 128 - route), F32)], axis=1)
    table_grad = jnp.concatenate([table_grad, jnp.zeros((table.shape[0], 128 - route), F32)], axis=1)
    summed = jnp.sum(wide_table * table_grad, axis=1, keepdims=True)
    table_grad = table_scale * table_grad - table_scale * table_scale * table_scale * wide_table * summed
    tiny = jnp.concatenate([table_grad, jnp.broadcast_to(sharp, (8, 128))], axis=0)
    tiny_ref[...] = tiny
    extra = jnp.transpose(extra_sum[...])
    if chunks <= 8:
        tiny = jnp.concatenate([tiny, jnp.zeros((128 - tiny.shape[0], 128), F32)], axis=0)
        tiny = pltpu.roll(jnp.transpose(tiny)[: extra_rows], EXACT, 1)
        lane = lax.broadcasted_iota(jnp.int32, tiny.shape, 1)
        tiny = split_exact(jnp.where((lane >= EXACT) & (lane < EXACT + 16), tiny, 0.0))
        tiny = jnp.concatenate([tiny] * (extra.shape[0] // extra_rows), axis=0)
        lane = lax.broadcasted_iota(jnp.int32, tiny.shape, 1)
        extra = jnp.where(lane < EXACT, extra, tiny)
    extra_ref[...] = extra.astype(BF)


def score_back_kernel(first, pairs, weights, spot_ref, label_ref, q_ref, k_ref, v_ref, att_grad_ref, lse_ref, delta_ref,
                      turned_ref, *refs):
    count = 3 + 3 * weights
    more_refs, out_refs, bias_ref = refs[: -1 - count], refs[-1 - count : -1], refs[-1]
    dq_ref, dk_ref, dv_ref = out_refs[:3]
    rows = label_ref.shape[2]
    low_lanes = lax.broadcasted_iota(jnp.int32, (rows, 128), 1) < HEAD_DIM
    for seq in range(label_ref.shape[0]):
        here = slice(seq * rows, (seq + 1) * rows)
        bias_ref[...] = same_label(label_ref[seq])
        for pair in range(pairs):
            there = slice(pair * 128, pair * 128 + 128)
            columns = slice((first + pair) * 128, (first + pair) * 128 + 128)
            q_pair, k_pair, v_pair = q_ref[here, columns], k_ref[here, columns], v_ref[here, columns]
            g_pair = att_grad_ref[here, columns]
            k_turned = jnp.transpose(k_pair)
            dk = jnp.zeros((rows, 128), F32)
            dv = jnp.zeros((rows, 128), F32)
            dq_turned = []
            for half in range(2):
                own = low_lanes if half == 0 else jnp.logical_not(low_lanes)
                q_own = jnp.where(own, q_pair.astype(F32), 0.0).astype(BF)
                g_own = jnp.where(own, g_pair.astype(F32), 0.0).astype(BF)
                head = (first + pair) * 2 + half
                head = slice(head, head + 1)
                probs = jnp.exp(mxu(k_pair, q_own, NT) + bias_ref[...] - lse_ref[head, here])
                prob_grad = mxu(v_pair, g_own, NT)
                score_grad = (probs * (prob_grad - delta_ref[head, here])).astype(BF)
                dv += mxu(probs.astype(BF), g_own)
                dk += mxu(score_grad, q_own)
                dq_turned.append(mxu(k_turned[half * HEAD_DIM : (half + 1) * HEAD_DIM], score_grad))
            dq = jnp.transpose(jnp.concatenate(dq_turned, axis=0)) * HEAD_DIM ** (-0.5)
            dq_ref[here, there] = dq.astype(BF)
            dk_ref[here, there] = dk.astype(BF)
            dv_ref[here, there] = dv.astype(BF)
    if weights:
        weight_grads(spot_ref[0], turned_ref, (dq_ref, dk_ref, dv_ref), more_refs, out_refs[3], out_refs[4:])


def weight_grads(spot, turned_ref, grad_refs, more_refs, keep_ref, send_refs):
    start = 0
    for ref in grad_refs:
        columns = slice(start, start + ref.shape[1])
        put_halves(spot, keep_ref, send_refs, columns, mxu(turned_ref[...], ref[...]).astype(BF))
        start += ref.shape[1]
    for more_ref in more_refs:
        columns = slice(start, start + more_ref.shape[1])
        put_halves(spot, keep_ref, send_refs, columns, more_ref[...])
        start += more_ref.shape[1]


def tokens_kernel(groups, spot_ref, turned_ref, x_ref, grad_ref, wq_ref, wk_ref, wv_ref, gain_ref, shift_ref, *refs):
    tokens_ref, keep_ref, send_ref, joined_ref, sums_ref, turned_sums_ref = refs[3 * groups :]
    one_grad = 0.0
    for part, w_ref in enumerate((wq_ref, wk_ref, wv_ref)):
        start = 0
        for group in range(groups):
            piece = refs[3 * group + part]
            joined_ref[part, :, start : start + piece.shape[1]] = piece[...]
            start += piece.shape[1]
        one_grad += mxu(joined_ref[part], w_ref[...], NT)
    unit, scale, _ = norm_of(x_ref[...].astype(F32), gain_ref[...], shift_ref[...])
    inner = one_grad * gain_ref[...]
    one_part = scale * (
        inner
        - jnp.mean(inner, axis=-1, keepdims=True)
        - unit * jnp.mean(inner * unit, axis=-1, keepdims=True)
    )
    tokens_ref[...] = (grad_ref[...] + one_part).astype(BF)
    sums_ref[...] = jnp.zeros_like(sums_ref)
    sums_ref[0:1, :] = jnp.sum(one_grad * unit, axis=0, keepdims=True)
    sums_ref[1:2, :] = jnp.sum(one_grad, axis=0, keepdims=True)
    turned_sums_ref[...] = jnp.transpose(sums_ref[...]).astype(BF)
    weight_grads(spot_ref[0], turned_ref, refs[3 * groups - 3 : 3 * groups], [turned_sums_ref], keep_ref, [send_ref])


def first_sum_kernel(exact, count, keep_ref, *refs):
    came_refs, out_refs = refs[:count], refs[count:]
    held = len(out_refs) // count
    for k, out_ref in enumerate(out_refs):
        came = came_refs[k // held][k % held].astype(F32)
        out_ref[...] = (keep_ref[k].astype(F32) + came).astype(BF)
        if exact is not None:
            here = slice(exact, exact + 128)
            out_ref[:, here] = split_exact(join_exact(keep_ref[k, :, here].astype(F32) + came[:, here])).astype(BF)


def second_sum_kernel(exact, place_ref, *refs):
    own_ref, send_refs, sum_ref = refs[4], refs[5:-1], refs[-1]
    sum_ref[...] = sum(ref[...].astype(F32) for ref in refs[:4])
    if exact is not None:
        sum_ref[:, exact : exact + 128] = split_exact(join_exact(sum_ref[:, exact : exact + 128]))
    size = own_ref.shape[0]
    group = len(send_refs) + 1
    own_ref[...] = sum_ref[pl.ds(pl.multiple_of(place_ref[0] * size, 8), size), :]
    if len(send_refs) == 1:
        (send_ref,) = send_refs
        filler = jnp.zeros((send_ref.shape[1] - size, send_ref.shape[2]), F32)
        for k in range(send_ref.shape[0]):
            block = jnp.where(place_ref[0] == k, 0.0, sum_ref[k * size : (k + 1) * size, :])
            send_ref[k] = jnp.concatenate([block, filler], axis=0).astype(BF)
        return
    for k, send_ref in enumerate(send_refs):
        there = lax.rem(place_ref[0] + k + 1, group)
        block = sum_ref[pl.ds(pl.multiple_of(there * size, 8), size), :]
        filler = jnp.zeros((send_ref.shape[0] - size, block.shape[1]), F32)
        send_ref[...] = jnp.concatenate([block, filler], axis=0).astype(BF)


def last_sum_kernel(first, last, route, group, experts_padded, counts, *refs):
    query_ref, key_ref, value_ref, outer_ref, router_ref, norms_ref, table_ref, sharp_ref = refs[sum(counts) :]
    rows, width = outer_ref.shape

    def total(parts, columns):
        value = parts[0][:, columns]
        for ref in parts[1:]:
            for sent in [ref] if len(ref.shape) == 2 else [ref.at[k] for k in range(ref.shape[0])]:
                value = value + sent[:, columns].astype(F32)[:rows]
        return value

    def turned(extra):
        return jnp.transpose(jnp.concatenate([extra, jnp.zeros((128 - rows, 128), F32)], axis=0))

    early, late = refs[: counts[0]], refs[counts[0] : sum(counts)]
    for part, ref in enumerate((query_ref, key_ref, value_ref)):
        ref[:, :first] = total(early, slice(part * first, (part + 1) * first))
        ref[:, first:] = total(late, slice(part * last, (part + 1) * last))
    outer_ref[...] = total(early, slice(3 * first, 3 * first + width))
    extra = join_exact(total(early, slice(3 * first + width, 3 * first + width + 128)))
    router_ref[...] = extra[:, :route]
    extra = turned(extra)
    norms = turned(total(late, slice(3 * last, 3 * last + 128)))
    norms_ref[...] = jnp.concatenate([norms[:2, :rows], extra[route : route + 2, :rows]], axis=0)
    table_ref[...] = extra[EXACT : EXACT + group, :route]
    sharp_ref[...] = extra[EXACT + experts_padded : EXACT + experts_padded + 1, :1]


def output_kernel(place_ref, residual_ref, weight_ref, pos_ref, out_ref, layer_ref, spots_ref):
    chunks, slots = out_ref.shape[:2]
    for k in range(chunks):
        spots_ref[k * slots : (k + 1) * slots, :] = out_ref[lax.rem(place_ref[0] + k, chunks)]
    rows = residual_ref.shape[0]
    both = jnp.concatenate([pos_ref[...].astype(F32), weight_ref[...], jnp.zeros((126, rows), F32)], axis=0)
    both = jnp.transpose(both)
    pos_column, weight_column = both[:, :1].astype(jnp.int32), both[:, 1:2]
    lanes = lax.broadcasted_iota(jnp.int32, (rows, spots_ref.shape[0]), 1)
    home = mxu((lanes == pos_column).astype(F32).astype(BF), spots_ref[...])
    layer_ref[...] = (residual_ref[...] + home * weight_column).astype(BF)


def swap(values, axis, mask):
    size = lax.axis_size(axis)
    return lax.ppermute(values, axis, [(i, i ^ mask) for i in range(size)])


def shift(values, axis, step):
    size = lax.axis_size(axis)
    return lax.ppermute(values, axis, [(i, (i + step) % size) for i in range(size)])


def pick(values, index, axis):
    return lax.dynamic_index_in_dim(values, index, axis, keepdims=False)


def held(arrays, deps):
    anywhere = pl.BlockSpec(memory_space=pl.ANY)
    return kernel_call(
        lambda *refs: None,
        0,
        deps,
        in_specs=[anywhere] * len(arrays),
        out_specs=[anywhere] * len(arrays),
        out_shape=[jax.ShapeDtypeStruct(array.shape, array.dtype) for array in arrays],
        input_output_aliases={k: k for k in range(len(arrays))},
    )(*arrays)[0]


def first_sum(keep, sends, exact, deps, weight):
    half, rows, width = keep.shape
    return kernel_call(
        partial(first_sum_kernel, exact, len(sends)),
        weight,
        deps,
        vmem=SUM1_VMEM,
        in_specs=[pl.BlockSpec()] * (1 + len(sends)),
        out_shape=[jax.ShapeDtypeStruct((rows, width), BF)] * half,
    )(keep, *[swap(send, "dp", 1) for send in sends])


def second_sum(parts, place_vec, exact, deps, weight, together=False):
    group = lax.axis_size("expert")
    came = [parts[0]] + [swap(parts[k], "dp", 2 * k) for k in range(1, len(parts))]
    rows, width = parts[0].shape
    if group > 8:
        return [sum(part.astype(F32) for part in came)], ()
    size = rows // group
    padded = (size + 15) // 16 * 16
    sd = jax.ShapeDtypeStruct
    return kernel_call(
        partial(second_sum_kernel, exact),
        weight,
        deps,
        vmem=SUM2_VMEM,
        in_specs=[pl.BlockSpec(memory_space=pltpu.SMEM)] + [pl.BlockSpec()] * len(came),
        out_shape=[sd((size, width), F32)]
        + ([sd((group, padded, width), BF)] if together else [sd((padded, width), BF)] * (group - 1)),
        scratch_shapes=[pltpu.VMEM((rows, width), F32)],
    )(place_vec, *came)


def sent_on(parts):
    if lax.axis_size("expert") > 8:
        return [lax.psum_scatter(parts[0], "expert", scatter_dimension=0, tiled=True)]
    if len(parts) == 2:
        return [parts[0], lax.all_to_all(parts[1], "expert", 0, 0, tiled=True)]
    return [parts[0]] + [shift(parts[k], "expert", k) for k in range(1, len(parts))]


def small_sum(values):
    group = lax.axis_size("expert")
    if group > 8:
        return lax.psum(values, ("dp", "expert"))
    values = values + swap(values, "dp", 1)
    values = values + sum(swap(values, "dp", mask) for mask in range(2, lax.axis_size("dp"), 2))
    return values + sum(shift(values, "expert", k) for k in range(1, group))


def exchange(blocks, sign):
    size = lax.axis_size("expert")
    if size <= 8:
        return [blocks[0]] + [shift(blocks[k], "expert", sign * k) for k in range(1, size)]
    stacked = jnp.stack(blocks)
    place = lax.axis_index("expert")
    across = (jnp.arange(size) - place) * sign % size
    there = lax.all_to_all(stacked[across], "expert", 0, 0, tiled=True)
    source = (place - sign * jnp.arange(size)) % size
    home = there[source]
    return [home[k] for k in range(size)]


WAYS = 4
SETS = ((0,), (1, 3), (2,))
CUTS = (512, 256)
D0_WEIGHT, D1_WEIGHT, FIRST_WEIGHT, TOKENS_WEIGHT = 0.1, 0.1, 0.05, 0.1
MID_WEIGHT, LATE_FIRST_WEIGHT, SECOND_WEIGHT, LATE_SECOND_WEIGHT, LAST_WEIGHT, OUTPUT_WEIGHT = 18, 1, 1, 7, 0.1, 0.1


def body(
    layer_inputs_matrix,
    upstream_output_sensitivity,
    mixer_layernorm_scale,
    mixer_layernorm_offset,
    asker_matrix,
    lookup_label_matrix,
    content_matrix,
    mixer_result_matrix,
    specialist_layernorm_scale,
    specialist_layernorm_offset,
    dispatch_projection_matrix,
    specialist_centroids,
    learned_sharpness,
    specialist_widening_matrix,
    specialist_narrowing_matrix,
    document_labels,
    chosen_specialist,
    placement_ranks,
):
    rows, width = layer_inputs_matrix.shape
    seqs, length = document_labels.shape
    head_count = width // HEAD_DIM
    group = lax.axis_size("expert")
    place = lax.axis_index("expert")
    dp_size = lax.axis_size("dp")
    wide, narrow = specialist_widening_matrix[0], specialist_narrowing_matrix[0]
    hidden = wide.shape[1]
    route = dispatch_projection_matrix.shape[1]
    slots = 3 * rows // (2 * group)
    spots = group * slots
    experts_padded = (group + 7) // 8 * 8
    sd = jax.ShapeDtypeStruct
    smem, vmem = (pl.BlockSpec(memory_space=space) for space in (pltpu.SMEM, pltpu.VMEM))
    int32 = jnp.int32
    place_vec = place.astype(int32).reshape(1)
    spot_vec = lax.axis_index("dp").astype(int32).reshape(1)
    vec = lambda v: v.reshape(1, -1)
    gain_one, shift_one = vec(mixer_layernorm_scale), vec(mixer_layernorm_offset)
    gain_two, shift_two = vec(specialist_layernorm_scale), vec(specialist_layernorm_offset)
    router = dispatch_projection_matrix.T
    table = jnp.zeros((experts_padded, route), F32).at[:group].set(specialist_centroids)
    labels = document_labels.reshape(seqs, 1, length)
    chosen = chosen_specialist.reshape(1, rows)

    row_block = pl.BlockSpec((length, width), lambda s: (s, 0))
    line = pl.BlockSpec((1, length), lambda s: (0, s))
    label_spec = pl.BlockSpec((1, 1, length), lambda s: (s, 0, 0))
    turned_block = pl.BlockSpec((width, length), lambda s: (0, s))
    heads_block = pl.BlockSpec((16, length), lambda s: (0, s))
    weight_spec = whole((width, width))
    vec_spec = whole((1, width))
    chunk_spec, tailed_spec = whole((slots, width)), whole((slots + TAIL, width))
    table_spec = whole((experts_padded, route))

    tailed = slots + TAIL
    (pos, rank, upstream_sent), _ = kernel_call(
        partial(route_kernel, slots),
        5,
        vmem=ROUTE_VMEM,
        in_specs=[smem] + [pl.BlockSpec()] * 3,
        out_shape=[sd((1, rows), int32)] * 2 + [pltpu.HBM((group, tailed, width), BF)],
    )(place_vec, placement_ranks, chosen, upstream_output_sensitivity)
    upstream_there = lax.all_to_all(upstream_sent, "expert", 0, 0, tiled=True)

    (turned, queries, keys, values, attended, lse, residual, projected, *entering_sent), _ = kernel_call(
        partial(attend_kernel, group, slots),
        20,
        vmem=ATTEND_VMEM,
        grid=(seqs,),
        in_specs=[row_block, label_spec] + [vec_spec] * 2 + [weight_spec] * 4 + [vec_spec] * 2
        + [whole((route, width)), table_spec, smem, line, line],
        out_specs=[turned_block] + [row_block] * 4
        + [heads_block, row_block, pl.BlockSpec((route, length), lambda s: (0, s))] + [tailed_spec] * group,
        out_shape=[pltpu.HBM((width, rows), BF)] + [pltpu.HBM((rows, width), BF)] * 4
        + [sd((16, rows), F32), pltpu.HBM((rows, width), F32), sd((route, rows), F32)]
        + [pltpu.HBM((tailed, width), BF)] * group,
        scratch_shapes=[pltpu.VMEM((length, length), F32), pltpu.VMEM((length, 128), F32)],
    )(
        layer_inputs_matrix, labels, gain_one, shift_one, asker_matrix, lookup_label_matrix,
        content_matrix, mixer_result_matrix, gain_two, shift_two, router, table, learned_sharpness, chosen, pos,
    )
    tails = upstream_there[:, slots : slots + 2, :experts_padded].astype(F32)
    tallies = (tails[:, 0] * 256.0 + tails[:, 1]).astype(int32)
    sources = jnp.arange(group)
    prior = jnp.sum(jnp.where(sources[:, None] < place, tallies, 0), axis=0)
    named = jnp.sum(jnp.where(jnp.arange(experts_padded) == place, tallies, 0), axis=1)
    earlier = jnp.sum(jnp.where(sources[:, None] < sources[None, :], named[:, None], 0), axis=0)
    counts = jnp.clip(rows - earlier, 0, named)
    relative = (place - sources) % group
    counts = jnp.sum(jnp.where(relative[:, None] == sources[None, :], counts[None, :], 0), axis=1)

    each = group // WAYS
    backs, produced, acts, pres, order = [None] * WAYS, [], [], [], []

    def experts(ids, counts, entered, graded, turn, deps):
        out, some, act, pre, done = expert_call(
            counts, turn, ids, produced, entered, graded, wide, narrow, [deps, order]
        )
        produced[:] = [out]
        for k, back in zip(ids, some):
            backs[k] = back
        acts.append(act)
        pres.append(pre)
        order.append(done)

    if each == 1:
        split = lambda chunks, _: list(chunks)
        turn_vec, graded, entered = place_vec, upstream_there, list(entering_sent)
        alone = jnp.sum((chosen == place).astype(int32)).reshape(1)
        experts(SETS[0], alone, entered[:1], upstream_sent, turn_vec, ())
        ready = upstream_there
        for ids in SETS[1:]:
            for k, sent in zip(ids, held([entered[k] for k in ids], [ready, order[0]])):
                entered[k] = shift(sent, "expert", k)
            ready = [entered[k] for k in ids]
        for ids in SETS[1:]:
            experts(ids, counts, [entered[k] for k in ids], graded, turn_vec, prior)
    else:
        entering_there = exchange(entering_sent, 1)
        valid = jnp.arange(slots)[None, :] < counts[:, None]
        counts = jnp.full((WAYS,), each * slots, int32)
        turn_vec = jnp.zeros((1,), int32)

        def join(blocks, masks):
            chunks = []
            for k in range(0, group, each):
                tail = [jnp.where(masks[j], blocks[j][slots:, :slots], 0) for j in range(k, k + each)]
                tail = jnp.concatenate(tail, axis=1)
                tail = jnp.pad(tail, ((0, 0), (0, width - tail.shape[1])))
                chunks.append(jnp.concatenate([blocks[j][:slots] for j in range(k, k + each)] + [tail]))
            return chunks

        def split(chunks, with_tail):
            pieces = []
            for chunk in chunks:
                for j in range(each):
                    piece = chunk[j * slots : (j + 1) * slots]
                    if with_tail:
                        tail = chunk[each * slots :, j * slots : (j + 1) * slots]
                        piece = jnp.concatenate([piece, jnp.pad(tail, ((0, 0), (0, width - slots)))])
                    pieces.append(piece)
            return pieces

        entered = join(entering_there, valid)
        graded = join([pick(upstream_there, relative[k], 0) for k in range(group)], valid)
        graded = jnp.stack([graded[-k % WAYS] for k in range(WAYS)])
        for ids in SETS:
            experts(ids, counts, [entered[k] for k in ids], graded, turn_vec, ())
    returned_home = exchange(split(backs, True), -1)
    ordered = [k for ids in SETS for k in ids]
    arrange = lambda chunks: [chunks[k] for k in ordered]
    depth = rows + 128 if each == 1 else spots
    keep_wide, send_wide, keep_narrow, send_narrow = weight_calls(
        counts, spot_vec, turn_vec, SETS, arrange(entered), graded, acts, pres, dp_size, depth,
        [returned_home[k] for k in SETS[1]],
    )
    half, block = dp_size // 2, width // dp_size
    (weight, residual_grad, attended_grad, delta, outer_part, extra_part, tiny), done = kernel_call(
        partial(home_kernel, group, slots, rows, group, width // (dp_size * group)),
        500,
        vmem=HOME_VMEM,
        in_specs=[smem, smem] + [vmem] * (12 + group),
        out_specs=[vmem] * 7,
        out_shape=[sd((1, rows), F32), sd((rows, width), F32), sd((rows, width), BF), sd((16, rows), F32),
                   sd((width, width), BF), sd((width, 128), BF), sd((experts_padded + 8, 128), F32)],
        scratch_shapes=[pltpu.VMEM((spots, width), BF), pltpu.VMEM((128, width), F32)],
    )(
        learned_sharpness, prior, chosen, rank, pos, residual, upstream_output_sensitivity, attended,
        projected, table, router, gain_two, shift_two, mixer_result_matrix, *returned_home,
    )
    half_rows = sd((block, hidden), BF)
    (weight_own, x_keep, x_send, y_keep, y_send), first_done = kernel_call(
        weight_first_kernel,
        1,
        done,
        vmem=SUM3_VMEM,
        in_specs=[pl.BlockSpec()] * 4,
        out_shape=[sd((block, 2 * hidden), BF)] + [half_rows, sd((2, block, hidden), BF)] * 2,
    )(keep_wide, swap(send_wide, "dp", 1), keep_narrow, swap(send_narrow, "dp", 1))
    (produced,) = held(produced, first_done)
    if each > 1:
        produced = jnp.stack(split([produced[-k % WAYS] for k in range(WAYS)], False))[relative]
    produced_home = lax.all_to_all(produced, "expert", 0, 0, tiled=True)

    pieces, start, done = [], 0, first_done
    for cut in CUTS:
        early = start == 0
        more = [outer_part, extra_part] if early else []
        columns = 3 * cut + width + 128
        pack = [sd((half, block, columns), BF)] + [sd((half // 2, block, columns), BF)] * 2 if early else []
        grads, done = kernel_call(
            partial(score_back_kernel, start // 128, cut // 128, early),
            D0_WEIGHT if early else D1_WEIGHT,
            done,
            vmem=SCORE_VMEM,
            in_specs=[smem] + [vmem] * (8 + len(more)),
            out_specs=[vmem] * (3 + len(pack)),
            out_shape=[sd((rows, cut), BF)] * 3 + pack,
            scratch_shapes=[pltpu.VMEM((length, length), F32)],
        )(spot_vec, labels, queries, keys, values, attended_grad, lse, delta, turned, *more)
        pieces.append(grads[:3])
        if early:
            keep, *sends = grads[3:]
        start += cut
    first, last = CUTS
    exact = 3 * first + width
    early, done = first_sum(keep, sends, exact, done, FIRST_WEIGHT)
    pack = sd((half, block, 3 * last + 128), BF)
    (tokens_grad, keep, send), done = kernel_call(
        partial(tokens_kernel, len(CUTS)),
        TOKENS_WEIGHT,
        done,
        vmem=TOKENS_VMEM,
        in_specs=[smem] + [vmem] * (8 + 3 * len(CUTS)),
        out_specs=[vmem] * 3,
        out_shape=[sd((rows, width), BF)] + [pack] * 2,
        scratch_shapes=[pltpu.VMEM((3, rows, width), BF), pltpu.VMEM((128, width), F32), pltpu.VMEM((width, 128), BF)],
    )(spot_vec, turned, layer_inputs_matrix, residual_grad, asker_matrix, lookup_label_matrix, content_matrix,
      gain_one, shift_one, *[piece for group_pieces in pieces for piece in group_pieces])
    (weight_sum, x_more, y_more), done = kernel_call(
        weight_second_kernel,
        MID_WEIGHT,
        done,
        vmem=SUM4_VMEM,
        in_specs=[pl.BlockSpec()] * 5,
        out_shape=[sd((block, 2 * hidden), F32)] + [half_rows] * 2,
    )(weight_own, x_keep, swap(x_send, "dp", 2), y_keep, swap(y_send, "dp", 4))
    late, done = first_sum(keep, [send], None, done, LATE_FIRST_WEIGHT)
    early, done = second_sum(early, place_vec, exact, done, SECOND_WEIGHT, True)
    x_more, y_more = held([x_more, y_more], done)
    late, done = second_sum(late, place_vec, None, done, LATE_SECOND_WEIGHT)
    (layer_output,), done = kernel_call(
        output_kernel,
        OUTPUT_WEIGHT,
        done,
        vmem=OUTPUT_VMEM,
        in_specs=[smem] + [vmem] * 4,
        out_specs=[vmem],
        out_shape=[sd((rows, width), BF)],
        scratch_shapes=[pltpu.VMEM((spots, width), BF)],
    )(place_vec, residual, weight, pos, produced_home)
    early, late = sent_on(early), sent_on(late)
    own = width // (dp_size * group)
    (query_grad, key_grad, value_grad, outer_grad, router_grad, norms, table_grad, sharp), done = kernel_call(
        partial(last_sum_kernel, first, last, route, group, experts_padded, (len(early), len(late))),
        1,
        done,
        vmem=SUM6_VMEM,
        in_specs=[pl.BlockSpec()] * (len(early) + len(late)),
        out_shape=[sd((own, width), F32)] * 4
        + [sd((own, route), F32), sd((4, own), F32), sd((group, route), F32), sd((1, 1), F32)],
    )(*early, *late)
    (hidden_grad, return_grad), done = kernel_call(
        weight_last_kernel,
        LAST_WEIGHT,
        done,
        vmem=SUM5_VMEM,
        in_specs=[pl.BlockSpec()] * 3,
        out_shape=[sd((block, hidden), F32), sd((hidden // dp_size, width), F32)],
    )(weight_sum, swap(x_more, "dp", 4), swap(y_more, "dp", 2))
    if group > 8:
        tiny = small_sum(tiny)
        table_grad, sharp = tiny[:group, :route], tiny[experts_padded, :1]
    return (
        layer_output,
        tokens_grad,
        norms[0],
        norms[1],
        query_grad,
        key_grad,
        value_grad,
        outer_grad,
        norms[2],
        norms[3],
        router_grad,
        table_grad,
        sharp.reshape(1),
        hidden_grad[None],
        return_grad[None],
    )


def solution(mesh):
    placed = (
        P(("dp", "expert"), None),
        P(("dp", "expert"), None),
        P(),
        P(),
        P(),
        P(),
        P(),
        P(),
        P(),
        P(),
        P(),
        P(),
        P(),
        P("expert", None, None),
        P("expert", None, None),
        P(("dp", "expert"), None),
        P(("dp", "expert"), None),
        P(("dp", "expert"), None),
    )
    return jax.shard_map(
        body,
        mesh=mesh,
        in_specs=placed,
        out_specs=(
            P(("dp", "expert"), None),
            P(("dp", "expert"), None),
            P(("dp", "expert")),
            P(("dp", "expert")),
            P(("dp", "expert"), None),
            P(("dp", "expert"), None),
            P(("dp", "expert"), None),
            P(("dp", "expert"), None),
            P(("dp", "expert")),
            P(("dp", "expert")),
            P(("dp", "expert"), None),
            P(),
            P(),
            P("expert", "dp", None),
            P("expert", "dp", None),
        ),
        check_vma=False,
    )
```

time: 376 us -> 308 us (0.82)
  waiting for transfers between devices: 89.5 us -> 45.1 us
  Pallas kernels: 210 us -> 174 us
  local copies, waits for them, and re-layouts: 25.6 us -> 36 us
    all_to_all x1, waiting for transfers between devices: 43.4 us -> 6.29 us  [body(): upstream_there = lax.all_to_all(upstream_sent, 'expert', 0, 0, tiled=True)]
    pallas_call x19 -> x24, Pallas kernels: 210 us -> 174 us  [made(): *outs, done = call(*args, *deps)]
    unnamed x66 -> x163, local copies, waits for them, and re-layouts: 13.1 us -> 32 us
    ppermute x13 -> x15, waiting for transfers between devices: 17.7 us -> 4.31 us  [swap(): return lax.ppermute(values, axis, [(i, i ^ mask) for i in range(size)])]
    all_to_all x1 -> x2, starting transfers between devices: 3.81 us -> 10.4 us  [the longest x1 5.22 us: sent_on(): return [parts[0], lax.all_to_all(parts[1], 'expert', 0, 0, tiled=True)]]
    slice x8 -> x0, local copies, waits for them, and re-layouts: 6.58 us -> none  [the longest x1 1.52 us: body(): early[:, 3 * first:exact]]
    ppermute x12 -> x9, waiting for transfers between devices: 28.3 us -> 34.5 us  [shift(): lax.ppermute(values, axis, [(i, (i + step) % size) for i in range(size)])]
    ppermute x12 -> x9, starting transfers between devices: 18.9 us -> 14.2 us  [shift(): lax.ppermute(values, axis, [(i, (i + step) % size) for i in range(size)])]
  transfers between devices with their start and end apart: 27 -> 27, of which waited for: 7 -> 8; matrix products, arithmetic and copies ran while one was open for 4% -> 2% of each run, Pallas kernels for 54% -> 52%
where the time goes in v3:
time: 308 us; the launch traced here: 304 us
  Pallas kernels  174 us (56%)
  waiting for transfers between devices  45.1 us (15%)
  starting transfers between devices  44.5 us (14%)
  local copies, waits for them, and re-layouts  36 us (12%)
    pallas_call x24, Pallas kernels, made(): *outs, done = call(*args, *deps)  174 us
    ppermute x9, waiting for transfers between devices, shift(): lax.ppermute(values, axis, [(i, (i + step) % size) for i in range(size)])  34.5 us
    unnamed x163, local copies, waits for them, and re-layouts  32 us
    ppermute x9, starting transfers between devices, shift(): lax.ppermute(values, axis, [(i, (i + step) % size) for i in range(size)])  14.2 us
    ppermute x15, starting transfers between devices, swap(): return lax.ppermute(values, axis, [(i, i ^ mask) for i in range(size)])  13.3 us
    all_to_all x1, starting transfers between devices, body(): upstream_there = lax.all_to_all(upstream_sent, 'expert', 0, 0, tiled=True)  6.63 us
    all_to_all x1, waiting for transfers between devices, body(): upstream_there = lax.all_to_all(upstream_sent, 'expert', 0, 0, tiled=True)  6.29 us
  transfers between devices with their start and end apart: 27, of which 8 were waited for; matrix products, arithmetic and copies ran while one was open for 2% of the time, Pallas kernels for 52%

profile of v3, /device:TPU:0, one launch (start us, length us, event | category | flops | bytes accessed | tf_op | source)
XLA Modules:
  0.0 303.6 jit_solution(15686189865352006596)
XLA Ops:
  1.3 1.4 copy-done.52
  3.4 5.1 %shard_map.289 = (s32[1,1024]{1,0:T(1,128)S(1)}, s32[1,1024]{1,0:T(1,128)S(1)}, bf16[4,400,768]{2,1,0:T(8,128)(2,1)}, f32[8,128]{1,0:T(8,128)}) custom-call(s32[1]{0:T(128)} %bitcast.refs_0_.refs_1_.refs_2_, s32[1,1024]{1,0:T(1,128)S(1)} %copy-done.64, s32[1,1024]{1,0:T(1,128)S(1)} %bitcast.21, bf16[1024,768]{1,0:T(8,128)(2,1)S(1)} %copy-done.52), custom_call_target="tpu_custom_call" | custom-call | flops 5368709120 | tf_op jit(solution)/shard_map/pallas_call | solution.py:82
  9.1 6.6 %all-to-all-start = ((bf16[4,400,768]{2,1,0:T(8,128)(2,1)}), bf16[4,400,768]{2,1,0:T(8,128)(2,1)S(1)}, u32[]{:S(2)}, u32[]{:S(2)}) async-start(bf16[4,400,768]{2,1,0:T(8,128)(2,1)} %get-tuple-element.133.refs_2_), calls=%async_computation | async-start | bytes 4915200 | tf_op jit(solution)/shard_map/all_to_all | solution.py:919
  20.7 28.9 %shard_map.290 = (bf16[768,1024]{1,0:T(8,128)(2,1)}, bf16[1024,768]{1,0:T(8,128)(2,1)}, bf16[1024,768]{1,0:T(8,128)(2,1)}, bf16[1024,768]{1,0:T(8,128)(2,1)}, bf...) custom-call(bf16[1024,768]{1,0:T(8,128)(2,1)} %refs_2_.1, ...), custom_call_target="tpu_custom_call" | custom-call | flops 21474836480 | tf_op jit(solution)/shard_map/pallas_call | solution.py:82
  49.6 1.1 copy-done.26
  50.7 13.3 %shard_map.291 = (bf16[4,384,768]{2,1,0:T(8,128)(2,1)}, bf16[400,768]{1,0:T(8,128)(2,1)S(1)}, bf16[384,3072]{1,0:T(8,128)(2,1)}, bf16[384,3072]{1,0:T(8,128)(2,1)}, f32[8,128]{1,0:T(8,128)S(1)}) custom-call(s32[1]{0:T(128)} %bitcast.4.refs_0_, s32[1]{0:T(128)} %bitcast.refs_0_.refs_1_.refs_2_, bf16[4,400,768]{2,1,0:T(8,128)(2,1)S(1)} %copy-done.18, ...), custom_call_target="tpu_custom_call" | custom-call | flops 10737418240 | tf_op jit(solution)/shard_map/pallas_call | solution.py:82
  65.4 6.3 %all-to-all-done.refs_2_.refs_3_ = bf16[4,400,768]{2,1,0:T(8,128)(2,1)S(1)} async-done(((bf16[4,400,768]{2,1,0:T(8,128)(2,1)}), bf16[4,400,768]{2,1,0:T(8,128)(2,1)S(1)}, u32[]{:S(2)}, u32[]{:S(2)}) %all-to-all-start) | async-done | bytes 2457632 | tf_op jit(solution)/shard_map/all_to_all | solution.py:919
  71.7 1.4 copy-done
  73.7 3.8 %collective-permute-start.1 = (bf16[400,768]{1,0:T(8,128)(2,1)}, bf16[400,768]{1,0:T(8,128)(2,1)S(1)}, u32[]{:S(2)}, u32[]{:S(2)}) collective-permute-start(bf16[400,768]{1,0:T(8,128)(2,1)} %get-tuple-element.143), channel_id=1, source_target_pairs={{0,3},{1,0},{2,1},{3,2},{4,7},{5,4},{6,5},{7,6},{8,11},{9,8},{10,9... | collective-permute-start | bytes 1843208 | tf_op jit(solution)/shard_map/ppermute | solution.py:766
  78.7 13.8 %collective-permute-done.refs_3_.refs_1_.refs_5_ = bf16[400,768]{1,0:T(8,128)(2,1)S(1)} collective-permute-done((bf16[400,768]{1,0:T(8,128)(2,1)}, bf16[400,768]{1,0:T(8,128)(2,1)S(1)}, u32[]{:S(2)}, u32[]{:S(2)}) %collective-permute-start) | collective-permute-done | bytes 614432 | tf_op jit(solution)/shard_map/ppermute | solution.py:766
  92.5 9.4 %collective-permute-done.1.refs_4_.refs_2_.refs_6_ = bf16[400,768]{1,0:T(8,128)(2,1)S(1)} collective-permute-done((bf16[400,768]{1,0:T(8,128)(2,1)}, bf16[400,768]{1,0:T(8,128)(2,1)S(1)}, u32[]{:S(2)}, u32[]{:S(2)}) %collective-permute-start.1) | collective-permute-done | bytes 614432 | tf_op jit(solution)/shard_map/ppermute | solution.py:766
  103.3 2.4 collective-permute-start.3
  105.7 1.1 copy-done.13
  106.8 1.1 copy-done.16
  107.9 23.2 %shard_map.293 = (bf16[4,384,768]{2,1,0:T(8,128)(2,1)}, bf16[400,768]{1,0:T(8,128)(2,1)}, bf16[400,768]{1,0:T(8,128)(2,1)}, bf16[768,3072]{1,0:T(8,128)(2,1)}, b...) custom-call(s32[4]{0:T(128)S(1)} %select_reduce_fusion.refs_0_, ...), custom_call_target="tpu_custom_call", output_to_operand_aliasing={{0}: (7, {})} | custom-call | flops 10737418240 | tf_op jit(solution)/shard_map/pallas_call | solution.py:82
  131.2 2.0 collective-permute-start.5
  133.2 13.1 %shard_map.295 = (bf16[4,384,768]{2,1,0:T(8,128)(2,1)}, bf16[400,768]{1,0:T(8,128)(2,1)}, bf16[384,3072]{1,0:T(8,128)(2,1)}, bf16[384,3072]{1,0:T(8,128)(2,1)}, f32[8,128]{1,0:T(8,128)}) custom-call(s32[4]{0:T(128)S(1)} %select_reduce_fusion.refs_0_, s32[1]{0:T(128)} %bitcast.refs_0_.refs_1_.refs_2_, ...), custom_call_target="tpu_custom_call", output_to_operand_aliasing={{0}: (6, {})} | custom-call | flops 10737418240 | tf_op jit(solution)/shard_map/pallas_call | solution.py:82
  147.5 1.1 copy-done.27
  148.5 1.1 copy-done.30
  149.6 12.4 %shard_map.297 = (bf16[4,96,3072]{2,1,0:T(8,128)(2,1)S(1)}, bf16[4,96,3072]{2,1,0:T(8,128)(2,1)}, f32[8,128]{1,0:T(8,128)S(1)}) custom-call(s32[4]{0:T(128)S(1)} %select_reduce_fusion.refs_0_, s32[1]{0:T(128)} %bitcast.7.refs_1_.refs_0_, bf16[400,768]{1,0:T(8,128)(2,1)S(1)} %copy-done.27, bf16[400,768]{1,0:T(8,128)(2,1)S(1)} %copy-done.14, ...), custom_call_target="tpu_custom_call" | custom-call | flops 5368709120 | tf_op jit(solution)/shard_map/pallas_call | solution.py:82
  162.2 12.8 %shard_map.298 = (bf16[4,768,384]{2,1,0:T(8,128)(2,1)S(1)}, bf16[4,768,384]{2,1,0:T(8,128)(2,1)}, f32[8,128]{1,0:T(8,128)}) custom-call(s32[4]{0:T(128)S(1)} %select_reduce_fusion.refs_0_, s32[1]{0:T(128)} %bitcast.7.refs_1_.refs_0_, s32[1]{0:T(128)} %bitcast.refs_0_.refs_1_.refs_2_, bf16[4,400,768]{2,1,0:T(8,128)(2,1)S(1)} %copy-done.1, ...), custom_call_target="tpu_custom_call" | custom-call | flops 1073741824 | tf_op jit(solution)/shard_map/pallas_call | solution.py:82
  175.5 9.0 %collective-permute-done.4.refs_16_ = bf16[400,768]{1,0:T(8,128)(2,1)} collective-permute-done((bf16[400,768]{1,0:T(8,128)(2,1)}, bf16[400,768]{1,0:T(8,128)(2,1)}, u32[]{:S(2)}, u32[]{:S(2)}) %collective-permute-start.4) | collective-permute-done | bytes 614432 | tf_op jit(solution)/shard_map/ppermute | solution.py:766
  184.6 12.1 %shard_map.296 = (f32[1,1024]{1,0:T(1,128)S(1)}, f32[1024,768]{1,0:T(8,128)S(1)}, bf16[1024,768]{1,0:T(8,128)(2,1)S(1)}, f32[16,1024]{1,0:T(8,128)S(1)}, bf16[76...) custom-call(f32[1]{0:T(128)S(6)} %copy.51.refs_12_.refs_0_, ...), custom_call_target="tpu_custom_call" | custom-call | flops 536870912000 | tf_op jit(solution)/shard_map/pallas_call | solution.py:82
  196.7 1.7 copy-done.10
  198.4 4.5 %shard_map.299 = (bf16[96,6144]{1,0:T(8,128)(2,1)S(1)}, bf16[96,3072]{1,0:T(8,128)(2,1)S(1)}, bf16[2,96,3072]{2,1,0:T(8,128)(2,1)S(1)}, bf16[96,3072]{1,0:T(8,12...) custom-call(bf16[4,96,3072]{2,1,0:T(8,128)(2,1)S(1)} %get-tuple-element.157.refs_0_, ...), custom_call_target="tpu_custom_call" | custom-call | flops 1073741824 | tf_op jit(solution)/shard_map/pallas_call | solution.py:82
  208.8 5.2 %all-to-all-start.1 = ((bf16[4,384,768]{2,1,0:T(8,128)(2,1)}), bf16[4,384,768]{2,1,0:T(8,128)(2,1)}, u32[]{:S(2)}, u32[]{:S(2)}) async-start(bf16[4,384,768]{2,1,0:T(8,128)(2,1)} %get-tuple-element.167), calls=%async_computation.1 | async-start | bytes 4718592 | tf_op jit(solution)/shard_map/all_to_all | solution.py:1039
  214.0 1.6 collective-permute-start.11
  215.6 1.5 collective-permute-start.12
  217.1 1.4 copy-done.4
  218.5 1.4 copy-done.5
  219.9 1.4 copy-done.7
  221.3 1.3 copy-done.24
  222.6 15.7 %shard_map.301 = (bf16[1024,512]{1,0:T(8,128)(2,1)S(1)}, bf16[1024,512]{1,0:T(8,128)(2,1)S(1)}, bf16[1024,512]{1,0:T(8,128)(2,1)S(1)}, bf16[4,96,2432]{2,1,0:T(8...) custom-call(s32[1]{0:T(128)} %bitcast.7.refs_1_.refs_0_, ...), custom_call_target="tpu_custom_call" | custom-call | flops 107374184 | tf_op jit(solution)/shard_map/pallas_call | solution.py:82
  238.9 6.1 %shard_map.302 = (bf16[1024,256]{1,0:T(8,128)(2,1)S(1)}, bf16[1024,256]{1,0:T(8,128)(2,1)S(1)}, bf16[1024,256]{1,0:T(8,128)(2,1)S(1)}, f32[8,128]{1,0:T(8,128)S(1)}) custom-call(s32[1]{0:T(128)} %bitcast.7.refs_1_.refs_0_, s32[2,1,512]{2,1,0:T(1,128)S(1)} %copy-done.35, bf16[1024,768]{1,0:T(8,128)(2,1)S(1)} %copy-done.3, bf16[1024,768]{1,0:T(8,128)(2,1)S(1)} %copy-done.4, ...), custom_call_target="tpu_custom_call" | custom-call | flops 107374184 | tf_op jit(solution)/shard_map/pallas_call | solution.py:82
  247.3 2.5 collective-permute-start.18
  249.8 10.2 %shard_map.304 = (bf16[1024,768]{1,0:T(8,128)(2,1)}, bf16[4,96,896]{2,1,0:T(8,128)(2,1)S(1)}, bf16[4,96,896]{2,1,0:T(8,128)(2,1)S(1)}, f32[8,128]{1,0:T(8,128)S(1)}) custom-call(s32[1]{0:T(128)} %bitcast.7.refs_1_.refs_0_, bf16[768,1024]{1,0:T(8,128)(2,1)S(1)} %copy-done.2, bf16[1024,768]{1,0:T(8,128)(2,1)S(1)} %copy-done.19, f32[1024,768]{1,0:T(8,128)S(1)} %copy-done.11, ...), custom_call_target="tpu_custom_call" | custom-call | flops 107374184 | tf_op jit(solution)/shard_map/pallas_call | solution.py:82
  260.6 1.6 collective-permute-done.10.refs_1_
  264.6 2.5 collective-permute-start.15
  267.1 1.8 collective-permute-done.17.refs_3_
  272.4 5.2 %all-to-all-start.2 = ((bf16[4,32,2432]{2,1,0:T(8,128)(2,1)}), bf16[4,32,2432]{2,1,0:T(8,128)(2,1)S(1)}, u32[]{:S(2)}, u32[]{:S(2)}) async-start(bf16[4,32,2432]{2,1,0:T(8,128)(2,1)} %copy-done.25), calls=%async_computation.2 | async-start | bytes 1245184 | tf_op jit(solution)/shard_map/all_to_all | solution.py:823
  278.2 1.5 collective-permute-start.22
  281.2 1.2 shard_map.308
  283.0 2.0 collective-permute-start.19
  285.0 2.4 collective-permute-start.20
  287.4 1.5 collective-permute-start.21
  288.9 5.9 %shard_map.309 = (bf16[1024,768]{1,0:T(8,128)(2,1)}, f32[8,128]{1,0:T(8,128)S(1)}) custom-call(s32[1]{0:T(128)} %bitcast.refs_0_.refs_1_.refs_2_, f32[1024,768]{1,0:T(8,128)S(1)} %copy-done.9, f32[1,1024]{1,0:T(1,128)S(1)} %get-tuple-element.152.refs_2_, s32[1,1024]{1,0:T(1,128)S(1)} %copy-done.43, bf16[4,384,768]{2,1,0:T(8,128)(2,1)} %all-to-all-done.1.refs_4_, ...), custom_call_target="tpu_custom_call" | custom-call | flops 107374184 | tf_op jit(solution)/shard_map/pallas_call | solution.py:82
  294.8 2.2 collective-permute-done.20.refs_4_
  299.9 3.5 %shard_map.312 = (f32[96,3072]{1,0:T(8,128)}, f32[384,768]{1,0:T(8,128)}, f32[8,128]{1,0:T(8,128)}) custom-call(f32[96,6144]{1,0:T(8,128)S(1)} %get-tuple-element.227.refs_0_, bf16[96,3072]{1,0:T(8,128)(2,1)} %collective-permute-done.22.refs_1_, bf16[96,3072]{1,0:T(8,128)(2,1)} %collective-permute-done.23.refs_2_, f32[8,128]{1,0:T(8,128)S(1)} %get-tuple-element.232.refs_3_), custom_call_target="tpu_custom_call" | custom-call | flops 107374184 | tf_op jit(solution)/shard_map/pallas_call | solution.py:82
  (210 shorter events, 33.4 us)
Async XLA Ops:
  9.1 10.9 %copy-start.47 = (s32[1024,1]{0,1:T(1,128)S(1)}, s32[1024,1]{0,1:T(1,128)}, u32[]{:S(2)}) copy-start(s32[1024,1]{0,1:T(1,128)} %param.36) | copy-start | bytes 12292
  9.1 62.5 %all-to-all-start = ((bf16[4,400,768]{2,1,0:T(8,128)(2,1)}), bf16[4,400,768]{2,1,0:T(8,128)(2,1)S(1)}, u32[]{:S(2)}, u32[]{:S(2)}) async-start(bf16[4,400,768]{2,1,0:T(8,128)(2,1)} %get-tuple-element.133.refs_2_), calls=%async_computation | async-start | bytes 4915200 | tf_op jit(solution)/shard_map/all_to_all | solution.py:919
  20.7 28.9 %copy-start.18 = (bf16[4,400,768]{2,1,0:T(8,128)(2,1)S(1)}, bf16[4,400,768]{2,1,0:T(8,128)(2,1)}, u32[]{:S(2)}) copy-start(bf16[4,400,768]{2,1,0:T(8,128)(2,1)} %get-tuple-element.133.refs_2_) | copy-start | bytes 7372804
  73.1 32.6 %copy-start.39 = (f32[8,128]{1,0:T(8,128)S(1)}, f32[8,128]{1,0:T(8,128)}, u32[]{:S(2)}) copy-start(f32[8,128]{1,0:T(8,128)} %copy-done.38) | copy-start | bytes 12292
  73.7 18.8 %collective-permute-start = (bf16[400,768]{1,0:T(8,128)(2,1)}, bf16[400,768]{1,0:T(8,128)(2,1)S(1)}, u32[]{:S(2)}, u32[]{:S(2)}) collective-permute-start(bf16[400,768]{1,0:T(8,128)(2,1)} %get-tuple-element.142), channel_id=1, source_target_pairs={{0,1},{1,2},{2,3},{3,0},{4,5},{5,6},{6,7},{7,4},{8,9},{9,10},{10,1... | collective-permute-start | bytes 1843208 | tf_op jit(solution)/shard_map/ppermute | solution.py:766
  73.7 28.2 %collective-permute-start.1 = (bf16[400,768]{1,0:T(8,128)(2,1)}, bf16[400,768]{1,0:T(8,128)(2,1)S(1)}, u32[]{:S(2)}, u32[]{:S(2)}) collective-permute-start(bf16[400,768]{1,0:T(8,128)(2,1)} %get-tuple-element.143), channel_id=1, source_target_pairs={{0,3},{1,0},{2,1},{3,2},{4,7},{5,4},{6,5},{7,6},{8,11},{9,8},{10,9... | collective-permute-start | bytes 1843208 | tf_op jit(solution)/shard_map/ppermute | solution.py:766
  103.3 29.8 %collective-permute-start.3 = (bf16[400,768]{1,0:T(8,128)(2,1)}, bf16[400,768]{1,0:T(8,128)(2,1)S(1)}, u32[]{:S(2)}, u32[]{:S(2)}) collective-permute-start(bf16[400,768]{1,0:T(8,128)(2,1)} %get-tuple-element.147), channel_id=1, source_target_pairs={{0,2},{1,3},{2,0},{3,1},{4,6},{5,7},{6,4},{7,5},{8,10},{9,11},{10,... | collective-permute-start | bytes 1843208 | tf_op jit(solution)/shard_map/ppermute | solution.py:766
  107.9 25.3 %copy-start.1 = (bf16[4,400,768]{2,1,0:T(8,128)(2,1)S(1)}, bf16[4,400,768]{2,1,0:T(8,128)(2,1)}, u32[]{:S(2)}) copy-start(bf16[4,400,768]{2,1,0:T(8,128)(2,1)} %copy-done) | copy-start | bytes 7372804
  131.1 30.9 %collective-permute-start.2 = (bf16[400,768]{1,0:T(8,128)(2,1)}, bf16[400,768]{1,0:T(8,128)(2,1)}, u32[]{:S(2)}, u32[]{:S(2)}) collective-permute-start(bf16[400,768]{1,0:T(8,128)(2,1)} %get-tuple-element.145), channel_id=1, source_target_pairs={{0,3},{1,0},{2,1},{3,2},{4,7},{5,4},{6,5},{7,6},{8,11},{9,8},{10,9... | collective-permute-start | bytes 1843208 | tf_op jit(solution)/shard_map/ppermute | solution.py:766
  131.2 30.8 %collective-permute-start.5 = (bf16[400,768]{1,0:T(8,128)(2,1)}, bf16[400,768]{1,0:T(8,128)(2,1)}, u32[]{:S(2)}, u32[]{:S(2)}) collective-permute-start(bf16[400,768]{1,0:T(8,128)(2,1)} %get-tuple-element.151), channel_id=1, source_target_pairs={{0,1},{1,2},{2,3},{3,0},{4,5},{5,6},{6,7},{7,4},{8,9},{9,10},{10,1... | collective-permute-start | bytes 1843208 | tf_op jit(solution)/shard_map/ppermute | solution.py:766
  133.2 13.1 %copy-start.29 = (bf16[400,768]{1,0:T(8,128)(2,1)}, bf16[400,768]{1,0:T(8,128)(2,1)S(1)}, u32[]{:S(2)}) copy-start(bf16[400,768]{1,0:T(8,128)(2,1)S(1)} %collective-permute-done.3.refs_3_.refs_5_.refs_7_) | copy-start | bytes 1843204
  133.2 13.2 %copy-start.14 = (bf16[400,768]{1,0:T(8,128)(2,1)S(1)}, bf16[400,768]{1,0:T(8,128)(2,1)}, u32[]{:S(2)}) copy-start(bf16[400,768]{1,0:T(8,128)(2,1)} %copy-done.12) | copy-start | bytes 1843204
  146.3 38.2 %collective-permute-start.4 = (bf16[400,768]{1,0:T(8,128)(2,1)}, bf16[400,768]{1,0:T(8,128)(2,1)}, u32[]{:S(2)}, u32[]{:S(2)}) collective-permute-start(bf16[400,768]{1,0:T(8,128)(2,1)} %get-tuple-element.150), channel_id=1, source_target_pairs={{0,2},{1,3},{2,0},{3,1},{4,6},{5,7},{6,4},{7,5},{8,10},{9,11},{10,... | collective-permute-start | bytes 1843208 | tf_op jit(solution)/shard_map/ppermute | solution.py:766
  149.6 12.4 %copy-start.28 = (bf16[400,768]{1,0:T(8,128)(2,1)S(1)}, bf16[400,768]{1,0:T(8,128)(2,1)}, u32[]{:S(2)}) copy-start(bf16[400,768]{1,0:T(8,128)(2,1)} %get-tuple-element.137.refs_3_.refs_2_.refs_4_) | copy-start | bytes 1843204
  149.6 12.4 %copy-start.31 = (bf16[400,768]{1,0:T(8,128)(2,1)S(1)}, bf16[400,768]{1,0:T(8,128)(2,1)}, u32[]{:S(2)}) copy-start(bf16[400,768]{1,0:T(8,128)(2,1)} %copy-done.29) | copy-start | bytes 1843204
  162.0 36.4 %collective-permute-start.6 = (bf16[4,96,3072]{2,1,0:T(8,128)(2,1)}, bf16[4,96,3072]{2,1,0:T(8,128)(2,1)}, u32[]{:S(2)}, u32[]{:S(2)}) collective-permute-start(bf16[4,96,3072]{2,1,0:T(8,128)(2,1)} %get-tuple-element.158), channel_id=1, source_target_pairs={{0,4},{4,0},{8,12},{12,8},{16,20},{20,16},{24,28},{28,24},{1,5},{5... | collective-permute-start | bytes 7077896 | tf_op jit(solution)/shard_map/ppermute | solution.py:761
  162.0 22.5 %copy-start.8 = (f32[1024,768]{1,0:T(8,128)S(1)}, f32[1024,768]{1,0:T(8,128)}, u32[]{:S(2)}) copy-start(f32[1024,768]{1,0:T(8,128)} %get-tuple-element.132.refs_5_.refs_1_) | copy-start | bytes 9437188
  162.0 22.5 %copy-start.43 = (s32[1,1024]{1,0:T(1,128)S(1)}, s32[1,1024]{1,0:T(1,128)}, u32[]{:S(2)}) copy-start(s32[1,1024]{1,0:T(1,128)} %copy-done.42) | copy-start | bytes 12292
  162.0 22.5 %copy-start.48 = (s32[1024,1]{0,1:T(1,128)S(1)}, s32[1024,1]{0,1:T(1,128)}, u32[]{:S(2)}) copy-start(s32[1024,1]{0,1:T(1,128)} %param.36) | copy-start | bytes 12292
  162.1 22.5 %copy-start.49 = (f32[8,16]{1,0:T(8,128)S(1)}, f32[8,16]{1,0:T(8,128)}, u32[]{:S(2)}) copy-start(f32[8,16]{1,0:T(8,128)} %scatter.4.refs_11_.refs_9_) | copy-start | bytes 1540
  162.1 22.5 %copy-start.50 = (f32[1,768]{1,0:T(1,128)S(1)}, f32[1,768]{1,0:T(1,128)}, u32[]{:S(2)}) copy-start(f32[1,768]{1,0:T(1,128)} %reshape.138.refs_8_.refs_11_) | copy-start | bytes 9220
  162.1 22.5 %copy-start.51 = (f32[1,768]{1,0:T(1,128)S(1)}, f32[1,768]{1,0:T(1,128)}, u32[]{:S(2)}) copy-start(f32[1,768]{1,0:T(1,128)} %reshape.139.refs_9_.refs_12_) | copy-start | bytes 9220
  162.1 22.5 %copy-start.53 = (bf16[1024,768]{1,0:T(8,128)(2,1)S(1)}, bf16[1024,768]{1,0:T(8,128)(2,1)}, u32[]{:S(2)}) copy-start(bf16[1024,768]{1,0:T(8,128)(2,1)} %refs_6_.4) | copy-start | bytes 4718596
  162.1 22.5 %copy-start.54 = (bf16[768,768]{1,0:T(8,128)(2,1)S(1)}, bf16[768,768]{1,0:T(8,128)(2,1)}, u32[]{:S(2)}) copy-start(bf16[768,768]{1,0:T(8,128)(2,1)} %refs_13_.1) | copy-start | bytes 3538948
  162.1 22.5 %copy-start.63 = (f32[768,16]{0,1:T(8,128)S(1)}, f32[768,16]{0,1:T(8,128)}, u32[]{:S(2)}) copy-start(f32[768,16]{0,1:T(8,128)} %param.30) | copy-start | bytes 147460
  162.1 22.5 %copy-start.72 = (bf16[400,768]{1,0:T(8,128)(2,1)S(1)}, bf16[400,768]{1,0:T(8,128)(2,1)}, u32[]{:S(2)}) copy-start(bf16[400,768]{1,0:T(8,128)(2,1)} %copy-done.71) | copy-start | bytes 1843204
  162.1 22.5 %copy-start.73 = (bf16[1024,768]{1,0:T(8,128)(2,1)S(1)}, bf16[1024,768]{1,0:T(8,128)(2,1)}, u32[]{:S(2)}) copy-start(bf16[1024,768]{1,0:T(8,128)(2,1)} %get-tuple-element.135.refs_7_) | copy-start | bytes 4718596
  162.1 22.5 %copy-start.74 = (f32[16,1024]{1,0:T(8,128)S(1)}, f32[16,1024]{1,0:T(8,128)}, u32[]{:S(2)}) copy-start(f32[16,1024]{1,0:T(8,128)} %get-tuple-element.136.refs_8_) | copy-start | bytes 196612
  175.0 23.4 %collective-permute-start.7 = (bf16[4,768,384]{2,1,0:T(8,128)(2,1)}, bf16[4,768,384]{2,1,0:T(8,128)(2,1)}, u32[]{:S(2)}, u32[]{:S(2)}) collective-permute-start(bf16[4,768,384]{2,1,0:T(8,128)(2,1)} %get-tuple-element.164), channel_id=1, source_target_pairs={{0,4},{4,0},{8,12},{12,8},{16,20},{20,16},{24,28},{28,24},{1,5},{5... | collective-permute-start | bytes 7077896 | tf_op jit(solution)/shard_map/ppermute | solution.py:761
  208.8 63.6 %all-to-all-start.1 = ((bf16[4,384,768]{2,1,0:T(8,128)(2,1)}), bf16[4,384,768]{2,1,0:T(8,128)(2,1)}, u32[]{:S(2)}, u32[]{:S(2)}) async-start(bf16[4,384,768]{2,1,0:T(8,128)(2,1)} %get-tuple-element.167), calls=%async_computation.1 | async-start | bytes 4718592 | tf_op jit(solution)/shard_map/all_to_all | solution.py:1039
  214.0 46.0 %collective-permute-start.11 = (bf16[2,96,3072]{2,1,0:T(8,128)(2,1)}, bf16[2,96,3072]{2,1,0:T(8,128)(2,1)S(1)}, u32[]{:S(2)}, u32[]{:S(2)}) collective-permute-start(bf16[2,96,3072]{2,1,0:T(8,128)(2,1)} %copy-done.58), channel_id=1, source_target_pairs={{0,8},{4,12},{8,0},{12,4},{16,24},{20,28},{24,16},{28,20},{1,9},{5... | collective-permute-start | bytes 3538952 | tf_op jit(solution)/shard_map/ppermute | solution.py:761
  215.6 44.5 %collective-permute-start.12 = (bf16[2,96,3072]{2,1,0:T(8,128)(2,1)}, bf16[2,96,3072]{2,1,0:T(8,128)(2,1)S(1)}, u32[]{:S(2)}, u32[]{:S(2)}) collective-permute-start(bf16[2,96,3072]{2,1,0:T(8,128)(2,1)} %copy-done.57), channel_id=1, source_target_pairs={{0,16},{4,20},{8,24},{12,28},{16,0},{20,4},{24,8},{28,12},{1,17},{... | collective-permute-start | bytes 3538952 | tf_op jit(solution)/shard_map/ppermute | solution.py:761
  238.3 6.8 %collective-permute-start.8 = (bf16[2,96,2432]{2,1,0:T(8,128)(2,1)S(1)}, bf16[2,96,2432]{2,1,0:T(8,128)(2,1)S(1)}, u32[]{:S(2)}, u32[]{:S(2)}) collective-permute-start(bf16[2,96,2432]{2,1,0:T(8,128)(2,1)S(1)} %get-tuple-element.186), channel_id=1, source_target_pairs={{0,4},{4,0},{8,12},{12,8},{16,20},{20,16},{24,28},{28,24},{1,5},{5... | collective-permute-start | bytes 2801672 | tf_op jit(solution)/shard_map/ppermute | solution.py:761
  238.4 6.7 %collective-permute-start.9 = (bf16[2,96,2432]{2,1,0:T(8,128)(2,1)S(1)}, bf16[2,96,2432]{2,1,0:T(8,128)(2,1)S(1)}, u32[]{:S(2)}, u32[]{:S(2)}) collective-permute-start(bf16[2,96,2432]{2,1,0:T(8,128)(2,1)S(1)} %get-tuple-element.187), channel_id=1, source_target_pairs={{0,4},{4,0},{8,12},{12,8},{16,20},{20,16},{24,28},{28,24},{1,5},{5... | collective-permute-start | bytes 2801672 | tf_op jit(solution)/shard_map/ppermute | solution.py:761
  238.9 10.8 %copy-start.22 = (bf16[768,768]{1,0:T(8,128)(2,1)S(1)}, bf16[768,768]{1,0:T(8,128)(2,1)}, u32[]{:S(2)}) copy-start(bf16[768,768]{1,0:T(8,128)(2,1)} %refs_6_.5) | copy-start | bytes 3538948
  246.2 18.5 %collective-permute-start.16 = (bf16[96,2432]{1,0:T(8,128)(2,1)S(1)}, bf16[96,2432]{1,0:T(8,128)(2,1)S(1)}, u32[]{:S(2)}, u32[]{:S(2)}) collective-permute-start(bf16[96,2432]{1,0:T(8,128)(2,1)S(1)} %get-tuple-element.204), channel_id=1, source_target_pairs={{0,8},{4,12},{8,0},{12,4},{16,24},{20,28},{24,16},{28,20},{1,9},{5... | collective-permute-start | bytes 1400840 | tf_op jit(solution)/shard_map/ppermute | solution.py:761
  246.8 22.1 %collective-permute-start.17 = (bf16[96,2432]{1,0:T(8,128)(2,1)S(1)}, bf16[96,2432]{1,0:T(8,128)(2,1)S(1)}, u32[]{:S(2)}, u32[]{:S(2)}) collective-permute-start(bf16[96,2432]{1,0:T(8,128)(2,1)S(1)} %get-tuple-element.205), channel_id=1, source_target_pairs={{0,16},{4,20},{8,24},{12,28},{16,0},{20,4},{24,8},{28,12},{1,17},{... | collective-permute-start | bytes 1400840 | tf_op jit(solution)/shard_map/ppermute | solution.py:761
  247.3 22.5 %collective-permute-start.18 = (bf16[96,2432]{1,0:T(8,128)(2,1)S(1)}, bf16[96,2432]{1,0:T(8,128)(2,1)S(1)}, u32[]{:S(2)}, u32[]{:S(2)}) collective-permute-start(bf16[96,2432]{1,0:T(8,128)(2,1)S(1)} %get-tuple-element.206), channel_id=1, source_target_pairs={{0,24},{4,28},{8,16},{12,20},{16,8},{20,12},{24,0},{28,4},{1,25},{... | collective-permute-start | bytes 1400840 | tf_op jit(solution)/shard_map/ppermute | solution.py:761
  260.0 2.1 collective-permute-start.10
  263.6 16.6 %collective-permute-start.13 = (bf16[96,896]{1,0:T(8,128)(2,1)}, bf16[96,896]{1,0:T(8,128)(2,1)S(1)}, u32[]{:S(2)}, u32[]{:S(2)}) collective-permute-start(bf16[96,896]{1,0:T(8,128)(2,1)} %get-tuple-element.200), channel_id=1, source_target_pairs={{0,8},{4,12},{8,0},{12,4},{16,24},{20,28},{24,16},{28,20},{1,9},{5... | collective-permute-start | bytes 516104 | tf_op jit(solution)/shard_map/ppermute | solution.py:761
  264.1 16.1 %collective-permute-start.14 = (bf16[96,896]{1,0:T(8,128)(2,1)}, bf16[96,896]{1,0:T(8,128)(2,1)S(1)}, u32[]{:S(2)}, u32[]{:S(2)}) collective-permute-start(bf16[96,896]{1,0:T(8,128)(2,1)} %get-tuple-element.201), channel_id=1, source_target_pairs={{0,16},{4,20},{8,24},{12,28},{16,0},{20,4},{24,8},{28,12},{1,17},{... | collective-permute-start | bytes 516104 | tf_op jit(solution)/shard_map/ppermute | solution.py:761
  264.6 15.6 %collective-permute-start.15 = (bf16[96,896]{1,0:T(8,128)(2,1)S(1)}, bf16[96,896]{1,0:T(8,128)(2,1)}, u32[]{:S(2)}, u32[]{:S(2)}) collective-permute-start(bf16[96,896]{1,0:T(8,128)(2,1)S(1)} %get-tuple-element.202), channel_id=1, source_target_pairs={{0,24},{4,28},{8,16},{12,20},{16,8},{20,12},{24,0},{28,4},{1,25},{... | collective-permute-start | bytes 516104 | tf_op jit(solution)/shard_map/ppermute | solution.py:761
  272.4 24.7 %all-to-all-start.2 = ((bf16[4,32,2432]{2,1,0:T(8,128)(2,1)}), bf16[4,32,2432]{2,1,0:T(8,128)(2,1)S(1)}, u32[]{:S(2)}, u32[]{:S(2)}) async-start(bf16[4,32,2432]{2,1,0:T(8,128)(2,1)} %copy-done.25), calls=%async_computation.2 | async-start | bytes 1245184 | tf_op jit(solution)/shard_map/all_to_all | solution.py:823
  278.2 21.7 %collective-permute-start.22 = (bf16[96,3072]{1,0:T(8,128)(2,1)}, bf16[96,3072]{1,0:T(8,128)(2,1)}, u32[]{:S(2)}, u32[]{:S(2)}) collective-permute-start(bf16[96,3072]{1,0:T(8,128)(2,1)} %get-tuple-element.230), channel_id=1, source_target_pairs={{0,16},{4,20},{8,24},{12,28},{16,0},{20,4},{24,8},{28,12},{1,17},{... | collective-permute-start | bytes 1769480 | tf_op jit(solution)/shard_map/ppermute | solution.py:761
  279.7 20.2 %collective-permute-start.23 = (bf16[96,3072]{1,0:T(8,128)(2,1)}, bf16[96,3072]{1,0:T(8,128)(2,1)}, u32[]{:S(2)}, u32[]{:S(2)}) collective-permute-start(bf16[96,3072]{1,0:T(8,128)(2,1)} %get-tuple-element.231), channel_id=1, source_target_pairs={{0,8},{4,12},{8,0},{12,4},{16,24},{20,28},{24,16},{28,20},{1,9},{5... | collective-permute-start | bytes 1769480 | tf_op jit(solution)/shard_map/ppermute | solution.py:761
  283.0 11.8 %collective-permute-start.19 = (bf16[32,896]{1,0:T(8,128)(2,1)S(1)}, bf16[32,896]{1,0:T(8,128)(2,1)S(1)}, u32[]{:S(2)}, u32[]{:S(2)}) collective-permute-start(bf16[32,896]{1,0:T(8,128)(2,1)S(1)} %get-tuple-element.215), channel_id=1, source_target_pairs={{0,1},{1,2},{2,3},{3,0},{4,5},{5,6},{6,7},{7,4},{8,9},{9,10},{10,1... | collective-permute-start | bytes 172040 | tf_op jit(solution)/shard_map/ppermute | solution.py:766
  285.0 12.0 %collective-permute-start.20 = (bf16[32,896]{1,0:T(8,128)(2,1)S(1)}, bf16[32,896]{1,0:T(8,128)(2,1)S(1)}, u32[]{:S(2)}, u32[]{:S(2)}) collective-permute-start(bf16[32,896]{1,0:T(8,128)(2,1)S(1)} %get-tuple-element.216), channel_id=1, source_target_pairs={{0,2},{1,3},{2,0},{3,1},{4,6},{5,7},{6,4},{7,5},{8,10},{9,11},{10,... | collective-permute-start | bytes 172040 | tf_op jit(solution)/shard_map/ppermute | solution.py:766
  287.4 9.6 %collective-permute-start.21 = (bf16[32,896]{1,0:T(8,128)(2,1)S(1)}, bf16[32,896]{1,0:T(8,128)(2,1)S(1)}, u32[]{:S(2)}, u32[]{:S(2)}) collective-permute-start(bf16[32,896]{1,0:T(8,128)(2,1)S(1)} %get-tuple-element.217), channel_id=1, source_target_pairs={{0,3},{1,0},{2,1},{3,2},{4,7},{5,4},{6,5},{7,6},{8,11},{9,8},{10,9... | collective-permute-start | bytes 172040 | tf_op jit(solution)/shard_map/ppermute | solution.py:766
  (60 other events, 263.4 us)

commit v4 on v3

--- a/solution.py
+++ b/solution.py
@@ -19,15 +19,15 @@
 SCORE_VMEM = 12
 TOKENS_VMEM = 18
 OUTPUT_VMEM = 10
-WIDE_VMEM = 36
-NARROW_VMEM = 36
+WIDE_VMEM = 28
+NARROW_VMEM = 28
 SUM1_VMEM = 8
 SUM2_VMEM = 8
 SUM3_VMEM = 10
 SUM4_VMEM = 8
 SUM5_VMEM = 8
 SUM6_VMEM = 8
-EXPERT_VMEM = (36, 50)
+EXPERT_VMEM = (28, 38)
 NN = (((1,), (0,)), ((), ()))
 NT = (((1,), (1,)), ((), ()))
 TN = (((0,), (0,)), ((), ()))
@@ -53,12 +53,16 @@
     )
 
 
-def kernel_call(body, weight, deps=(), vmem=56, **kwargs):
+def kernel_call(body, weight, deps=(), vmem=2, **kwargs):
     deps = jax.tree.leaves(deps)
     inputs, outputs = len(kwargs["in_specs"]), len(kwargs["out_shape"])
     first = inputs + len(deps)
-    any_spec = pl.BlockSpec(memory_space=pl.ANY)
-    kwargs["in_specs"] = list(kwargs["in_specs"]) + [any_spec] * len(deps)
+    kwargs["in_specs"] = list(kwargs["in_specs"]) + [
+        pl.BlockSpec((1,) * (dep.ndim - 2) + (min(16, dep.shape[-2]), 128), lambda *_, rank=dep.ndim: (0,) * rank)
+        if dep.ndim > 1 and "grid" in kwargs
+        else pl.BlockSpec(memory_space=pl.ANY)
+        for dep in deps
+    ]
     kwargs["out_shape"] = list(kwargs["out_shape"]) + [jax.ShapeDtypeStruct((8, 128), F32)]
     if "out_specs" in kwargs:
         done_spec = whole((8, 128)) if "grid" in kwargs else pl.BlockSpec(memory_space=pltpu.VMEM)
@@ -178,7 +182,7 @@
             largest = jnp.max(scores, axis=-1, keepdims=True)
             weights = jnp.exp(scores - largest)
             total = jnp.sum(weights, axis=-1, keepdims=True)
-            outs.append(mxu(weights.astype(BF), v_pair) * (1.0 / total))
+            outs.append(mxu((weights * (1.0 / total)).astype(BF), v_pair))
             lse_cols = jnp.where(lane == pair * 2 + half, largest + jnp.log(total), lse_cols)
         att_ref[:, columns] = jnp.where(low_lanes, outs[0], outs[1]).astype(BF)
     lse_cols_ref[...] = lse_cols
@@ -237,13 +241,13 @@
     return lax.rem(place_ref[0] - k + group, group)
 
 
-def expert_kernel(ids, past, block, counts_ref, place_ref, u_ref, *refs):
+def expert_kernel(ids, block, counts_ref, place_ref, u_ref, *refs):
     chunks = len(ids)
     x_refs = refs[:chunks]
     wide_ref, narrow_ref = refs[chunks : chunks + 2]
-    rest = refs[chunks + 2 + past :]
-    out_ref, back_refs = rest[0], rest[1 : 1 + chunks]
-    act_ref, pre_ref, xs, us, out_sum, back_sum, sums, outs, sent = rest[1 + chunks :]
+    rest = refs[chunks + 2 :]
+    out_refs, back_refs = rest[:chunks], rest[chunks : 2 * chunks]
+    act_ref, pre_ref, xs, us, out_sum, back_sum, sums = rest[2 * chunks :]
     step, steps = pl.program_id(0), pl.num_programs(0)
     rows = x_refs[0].shape[0] - TAIL
     offsets, total = pack_offsets(counts_ref, ids)
@@ -288,16 +292,9 @@
         out = out_sum[...].astype(BF).astype(F32)
         gates = jnp.sum(out * us[...].astype(F32), axis=1, keepdims=True)
         sums[...] = jnp.broadcast_to(gates, sums.shape)
-        moves = []
         for k in range(chunks):
             here = pl.ds(offsets[k], rows)
-            outs[k] = out_sum[here, :].astype(BF)
-            moves.append(
-                pltpu.make_async_copy(
-                    outs.at[k], out_ref.at[source_of(place_ref, ids[k], u_ref.shape[0])], sent.at[k]
-                )
-            )
-            moves[k].start()
+            out_refs[k][...] = out_sum[here, :].astype(BF)
             back_refs[k][:rows, :] = back_sum[here, :].astype(BF)
             gate = jnp.transpose(sums[here, :])[:1]
             high = gate.astype(BF).astype(F32)
@@ -306,35 +303,31 @@
             tail = jnp.where(place == 0, high, jnp.where(place == 1, mid, jnp.where(place == 2, gate - high - mid, 0.0)))
             tail = jnp.concatenate([tail, jnp.zeros((TAIL, out.shape[1] - rows), F32)], axis=1)
             back_refs[k][rows:, :] = tail.astype(BF)
-        for move in moves:
-            move.wait()
-
-
-def expert_call(counts, place, ids, past, xs, us, wide, narrow, deps, block=384, parts=4):
+
+
+def expert_call(counts, place, ids, xs, us, wide, narrow, deps, block=384, parts=4):
     chunks, (tailed, width), hidden = len(xs), xs[0].shape, wide.shape[1]
     rows = tailed - TAIL
     cut, most = hidden // parts, chunks * rows
     sd = jax.ShapeDtypeStruct
-    smem, anywhere = (pl.BlockSpec(memory_space=space) for space in (pltpu.SMEM, pl.ANY))
-    chunk, every = whole((tailed, width)), (us.shape[0], rows, width)
+    smem = pl.BlockSpec(memory_space=pltpu.SMEM)
+    chunk, plain = whole((tailed, width)), whole((rows, width))
     inner = pl.BlockSpec((most, cut), lambda f: (0, f))
     outs, done = kernel_call(
-        partial(expert_kernel, ids, len(past), block),
+        partial(expert_kernel, ids, block),
         10,
         deps,
         vmem=EXPERT_VMEM[len(ids) - 1],
         grid=(parts,),
         in_specs=[smem] * 2 + [whole(us.shape)] + [chunk] * chunks
-        + [pl.BlockSpec((width, cut), lambda f: (0, f)), pl.BlockSpec((cut, width), lambda f: (f, 0))]
-        + [anywhere] * len(past),
-        out_specs=[anywhere] + [chunk] * chunks + [inner, inner],
-        out_shape=[pltpu.HBM(every, BF)] + [sd((tailed, width), BF)] * chunks + [pltpu.HBM((most, hidden), BF)] * 2,
-        input_output_aliases={5 + chunks: 0} if past else {},
+        + [pl.BlockSpec((width, cut), lambda f: (0, f)), pl.BlockSpec((cut, width), lambda f: (f, 0))],
+        out_specs=[plain] * chunks + [chunk] * chunks + [inner, inner],
+        out_shape=[pltpu.HBM((rows, width), BF)] * chunks + [sd((tailed, width), BF)] * chunks
+        + [pltpu.HBM((most, hidden), BF)] * 2,
         scratch_shapes=[pltpu.VMEM((most, width), BF)] * 2
-        + [pltpu.VMEM((most, width), F32)] * 2 + [pltpu.VMEM((most, 128), F32)]
-        + [pltpu.VMEM((chunks, rows, width), BF), pltpu.SemaphoreType.DMA((chunks,))],
-    )(counts, place, us, *xs, hbm(wide), hbm(narrow), *map(hbm, past))
-    return outs[0], outs[1 : 1 + chunks], outs[-2], outs[-1], done
+        + [pltpu.VMEM((most, width), F32)] * 2 + [pltpu.VMEM((most, 128), F32)],
+    )(counts, place, us, *xs, hbm(wide), hbm(narrow))
+    return outs[:chunks], outs[chunks : 2 * chunks], outs[-2], outs[-1], done
 
 
 def pack_weighed(ids, counts_ref, x_refs, rows_of, depth, packed_ref, turned_ref):
@@ -608,7 +601,7 @@
 
 def score_back_kernel(first, pairs, weights, spot_ref, label_ref, q_ref, k_ref, v_ref, att_grad_ref, lse_ref, delta_ref,
                       turned_ref, *refs):
-    count = 3 + 3 * weights
+    count = 3 + (1 + SENDS) * weights
     more_refs, out_refs, bias_ref = refs[: -1 - count], refs[-1 - count : -1], refs[-1]
     dq_ref, dk_ref, dv_ref = out_refs[:3]
     rows = label_ref.shape[2]
@@ -743,10 +736,11 @@
     sharp_ref[...] = extra[EXACT + experts_padded : EXACT + experts_padded + 1, :1]
 
 
-def output_kernel(place_ref, residual_ref, weight_ref, pos_ref, out_ref, layer_ref, spots_ref):
-    chunks, slots = out_ref.shape[:2]
-    for k in range(chunks):
-        spots_ref[k * slots : (k + 1) * slots, :] = out_ref[lax.rem(place_ref[0] + k, chunks)]
+def output_kernel(residual_ref, weight_ref, pos_ref, *refs):
+    out_refs, layer_ref, spots_ref = refs[:-2], refs[-2], refs[-1]
+    slots = out_refs[0].shape[0]
+    for k, out_ref in enumerate(out_refs):
+        spots_ref[k * slots : (k + 1) * slots, :] = out_ref[...]
     rows = residual_ref.shape[0]
     both = jnp.concatenate([pos_ref[...].astype(F32), weight_ref[...], jnp.zeros((126, rows), F32)], axis=0)
     both = jnp.transpose(both)
@@ -776,11 +770,16 @@
         lambda *refs: None,
         0,
         deps,
+        grid=(1,),
         in_specs=[anywhere] * len(arrays),
         out_specs=[anywhere] * len(arrays),
         out_shape=[jax.ShapeDtypeStruct(array.shape, array.dtype) for array in arrays],
         input_output_aliases={k: k for k in range(len(arrays))},
-    )(*arrays)[0]
+    )(*arrays)
+
+
+def seen(arrays):
+    return kernel_call(lambda *refs: None, 0, jax.tree.leaves(arrays), grid=(1,), in_specs=[], out_specs=[], out_shape=[])()[1]
 
 
 def first_sum(keep, sends, exact, deps, weight):
@@ -849,6 +848,7 @@
 WAYS = 4
 SETS = ((0,), (1, 3), (2,))
 CUTS = (512, 256)
+SENDS = 2
 D0_WEIGHT, D1_WEIGHT, FIRST_WEIGHT, TOKENS_WEIGHT = 0.1, 0.1, 0.05, 0.1
 MID_WEIGHT, LATE_FIRST_WEIGHT, SECOND_WEIGHT, LATE_SECOND_WEIGHT, LAST_WEIGHT, OUTPUT_WEIGHT = 18, 1, 1, 7, 0.1, 0.1
 
@@ -946,15 +946,12 @@
     counts = jnp.sum(jnp.where(relative[:, None] == sources[None, :], counts[None, :], 0), axis=1)
 
     each = group // WAYS
-    backs, produced, acts, pres, order = [None] * WAYS, [], [], [], []
+    backs, produced, acts, pres, order = [None] * WAYS, [None] * WAYS, [], [], []
 
     def experts(ids, counts, entered, graded, turn, deps):
-        out, some, act, pre, done = expert_call(
-            counts, turn, ids, produced, entered, graded, wide, narrow, [deps, order]
-        )
-        produced[:] = [out]
-        for k, back in zip(ids, some):
-            backs[k] = back
+        outs, some, act, pre, done = expert_call(counts, turn, ids, entered, graded, wide, narrow, [deps, order])
+        for k, out, back in zip(ids, outs, some):
+            produced[k], backs[k] = out, back
         acts.append(act)
         pres.append(pre)
         order.append(done)
@@ -964,9 +961,9 @@
         turn_vec, graded, entered = place_vec, upstream_there, list(entering_sent)
         alone = jnp.sum((chosen == place).astype(int32)).reshape(1)
         experts(SETS[0], alone, entered[:1], upstream_sent, turn_vec, ())
-        ready = upstream_there
+        ready = []
         for ids in SETS[1:]:
-            for k, sent in zip(ids, held([entered[k] for k in ids], [ready, order[0]])):
+            for k, sent in zip(ids, held([entered[k] for k in ids], ready)[0] if ready else [entered[k] for k in ids]):
                 entered[k] = shift(sent, "expert", k)
             ready = [entered[k] for k in ids]
         for ids in SETS[1:]:
@@ -1033,21 +1030,29 @@
         in_specs=[pl.BlockSpec()] * 4,
         out_shape=[sd((block, 2 * hidden), BF)] + [half_rows, sd((2, block, hidden), BF)] * 2,
     )(keep_wide, swap(send_wide, "dp", 1), keep_narrow, swap(send_narrow, "dp", 1))
-    (produced,) = held(produced, first_done)
-    if each > 1:
-        produced = jnp.stack(split([produced[-k % WAYS] for k in range(WAYS)], False))[relative]
-    produced_home = lax.all_to_all(produced, "expert", 0, 0, tiled=True)
-
+    if each == 1:
+        ready, starts = [first_done], []
+        for ids in SETS[1:]:
+            sends, held_done = held([produced[k] for k in ids], ready)
+            for k, sent in zip(ids, sends):
+                produced[k] = shift(sent, "expert", -k)
+            ready = [produced[k] for k in ids]
+            starts.append(held_done)
+        produced_home = produced
+    else:
+        produced_home, starts, ready = exchange(split(produced, False), -1), [(), ()], []
+
+    x_came, y_came = swap(x_send, "dp", 2), swap(y_send, "dp", 4)
     pieces, start, done = [], 0, first_done
     for cut in CUTS:
         early = start == 0
         more = [outer_part, extra_part] if early else []
         columns = 3 * cut + width + 128
-        pack = [sd((half, block, columns), BF)] + [sd((half // 2, block, columns), BF)] * 2 if early else []
+        pack = [sd((half, block, columns), BF)] + [sd((half // SENDS, block, columns), BF)] * SENDS if early else []
         grads, done = kernel_call(
             partial(score_back_kernel, start // 128, cut // 128, early),
             D0_WEIGHT if early else D1_WEIGHT,
-            done,
+            done if early else [done, starts[1]],
             vmem=SCORE_VMEM,
             in_specs=[smem] + [vmem] * (8 + len(more)),
             out_specs=[vmem] * (3 + len(pack)),
@@ -1065,7 +1070,7 @@
     (tokens_grad, keep, send), done = kernel_call(
         partial(tokens_kernel, len(CUTS)),
         TOKENS_WEIGHT,
-        done,
+        [done, seen([x_came, y_came])],
         vmem=TOKENS_VMEM,
         in_specs=[smem] + [vmem] * (8 + 3 * len(CUTS)),
         out_specs=[vmem] * 3,
@@ -1076,25 +1081,25 @@
     (weight_sum, x_more, y_more), done = kernel_call(
         weight_second_kernel,
         MID_WEIGHT,
-        done,
+        seen([done, ready]),
         vmem=SUM4_VMEM,
         in_specs=[pl.BlockSpec()] * 5,
         out_shape=[sd((block, 2 * hidden), F32)] + [half_rows] * 2,
-    )(weight_own, x_keep, swap(x_send, "dp", 2), y_keep, swap(y_send, "dp", 4))
+    )(weight_own, x_keep, x_came, y_keep, y_came)
     late, done = first_sum(keep, [send], None, done, LATE_FIRST_WEIGHT)
     early, done = second_sum(early, place_vec, exact, done, SECOND_WEIGHT, True)
-    x_more, y_more = held([x_more, y_more], done)
+    (x_more, y_more), _ = held([x_more, y_more], done)
     late, done = second_sum(late, place_vec, None, done, LATE_SECOND_WEIGHT)
     (layer_output,), done = kernel_call(
         output_kernel,
         OUTPUT_WEIGHT,
         done,
         vmem=OUTPUT_VMEM,
-        in_specs=[smem] + [vmem] * 4,
+        in_specs=[vmem] * (3 + group),
         out_specs=[vmem],
         out_shape=[sd((rows, width), BF)],
         scratch_shapes=[pltpu.VMEM((spots, width), BF)],
-    )(place_vec, residual, weight, pos, produced_home)
+    )(residual, weight, pos, *produced_home)
     early, late = sent_on(early), sent_on(late)
     own = width // (dp_size * group)
     (query_grad, key_grad, value_grad, outer_grad, router_grad, norms, table_grad, sharp), done = kernel_call(

time: 308 us -> 299 us (0.971)
  local copies, waits for them, and re-layouts: 36 us -> 17.3 us
  waiting for transfers between devices: 45.1 us -> 53.9 us
  starting transfers between devices: 44.5 us -> 51.3 us
    ppermute x9 -> x12, waiting for transfers between devices: 34.5 us -> 53.8 us  [shift(): lax.ppermute(values, axis, [(i, (i + step) % size) for i in range(size)])]
    unnamed x163 -> x111, local copies, waits for them, and re-layouts: 32 us -> 13.2 us
    ppermute x9 -> x12, starting transfers between devices: 14.2 us -> 26.1 us  [shift(): lax.ppermute(values, axis, [(i, (i + step) % size) for i in range(size)])]
    all_to_all x1, waiting for transfers between devices: 6.29 us -> 0.01 us  [body(): upstream_there = lax.all_to_all(upstream_sent, 'expert', 0, 0, tiled=True)]
    all_to_all x1 -> x0, starting transfers between devices: 5.2 us -> none  [body(): produced_home = lax.all_to_all(produced, 'expert', 0, 0, tiled=True)]
    ppermute x15, waiting for transfers between devices: 4.31 us -> 0.04 us  [swap(): return lax.ppermute(values, axis, [(i, i ^ mask) for i in range(size)])]
    pallas_call x24 -> x26, Pallas kernels: 174 us -> 171 us  [made(): *outs, done = call(*args, *deps)]
  transfers between devices with their start and end apart: 27 -> 29, of which waited for: 8 -> 8; matrix products, arithmetic and copies ran while one was open for 2% -> 2% of each run, Pallas kernels for 52% -> 53%
where the time goes in v4:
time: 299 us; the launch traced here: 297 us
  Pallas kernels  171 us (57%)
  waiting for transfers between devices  53.9 us (18%)
  starting transfers between devices  51.3 us (17%)
  local copies, waits for them, and re-layouts  17.3 us (6%)
    pallas_call x26, Pallas kernels, made(): *outs, done = call(*args, *deps)  171 us
    ppermute x12, waiting for transfers between devices, shift(): lax.ppermute(values, axis, [(i, (i + step) % size) for i in range(size)])  53.8 us
    ppermute x12, starting transfers between devices, shift(): lax.ppermute(values, axis, [(i, (i + step) % size) for i in range(size)])  26.1 us
    ppermute x15, starting transfers between devices, swap(): return lax.ppermute(values, axis, [(i, i ^ mask) for i in range(size)])  14.9 us
    unnamed x111, local copies, waits for them, and re-layouts  13.2 us
    all_to_all x1, starting transfers between devices, body(): upstream_there = lax.all_to_all(upstream_sent, 'expert', 0, 0, tiled=True)  6.63 us
  transfers between devices with their start and end apart: 29, of which 8 were waited for; matrix products, arithmetic and copies ran while one was open for 2% of the time, Pallas kernels for 53%

profile of v4, /device:TPU:0, one launch (start us, length us, event | category | flops | bytes accessed | tf_op | source)
XLA Modules:
  0.0 296.9 jit_solution(4118329313637358607)
XLA Ops:
  1.3 1.4 copy-done.36
  3.4 5.0 %shard_map.289 = (s32[1,1024]{1,0:T(1,128)S(1)}, s32[1,1024]{1,0:T(1,128)S(1)}, bf16[4,400,768]{2,1,0:T(8,128)(2,1)}, f32[8,128]{1,0:T(8,128)}) custom-call(s32[1]{0:T(128)} %bitcast.2.refs_0_.refs_1_.refs_2_, s32[1,1024]{1,0:T(1,128)S(1)} %copy-done.40, s32[1,1024]{1,0:T(1,128)S(1)} %bitcast.21, bf16[1024,768]{1,0:T(8,128)(2,1)S(1)} %copy-done.36), custom_call_target="tpu_custom_call" | custom-call | flops 5368709120 | tf_op jit(solution)/shard_map/pallas_call | solution.py:86
  9.1 6.6 %all-to-all-start = ((bf16[4,400,768]{2,1,0:T(8,128)(2,1)}), bf16[4,400,768]{2,1,0:T(8,128)(2,1)S(1)}, u32[]{:S(2)}, u32[]{:S(2)}) async-start(bf16[4,400,768]{2,1,0:T(8,128)(2,1)} %get-tuple-element.135.refs_2_), calls=%async_computation | async-start | bytes 4915200 | tf_op jit(solution)/shard_map/all_to_all | solution.py:919
  20.0 30.7 %shard_map.290 = (bf16[768,1024]{1,0:T(8,128)(2,1)}, bf16[1024,768]{1,0:T(8,128)(2,1)}, bf16[1024,768]{1,0:T(8,128)(2,1)}, bf16[1024,768]{1,0:T(8,128)(2,1)}, bf...) custom-call(bf16[1024,768]{1,0:T(8,128)(2,1)} %refs_2_.1, ...), custom_call_target="tpu_custom_call" | custom-call | flops 21474836480 | tf_op jit(solution)/shard_map/pallas_call | solution.py:86
  50.7 2.1 collective-permute-start
  52.8 2.3 collective-permute-start.1
  55.8 1.1 copy-done.18
  56.8 12.5 %shard_map.291 = (bf16[384,768]{1,0:T(8,128)(2,1)}, bf16[400,768]{1,0:T(8,128)(2,1)S(1)}, bf16[384,3072]{1,0:T(8,128)(2,1)}, bf16[384,3072]{1,0:T(8,128)(2,1)}, f32[8,128]{1,0:T(8,128)S(1)}) custom-call(s32[1]{0:T(128)} %bitcast.4.refs_0_, s32[1]{0:T(128)} %bitcast.2.refs_0_.refs_1_.refs_2_, bf16[4,400,768]{2,1,0:T(8,128)(2,1)S(1)} %copy-done.10, ...), custom_call_target="tpu_custom_call" | custom-call | flops 10737418240 | tf_op jit(solution)/shard_map/pallas_call | solution.py:86
  69.3 4.8 %collective-permute-done.refs_3_.refs_1_.refs_5_ = bf16[400,768]{1,0:T(8,128)(2,1)S(1)} collective-permute-done((bf16[400,768]{1,0:T(8,128)(2,1)}, bf16[400,768]{1,0:T(8,128)(2,1)S(1)}, u32[]{:S(2)}, u32[]{:S(2)}) %collective-permute-start) | collective-permute-done | bytes 614432 | tf_op jit(solution)/shard_map/ppermute | solution.py:760
  74.1 19.3 %collective-permute-done.1.refs_4_.refs_2_.refs_6_ = bf16[400,768]{1,0:T(8,128)(2,1)S(1)} collective-permute-done((bf16[400,768]{1,0:T(8,128)(2,1)}, bf16[400,768]{1,0:T(8,128)(2,1)S(1)}, u32[]{:S(2)}, u32[]{:S(2)}) %collective-permute-start.1) | collective-permute-done | bytes 614432 | tf_op jit(solution)/shard_map/ppermute | solution.py:760
  94.3 5.1 %collective-permute-start.3 = (bf16[400,768]{1,0:T(8,128)(2,1)}, bf16[400,768]{1,0:T(8,128)(2,1)}, u32[]{:S(2)}, u32[]{:S(2)}) collective-permute-start(bf16[400,768]{1,0:T(8,128)(2,1)} %get-tuple-element.146), channel_id=1, source_target_pairs={{0,2},{1,3},{2,0},{3,1},{4,6},{5,7},{6,4},{7,5},{8,10},{9,11},{10,... | collective-permute-start | bytes 1843208 | tf_op jit(solution)/shard_map/ppermute | solution.py:760
  99.9 1.1 copy-done.7
  100.9 22.0 %shard_map.292 = (bf16[384,768]{1,0:T(8,128)(2,1)}, bf16[384,768]{1,0:T(8,128)(2,1)}, bf16[400,768]{1,0:T(8,128)(2,1)}, bf16[400,768]{1,0:T(8,128)(2,1)}, bf16[7...) custom-call(s32[4]{0:T(128)S(1)} %select_reduce_fusion.refs_0_, ...), custom_call_target="tpu_custom_call" | custom-call | flops 10737418240 | tf_op jit(solution)/shard_map/pallas_call | solution.py:86
  122.9 2.0 collective-permute-start.5
  124.9 1.8 collective-permute-done.3.refs_3_.refs_5_.refs_7_
  126.7 12.3 %shard_map.294 = (bf16[384,768]{1,0:T(8,128)(2,1)}, bf16[400,768]{1,0:T(8,128)(2,1)}, bf16[384,3072]{1,0:T(8,128)(2,1)}, bf16[384,3072]{1,0:T(8,128)(2,1)}, f32[8,128]{1,0:T(8,128)}) custom-call(s32[4]{0:T(128)S(1)} %select_reduce_fusion.refs_0_, s32[1]{0:T(128)} %bitcast.2.refs_0_.refs_1_.refs_2_, bf16[4,400,768]{2,1,0:T(8,128)(2,1)S(1)} %all-to-all-done.refs_2_.refs_3_, ...), custom_call_target="tpu_custom_call" | custom-call | flops 10737418240 | tf_op jit(solution)/shard_map/pallas_call | solution.py:86
  139.0 1.1 copy-done.8
  140.1 1.1 copy-done.19
  141.1 12.9 %shard_map.296 = (bf16[4,96,3072]{2,1,0:T(8,128)(2,1)S(1)}, bf16[4,96,3072]{2,1,0:T(8,128)(2,1)}, f32[8,128]{1,0:T(8,128)S(1)}) custom-call(s32[4]{0:T(128)S(1)} %select_reduce_fusion.refs_0_, s32[1]{0:T(128)} %bitcast.7.refs_1_.refs_0_, bf16[400,768]{1,0:T(8,128)(2,1)S(1)} %copy-done.19, bf16[400,768]{1,0:T(8,128)(2,1)S(1)} %collective-permute-done.refs_3_.refs_1_.refs_5_, ...), custom_call_target="tpu_custom_call" | custom-call | flops 5368709120 | tf_op jit(solution)/shard_map/pallas_call | solution.py:86
  154.2 13.4 %shard_map.297 = (bf16[4,768,384]{2,1,0:T(8,128)(2,1)S(1)}, bf16[4,768,384]{2,1,0:T(8,128)(2,1)}, f32[8,128]{1,0:T(8,128)}) custom-call(s32[4]{0:T(128)S(1)} %select_reduce_fusion.refs_0_, s32[1]{0:T(128)} %bitcast.7.refs_1_.refs_0_, s32[1]{0:T(128)} %bitcast.2.refs_0_.refs_1_.refs_2_, bf16[4,400,768]{2,1,0:T(8,128)(2,1)S(1)} %all-to-all-done.refs_2_.refs_3_, ...), custom_call_target="tpu_custom_call" | custom-call | flops 1073741824 | tf_op jit(solution)/shard_map/pallas_call | solution.py:86
  168.2 10.1 %collective-permute-done.4.refs_16_ = bf16[400,768]{1,0:T(8,128)(2,1)} collective-permute-done((bf16[400,768]{1,0:T(8,128)(2,1)}, bf16[400,768]{1,0:T(8,128)(2,1)}, u32[]{:S(2)}, u32[]{:S(2)}) %collective-permute-start.4) | collective-permute-done | bytes 614432 | tf_op jit(solution)/shard_map/ppermute | solution.py:760
  178.3 12.2 %shard_map.295 = (f32[1,1024]{1,0:T(1,128)S(1)}, f32[1024,768]{1,0:T(8,128)S(1)}, bf16[1024,768]{1,0:T(8,128)(2,1)S(1)}, f32[16,1024]{1,0:T(8,128)S(1)}, bf16[76...) custom-call(f32[1]{0:T(128)S(6)} %copy.47.refs_12_.refs_0_, ...), custom_call_target="tpu_custom_call" | custom-call | flops 536870912000 | tf_op jit(solution)/shard_map/pallas_call | solution.py:86
  190.6 3.8 %shard_map.298 = (bf16[96,6144]{1,0:T(8,128)(2,1)S(1)}, bf16[96,3072]{1,0:T(8,128)(2,1)S(1)}, bf16[2,96,3072]{2,1,0:T(8,128)(2,1)S(1)}, bf16[96,3072]{1,0:T(8,12...) custom-call(bf16[4,96,3072]{2,1,0:T(8,128)(2,1)S(1)} %get-tuple-element.157.refs_0_, ...), custom_call_target="tpu_custom_call" | custom-call | flops 1073741824 | tf_op jit(solution)/shard_map/pallas_call | solution.py:86
  195.0 5.7 %collective-permute-start.8 = (bf16[384,768]{1,0:T(8,128)(2,1)S(1)}, bf16[384,768]{1,0:T(8,128)(2,1)S(1)}, u32[]{:S(2)}, u32[]{:S(2)}) collective-permute-start(bf16[384,768]{1,0:T(8,128)(2,1)S(1)} %get-tuple-element.167), channel_id=1, source_target_pairs={{0,3},{1,0},{2,1},{3,2},{4,7},{5,4},{6,5},{7,6},{8,11},{9,8},{10,9... | collective-permute-start | bytes 1769480 | tf_op jit(solution)/shard_map/ppermute | solution.py:760
  200.7 3.1 %collective-permute-start.13 = (bf16[2,96,3072]{2,1,0:T(8,128)(2,1)S(1)}, bf16[2,96,3072]{2,1,0:T(8,128)(2,1)S(1)}, u32[]{:S(2)}, u32[]{:S(2)}) collective-permute-start(bf16[2,96,3072]{2,1,0:T(8,128)(2,1)S(1)} %get-tuple-element.194), channel_id=1, source_target_pairs={{0,8},{4,12},{8,0},{12,4},{16,24},{20,28},{24,16},{28,20},{1,9},{5... | collective-permute-start | bytes 3538952 | tf_op jit(solution)/shard_map/ppermute | solution.py:755
  204.7 15.5 %shard_map.301 = (bf16[1024,512]{1,0:T(8,128)(2,1)S(1)}, bf16[1024,512]{1,0:T(8,128)(2,1)S(1)}, bf16[1024,512]{1,0:T(8,128)(2,1)S(1)}, bf16[4,96,2432]{2,1,0:T(8...) custom-call(s32[1]{0:T(128)} %bitcast.7.refs_1_.refs_0_, ...), custom_call_target="tpu_custom_call" | custom-call | flops 107374184 | tf_op jit(solution)/shard_map/pallas_call | solution.py:86
  220.4 7.1 %collective-permute-done.8.refs_1_.refs_4_ = bf16[384,768]{1,0:T(8,128)(2,1)S(1)} collective-permute-done((bf16[384,768]{1,0:T(8,128)(2,1)S(1)}, bf16[384,768]{1,0:T(8,128)(2,1)S(1)}, u32[]{:S(2)}, u32[]{:S(2)}) %collective-permute-start.8) | collective-permute-done | bytes 589856 | tf_op jit(solution)/shard_map/ppermute | solution.py:760
  227.4 2.1 collective-permute-start.10
  229.5 6.0 %shard_map.302 = (bf16[1024,256]{1,0:T(8,128)(2,1)S(1)}, bf16[1024,256]{1,0:T(8,128)(2,1)S(1)}, bf16[1024,256]{1,0:T(8,128)(2,1)S(1)}, f32[8,128]{1,0:T(8,128)S(1)}) custom-call(s32[1]{0:T(128)} %bitcast.7.refs_1_.refs_0_, s32[2,1,512]{2,1,0:T(1,128)S(1)} %copy-done.26, bf16[1024,768]{1,0:T(8,128)(2,1)S(1)} %copy-done.1, bf16[1024,768]{1,0:T(8,128)(2,1)S(1)} %copy-done.2, ...), custom_call_target="tpu_custom_call" | custom-call | flops 107374184 | tf_op jit(solution)/shard_map/pallas_call | solution.py:86
  235.6 1.1 shard_map.303
  236.7 3.1 %collective-permute-start.19 = (bf16[96,2432]{1,0:T(8,128)(2,1)S(1)}, bf16[96,2432]{1,0:T(8,128)(2,1)S(1)}, u32[]{:S(2)}, u32[]{:S(2)}) collective-permute-start(bf16[96,2432]{1,0:T(8,128)(2,1)S(1)} %get-tuple-element.208), channel_id=1, source_target_pairs={{0,8},{4,12},{8,0},{12,4},{16,24},{20,28},{24,16},{28,20},{1,9},{5... | collective-permute-start | bytes 1400840 | tf_op jit(solution)/shard_map/ppermute | solution.py:755
  239.8 1.5 collective-permute-start.21
  241.4 10.2 %shard_map.305 = (bf16[1024,768]{1,0:T(8,128)(2,1)}, bf16[4,96,896]{2,1,0:T(8,128)(2,1)S(1)}, bf16[4,96,896]{2,1,0:T(8,128)(2,1)S(1)}, f32[8,128]{1,0:T(8,128)S(1)}) custom-call(s32[1]{0:T(128)} %bitcast.7.refs_1_.refs_0_, bf16[768,1024]{1,0:T(8,128)(2,1)S(1)} %copy-done, bf16[1024,768]{1,0:T(8,128)(2,1)S(1)} %copy-done.13, ...), custom_call_target="tpu_custom_call" | custom-call | flops 107374184 | tf_op jit(solution)/shard_map/pallas_call | solution.py:86
  251.6 5.2 %collective-permute-done.10.refs_1_.refs_5_ = bf16[384,768]{1,0:T(8,128)(2,1)S(1)} collective-permute-done((bf16[384,768]{1,0:T(8,128)(2,1)S(1)}, bf16[384,768]{1,0:T(8,128)(2,1)S(1)}, u32[]{:S(2)}, u32[]{:S(2)}) %collective-permute-start.10) | collective-permute-done | bytes 589856 | tf_op jit(solution)/shard_map/ppermute | solution.py:760
  256.8 1.4 shard_map.307
  258.2 1.4 copy-done.11
  260.4 3.1 %collective-permute-start.16 = (bf16[96,896]{1,0:T(8,128)(2,1)S(1)}, bf16[96,896]{1,0:T(8,128)(2,1)S(1)}, u32[]{:S(2)}, u32[]{:S(2)}) collective-permute-start(bf16[96,896]{1,0:T(8,128)(2,1)S(1)} %get-tuple-element.204), channel_id=1, source_target_pairs={{0,8},{4,12},{8,0},{12,4},{16,24},{20,28},{24,16},{28,20},{1,9},{5... | collective-permute-start | bytes 516104 | tf_op jit(solution)/shard_map/ppermute | solution.py:755
  263.5 1.5 collective-permute-start.18
  267.0 3.7 %all-to-all-start.1 = ((bf16[4,32,2432]{2,1,0:T(8,128)(2,1)}), bf16[4,32,2432]{2,1,0:T(8,128)(2,1)S(1)}, u32[]{:S(2)}, u32[]{:S(2)}) async-start(bf16[4,32,2432]{2,1,0:T(8,128)(2,1)} %copy-done.17), calls=%async_computation.1 | async-start | bytes 1245184 | tf_op jit(solution)/shard_map/all_to_all | solution.py:822
  271.8 1.5 collective-permute-start.26
  274.2 1.2 shard_map.310
  275.4 2.1 collective-permute-start.22
  277.5 2.4 collective-permute-start.23
  279.9 1.5 collective-permute-start.24
  281.3 4.2 %shard_map.311 = (bf16[1024,768]{1,0:T(8,128)(2,1)}, f32[8,128]{1,0:T(8,128)S(1)}) custom-call(f32[1024,768]{1,0:T(8,128)S(1)} %copy-done.5, f32[1,1024]{1,0:T(1,128)S(1)} %get-tuple-element.150.refs_1_, s32[1,1024]{1,0:T(1,128)S(1)} %copy-done.30, bf16[384,768]{1,0:T(8,128)(2,1)S(1)} %copy-done.21, ...), custom_call_target="tpu_custom_call" | custom-call | flops 107374184 | tf_op jit(solution)/shard_map/pallas_call | solution.py:86
  285.5 1.4 collective-permute-done.22.refs_3_
  286.9 4.2 %collective-permute-done.23.refs_4_ = bf16[32,896]{1,0:T(8,128)(2,1)S(1)} collective-permute-done((bf16[32,896]{1,0:T(8,128)(2,1)S(1)}, bf16[32,896]{1,0:T(8,128)(2,1)S(1)}, u32[]{:S(2)}, u32[]{:S(2)}) %collective-permute-start.23) | collective-permute-done | bytes 57376 | tf_op jit(solution)/shard_map/ppermute | solution.py:760
  293.2 3.4 %shard_map.314 = (f32[96,3072]{1,0:T(8,128)}, f32[384,768]{1,0:T(8,128)}, f32[8,128]{1,0:T(8,128)}) custom-call(f32[96,6144]{1,0:T(8,128)S(1)} %copy-done.12, bf16[96,3072]{1,0:T(8,128)(2,1)} %collective-permute-done.25.refs_1_, bf16[96,3072]{1,0:T(8,128)(2,1)} %collective-permute-done.26.refs_2_, f32[8,128]{1,0:T(8,128)S(1)} %get-tuple-element.236.refs_3_), custom_call_target="tpu_custom_call" | custom-call | flops 107374184 | tf_op jit(solution)/shard_map/pallas_call | solution.py:86
  (164 shorter events, 16.7 us)
Async XLA Ops:
  9.1 90.3 %all-to-all-start = ((bf16[4,400,768]{2,1,0:T(8,128)(2,1)}), bf16[4,400,768]{2,1,0:T(8,128)(2,1)S(1)}, u32[]{:S(2)}, u32[]{:S(2)}) async-start(bf16[4,400,768]{2,1,0:T(8,128)(2,1)} %get-tuple-element.135.refs_2_), calls=%async_computation | async-start | bytes 4915200 | tf_op jit(solution)/shard_map/all_to_all | solution.py:919
  20.0 35.1 %copy-start.32 = (s32[1024,1]{0,1:T(1,128)S(1)}, s32[1024,1]{0,1:T(1,128)}, u32[]{:S(2)}) copy-start(s32[1024,1]{0,1:T(1,128)} %param.36) | copy-start | bytes 12292
  20.0 35.8 %copy-start.10 = (bf16[4,400,768]{2,1,0:T(8,128)(2,1)S(1)}, bf16[4,400,768]{2,1,0:T(8,128)(2,1)}, u32[]{:S(2)}) copy-start(bf16[4,400,768]{2,1,0:T(8,128)(2,1)} %get-tuple-element.135.refs_2_) | copy-start | bytes 7372804
  50.7 23.4 %collective-permute-start = (bf16[400,768]{1,0:T(8,128)(2,1)}, bf16[400,768]{1,0:T(8,128)(2,1)S(1)}, u32[]{:S(2)}, u32[]{:S(2)}) collective-permute-start(bf16[400,768]{1,0:T(8,128)(2,1)} %get-tuple-element.141), channel_id=1, source_target_pairs={{0,1},{1,2},{2,3},{3,0},{4,5},{5,6},{6,7},{7,4},{8,9},{9,10},{10,1... | collective-permute-start | bytes 1843208 | tf_op jit(solution)/shard_map/ppermute | solution.py:760
  52.8 40.6 %collective-permute-start.1 = (bf16[400,768]{1,0:T(8,128)(2,1)}, bf16[400,768]{1,0:T(8,128)(2,1)S(1)}, u32[]{:S(2)}, u32[]{:S(2)}) collective-permute-start(bf16[400,768]{1,0:T(8,128)(2,1)} %get-tuple-element.142), channel_id=1, source_target_pairs={{0,3},{1,0},{2,1},{3,2},{4,7},{5,4},{6,5},{7,6},{8,11},{9,8},{10,9... | collective-permute-start | bytes 1843208 | tf_op jit(solution)/shard_map/ppermute | solution.py:760
  69.3 24.8 %copy-start.45 = (bf16[400,768]{1,0:T(8,128)(2,1)}, bf16[400,768]{1,0:T(8,128)(2,1)S(1)}, u32[]{:S(2)}) copy-start(bf16[400,768]{1,0:T(8,128)(2,1)S(1)} %get-tuple-element.140.refs_14_) | copy-start | bytes 1843204
  94.3 32.4 %collective-permute-start.3 = (bf16[400,768]{1,0:T(8,128)(2,1)}, bf16[400,768]{1,0:T(8,128)(2,1)}, u32[]{:S(2)}, u32[]{:S(2)}) collective-permute-start(bf16[400,768]{1,0:T(8,128)(2,1)} %get-tuple-element.146), channel_id=1, source_target_pairs={{0,2},{1,3},{2,0},{3,1},{4,6},{5,7},{6,4},{7,5},{8,10},{9,11},{10,... | collective-permute-start | bytes 1843208 | tf_op jit(solution)/shard_map/ppermute | solution.py:760
  122.9 31.2 %collective-permute-start.2 = (bf16[400,768]{1,0:T(8,128)(2,1)}, bf16[400,768]{1,0:T(8,128)(2,1)}, u32[]{:S(2)}, u32[]{:S(2)}) collective-permute-start(bf16[400,768]{1,0:T(8,128)(2,1)} %get-tuple-element.144), channel_id=1, source_target_pairs={{0,3},{1,0},{2,1},{3,2},{4,7},{5,4},{6,5},{7,6},{8,11},{9,8},{10,9... | collective-permute-start | bytes 1843208 | tf_op jit(solution)/shard_map/ppermute | solution.py:760
  122.9 31.2 %collective-permute-start.5 = (bf16[400,768]{1,0:T(8,128)(2,1)}, bf16[400,768]{1,0:T(8,128)(2,1)}, u32[]{:S(2)}, u32[]{:S(2)}) collective-permute-start(bf16[400,768]{1,0:T(8,128)(2,1)} %get-tuple-element.149), channel_id=1, source_target_pairs={{0,1},{1,2},{2,3},{3,0},{4,5},{5,6},{6,7},{7,4},{8,9},{9,10},{10,1... | collective-permute-start | bytes 1843208 | tf_op jit(solution)/shard_map/ppermute | solution.py:760
  139.0 39.2 %collective-permute-start.4 = (bf16[400,768]{1,0:T(8,128)(2,1)}, bf16[400,768]{1,0:T(8,128)(2,1)}, u32[]{:S(2)}, u32[]{:S(2)}) collective-permute-start(bf16[400,768]{1,0:T(8,128)(2,1)} %get-tuple-element.148), channel_id=1, source_target_pairs={{0,2},{1,3},{2,0},{3,1},{4,6},{5,7},{6,4},{7,5},{8,10},{9,11},{10,... | collective-permute-start | bytes 1843208 | tf_op jit(solution)/shard_map/ppermute | solution.py:760
  154.1 36.4 %collective-permute-start.6 = (bf16[4,96,3072]{2,1,0:T(8,128)(2,1)}, bf16[4,96,3072]{2,1,0:T(8,128)(2,1)}, u32[]{:S(2)}, u32[]{:S(2)}) collective-permute-start(bf16[4,96,3072]{2,1,0:T(8,128)(2,1)} %get-tuple-element.158), channel_id=1, source_target_pairs={{0,4},{4,0},{8,12},{12,8},{16,20},{20,16},{24,28},{28,24},{1,5},{5... | collective-permute-start | bytes 7077896 | tf_op jit(solution)/shard_map/ppermute | solution.py:755
  154.1 24.1 %copy-start.4 = (f32[1024,768]{1,0:T(8,128)S(1)}, f32[1024,768]{1,0:T(8,128)}, u32[]{:S(2)}) copy-start(f32[1024,768]{1,0:T(8,128)} %get-tuple-element.134.refs_5_.refs_0_) | copy-start | bytes 9437188
  154.1 24.1 %copy-start.30 = (s32[1,1024]{1,0:T(1,128)S(1)}, s32[1,1024]{1,0:T(1,128)}, u32[]{:S(2)}) copy-start(s32[1,1024]{1,0:T(1,128)} %copy-done.29) | copy-start | bytes 12292
  154.1 24.1 %copy-start.33 = (f32[8,16]{1,0:T(8,128)S(1)}, f32[8,16]{1,0:T(8,128)}, u32[]{:S(2)}) copy-start(f32[8,16]{1,0:T(8,128)} %scatter.4.refs_11_.refs_9_) | copy-start | bytes 1540
  154.2 24.1 %copy-start.34 = (f32[1,768]{1,0:T(1,128)S(1)}, f32[1,768]{1,0:T(1,128)}, u32[]{:S(2)}) copy-start(f32[1,768]{1,0:T(1,128)} %reshape.137.refs_8_.refs_11_) | copy-start | bytes 9220
  154.2 24.1 %copy-start.35 = (f32[1,768]{1,0:T(1,128)S(1)}, f32[1,768]{1,0:T(1,128)}, u32[]{:S(2)}) copy-start(f32[1,768]{1,0:T(1,128)} %reshape.138.refs_9_.refs_12_) | copy-start | bytes 9220
  154.2 24.1 %copy-start.37 = (bf16[1024,768]{1,0:T(8,128)(2,1)S(1)}, bf16[1024,768]{1,0:T(8,128)(2,1)}, u32[]{:S(2)}) copy-start(bf16[1024,768]{1,0:T(8,128)(2,1)} %refs_6_.4) | copy-start | bytes 4718596
  154.2 24.1 %copy-start.38 = (bf16[768,768]{1,0:T(8,128)(2,1)S(1)}, bf16[768,768]{1,0:T(8,128)(2,1)}, u32[]{:S(2)}) copy-start(bf16[768,768]{1,0:T(8,128)(2,1)} %refs_13_.1) | copy-start | bytes 3538948
  154.2 24.1 %copy-start.39 = (f32[768,16]{0,1:T(8,128)S(1)}, f32[768,16]{0,1:T(8,128)}, u32[]{:S(2)}) copy-start(f32[768,16]{0,1:T(8,128)} %param.30) | copy-start | bytes 147460
  154.2 24.1 %copy-start.46 = (bf16[400,768]{1,0:T(8,128)(2,1)S(1)}, bf16[400,768]{1,0:T(8,128)(2,1)}, u32[]{:S(2)}) copy-start(bf16[400,768]{1,0:T(8,128)(2,1)} %copy-done.45) | copy-start | bytes 1843204
  154.2 24.1 %copy-start.47 = (bf16[1024,768]{1,0:T(8,128)(2,1)S(1)}, bf16[1024,768]{1,0:T(8,128)(2,1)}, u32[]{:S(2)}) copy-start(bf16[1024,768]{1,0:T(8,128)(2,1)} %get-tuple-element.137.refs_7_) | copy-start | bytes 4718596
  154.2 24.1 %copy-start.48 = (f32[16,1024]{1,0:T(8,128)S(1)}, f32[16,1024]{1,0:T(8,128)}, u32[]{:S(2)}) copy-start(f32[16,1024]{1,0:T(8,128)} %get-tuple-element.138.refs_8_) | copy-start | bytes 196612
  167.6 22.9 %collective-permute-start.7 = (bf16[4,768,384]{2,1,0:T(8,128)(2,1)}, bf16[4,768,384]{2,1,0:T(8,128)(2,1)}, u32[]{:S(2)}, u32[]{:S(2)}) collective-permute-start(bf16[4,768,384]{2,1,0:T(8,128)(2,1)} %get-tuple-element.164), channel_id=1, source_target_pairs={{0,4},{4,0},{8,12},{12,8},{16,20},{20,16},{24,28},{28,24},{1,5},{5... | collective-permute-start | bytes 7077896 | tf_op jit(solution)/shard_map/ppermute | solution.py:755
  190.5 14.1 %copy-start = (bf16[768,1024]{1,0:T(8,128)(2,1)S(1)}, bf16[768,1024]{1,0:T(8,128)(2,1)}, u32[]{:S(2)}) copy-start(bf16[768,1024]{1,0:T(8,128)(2,1)} %get-tuple-element.171.refs_8_.refs_1_) | copy-start | bytes 4718596
  190.6 14.1 %copy-start.1 = (bf16[1024,768]{1,0:T(8,128)(2,1)S(1)}, bf16[1024,768]{1,0:T(8,128)(2,1)}, u32[]{:S(2)}) copy-start(bf16[1024,768]{1,0:T(8,128)(2,1)} %get-tuple-element.173.refs_2_) | copy-start | bytes 4718596
  190.6 14.1 %copy-start.2 = (bf16[1024,768]{1,0:T(8,128)(2,1)S(1)}, bf16[1024,768]{1,0:T(8,128)(2,1)}, u32[]{:S(2)}) copy-start(bf16[1024,768]{1,0:T(8,128)(2,1)} %get-tuple-element.174.refs_3_) | copy-start | bytes 4718596
  190.6 14.1 %copy-start.3 = (bf16[1024,768]{1,0:T(8,128)(2,1)S(1)}, bf16[1024,768]{1,0:T(8,128)(2,1)}, u32[]{:S(2)}) copy-start(bf16[1024,768]{1,0:T(8,128)(2,1)} %get-tuple-element.175.refs_4_) | copy-start | bytes 4718596
  195.0 32.4 %collective-permute-start.8 = (bf16[384,768]{1,0:T(8,128)(2,1)S(1)}, bf16[384,768]{1,0:T(8,128)(2,1)S(1)}, u32[]{:S(2)}, u32[]{:S(2)}) collective-permute-start(bf16[384,768]{1,0:T(8,128)(2,1)S(1)} %get-tuple-element.167), channel_id=1, source_target_pairs={{0,3},{1,0},{2,1},{3,2},{4,7},{5,4},{6,5},{7,6},{8,11},{9,8},{10,9... | collective-permute-start | bytes 1769480 | tf_op jit(solution)/shard_map/ppermute | solution.py:760
  200.7 39.1 %collective-permute-start.13 = (bf16[2,96,3072]{2,1,0:T(8,128)(2,1)S(1)}, bf16[2,96,3072]{2,1,0:T(8,128)(2,1)S(1)}, u32[]{:S(2)}, u32[]{:S(2)}) collective-permute-start(bf16[2,96,3072]{2,1,0:T(8,128)(2,1)S(1)} %get-tuple-element.194), channel_id=1, source_target_pairs={{0,8},{4,12},{8,0},{12,4},{16,24},{20,28},{24,16},{28,20},{1,9},{5... | collective-permute-start | bytes 3538952 | tf_op jit(solution)/shard_map/ppermute | solution.py:755
  203.7 37.6 %collective-permute-start.14 = (bf16[2,96,3072]{2,1,0:T(8,128)(2,1)S(1)}, bf16[2,96,3072]{2,1,0:T(8,128)(2,1)S(1)}, u32[]{:S(2)}, u32[]{:S(2)}) collective-permute-start(bf16[2,96,3072]{2,1,0:T(8,128)(2,1)S(1)} %get-tuple-element.195), channel_id=1, source_target_pairs={{0,16},{4,20},{8,24},{12,28},{16,0},{20,4},{24,8},{28,12},{1,17},{... | collective-permute-start | bytes 3538952 | tf_op jit(solution)/shard_map/ppermute | solution.py:755
  203.7 23.7 %collective-permute-start.9 = (bf16[384,768]{1,0:T(8,128)(2,1)S(1)}, bf16[384,768]{1,0:T(8,128)(2,1)S(1)}, u32[]{:S(2)}, u32[]{:S(2)}) collective-permute-start(bf16[384,768]{1,0:T(8,128)(2,1)S(1)} %get-tuple-element.169), channel_id=1, source_target_pairs={{0,1},{1,2},{2,3},{3,0},{4,5},{5,6},{6,7},{7,4},{8,9},{9,10},{10,1... | collective-permute-start | bytes 1769480 | tf_op jit(solution)/shard_map/ppermute | solution.py:760
  204.7 22.7 %copy-start.22 = (bf16[384,768]{1,0:T(8,128)(2,1)S(1)}, bf16[384,768]{1,0:T(8,128)(2,1)}, u32[]{:S(2)}) copy-start(bf16[384,768]{1,0:T(8,128)(2,1)} %get-tuple-element.168.refs_0_) | copy-start | bytes 1769476
  220.3 15.3 %collective-permute-start.11 = (bf16[2,96,2432]{2,1,0:T(8,128)(2,1)S(1)}, bf16[2,96,2432]{2,1,0:T(8,128)(2,1)S(1)}, u32[]{:S(2)}, u32[]{:S(2)}) collective-permute-start(bf16[2,96,2432]{2,1,0:T(8,128)(2,1)S(1)} %get-tuple-element.190), channel_id=1, source_target_pairs={{0,4},{4,0},{8,12},{12,8},{16,20},{20,16},{24,28},{28,24},{1,5},{5... | collective-permute-start | bytes 2801672 | tf_op jit(solution)/shard_map/ppermute | solution.py:755
  227.4 8.2 %collective-permute-start.12 = (bf16[2,96,2432]{2,1,0:T(8,128)(2,1)S(1)}, bf16[2,96,2432]{2,1,0:T(8,128)(2,1)S(1)}, u32[]{:S(2)}, u32[]{:S(2)}) collective-permute-start(bf16[2,96,2432]{2,1,0:T(8,128)(2,1)S(1)} %get-tuple-element.191), channel_id=1, source_target_pairs={{0,4},{4,0},{8,12},{12,8},{16,20},{20,16},{24,28},{28,24},{1,5},{5... | collective-permute-start | bytes 2801672 | tf_op jit(solution)/shard_map/ppermute | solution.py:755
  227.4 29.3 %collective-permute-start.10 = (bf16[384,768]{1,0:T(8,128)(2,1)S(1)}, bf16[384,768]{1,0:T(8,128)(2,1)S(1)}, u32[]{:S(2)}, u32[]{:S(2)}) collective-permute-start(bf16[384,768]{1,0:T(8,128)(2,1)S(1)} %get-tuple-element.170), channel_id=1, source_target_pairs={{0,2},{1,3},{2,0},{3,1},{4,6},{5,7},{6,4},{7,5},{8,10},{9,11},{10,... | collective-permute-start | bytes 1769480 | tf_op jit(solution)/shard_map/ppermute | solution.py:760
  236.7 26.8 %collective-permute-start.19 = (bf16[96,2432]{1,0:T(8,128)(2,1)S(1)}, bf16[96,2432]{1,0:T(8,128)(2,1)S(1)}, u32[]{:S(2)}, u32[]{:S(2)}) collective-permute-start(bf16[96,2432]{1,0:T(8,128)(2,1)S(1)} %get-tuple-element.208), channel_id=1, source_target_pairs={{0,8},{4,12},{8,0},{12,4},{16,24},{20,28},{24,16},{28,20},{1,9},{5... | collective-permute-start | bytes 1400840 | tf_op jit(solution)/shard_map/ppermute | solution.py:755
  239.8 25.2 %collective-permute-start.20 = (bf16[96,2432]{1,0:T(8,128)(2,1)S(1)}, bf16[96,2432]{1,0:T(8,128)(2,1)S(1)}, u32[]{:S(2)}, u32[]{:S(2)}) collective-permute-start(bf16[96,2432]{1,0:T(8,128)(2,1)S(1)} %get-tuple-element.209), channel_id=1, source_target_pairs={{0,16},{4,20},{8,24},{12,28},{16,0},{20,4},{24,8},{28,12},{1,17},{... | collective-permute-start | bytes 1400840 | tf_op jit(solution)/shard_map/ppermute | solution.py:755
  239.8 25.1 %collective-permute-start.21 = (bf16[96,2432]{1,0:T(8,128)(2,1)S(1)}, bf16[96,2432]{1,0:T(8,128)(2,1)S(1)}, u32[]{:S(2)}, u32[]{:S(2)}) collective-permute-start(bf16[96,2432]{1,0:T(8,128)(2,1)S(1)} %get-tuple-element.210), channel_id=1, source_target_pairs={{0,24},{4,28},{8,16},{12,20},{16,8},{20,12},{24,0},{28,4},{1,25},{... | collective-permute-start | bytes 1400840 | tf_op jit(solution)/shard_map/ppermute | solution.py:755
  251.6 8.0 %collective-permute-start.15 = (bf16[4,96,896]{2,1,0:T(8,128)(2,1)S(1)}, bf16[4,96,896]{2,1,0:T(8,128)(2,1)S(1)}, u32[]{:S(2)}, u32[]{:S(2)}) collective-permute-start(bf16[4,96,896]{2,1,0:T(8,128)(2,1)S(1)} %get-tuple-element.197), channel_id=1, source_target_pairs={{0,4},{4,0},{8,12},{12,8},{16,20},{20,16},{24,28},{28,24},{1,5},{5... | collective-permute-start | bytes 2064392 | tf_op jit(solution)/shard_map/ppermute | solution.py:755
  260.4 12.8 %collective-permute-start.16 = (bf16[96,896]{1,0:T(8,128)(2,1)S(1)}, bf16[96,896]{1,0:T(8,128)(2,1)S(1)}, u32[]{:S(2)}, u32[]{:S(2)}) collective-permute-start(bf16[96,896]{1,0:T(8,128)(2,1)S(1)} %get-tuple-element.204), channel_id=1, source_target_pairs={{0,8},{4,12},{8,0},{12,4},{16,24},{20,28},{24,16},{28,20},{1,9},{5... | collective-permute-start | bytes 516104 | tf_op jit(solution)/shard_map/ppermute | solution.py:755
  263.5 9.8 %collective-permute-start.17 = (bf16[96,896]{1,0:T(8,128)(2,1)S(1)}, bf16[96,896]{1,0:T(8,128)(2,1)S(1)}, u32[]{:S(2)}, u32[]{:S(2)}) collective-permute-start(bf16[96,896]{1,0:T(8,128)(2,1)S(1)} %get-tuple-element.205), channel_id=1, source_target_pairs={{0,16},{4,20},{8,24},{12,28},{16,0},{20,4},{24,8},{28,12},{1,17},{... | collective-permute-start | bytes 516104 | tf_op jit(solution)/shard_map/ppermute | solution.py:755
  263.5 9.8 %collective-permute-start.18 = (bf16[96,896]{1,0:T(8,128)(2,1)S(1)}, bf16[96,896]{1,0:T(8,128)(2,1)}, u32[]{:S(2)}, u32[]{:S(2)}) collective-permute-start(bf16[96,896]{1,0:T(8,128)(2,1)S(1)} %get-tuple-element.206), channel_id=1, source_target_pairs={{0,24},{4,28},{8,16},{12,20},{16,8},{20,12},{24,0},{28,4},{1,25},{... | collective-permute-start | bytes 516104 | tf_op jit(solution)/shard_map/ppermute | solution.py:755
  267.0 24.2 %all-to-all-start.1 = ((bf16[4,32,2432]{2,1,0:T(8,128)(2,1)}), bf16[4,32,2432]{2,1,0:T(8,128)(2,1)S(1)}, u32[]{:S(2)}, u32[]{:S(2)}) async-start(bf16[4,32,2432]{2,1,0:T(8,128)(2,1)} %copy-done.17), calls=%async_computation.1 | async-start | bytes 1245184 | tf_op jit(solution)/shard_map/all_to_all | solution.py:822
  271.3 22.0 %collective-permute-start.25 = (bf16[96,3072]{1,0:T(8,128)(2,1)}, bf16[96,3072]{1,0:T(8,128)(2,1)}, u32[]{:S(2)}, u32[]{:S(2)}) collective-permute-start(bf16[96,3072]{1,0:T(8,128)(2,1)} %get-tuple-element.234), channel_id=1, source_target_pairs={{0,16},{4,20},{8,24},{12,28},{16,0},{20,4},{24,8},{28,12},{1,17},{... | collective-permute-start | bytes 1769480 | tf_op jit(solution)/shard_map/ppermute | solution.py:755
  271.8 21.4 %collective-permute-start.26 = (bf16[96,3072]{1,0:T(8,128)(2,1)}, bf16[96,3072]{1,0:T(8,128)(2,1)}, u32[]{:S(2)}, u32[]{:S(2)}) collective-permute-start(bf16[96,3072]{1,0:T(8,128)(2,1)} %get-tuple-element.235), channel_id=1, source_target_pairs={{0,8},{4,12},{8,0},{12,4},{16,24},{20,28},{24,16},{28,20},{1,9},{5... | collective-permute-start | bytes 1769480 | tf_op jit(solution)/shard_map/ppermute | solution.py:755
  275.4 11.5 %collective-permute-start.22 = (bf16[32,896]{1,0:T(8,128)(2,1)S(1)}, bf16[32,896]{1,0:T(8,128)(2,1)S(1)}, u32[]{:S(2)}, u32[]{:S(2)}) collective-permute-start(bf16[32,896]{1,0:T(8,128)(2,1)S(1)} %get-tuple-element.219), channel_id=1, source_target_pairs={{0,1},{1,2},{2,3},{3,0},{4,5},{5,6},{6,7},{7,4},{8,9},{9,10},{10,1... | collective-permute-start | bytes 172040 | tf_op jit(solution)/shard_map/ppermute | solution.py:760
  277.5 13.7 %collective-permute-start.23 = (bf16[32,896]{1,0:T(8,128)(2,1)S(1)}, bf16[32,896]{1,0:T(8,128)(2,1)S(1)}, u32[]{:S(2)}, u32[]{:S(2)}) collective-permute-start(bf16[32,896]{1,0:T(8,128)(2,1)S(1)} %get-tuple-element.220), channel_id=1, source_target_pairs={{0,2},{1,3},{2,0},{3,1},{4,6},{5,7},{6,4},{7,5},{8,10},{9,11},{10,... | collective-permute-start | bytes 172040 | tf_op jit(solution)/shard_map/ppermute | solution.py:760
  279.9 11.3 %collective-permute-start.24 = (bf16[32,896]{1,0:T(8,128)(2,1)S(1)}, bf16[32,896]{1,0:T(8,128)(2,1)S(1)}, u32[]{:S(2)}, u32[]{:S(2)}) collective-permute-start(bf16[32,896]{1,0:T(8,128)(2,1)S(1)} %get-tuple-element.221), channel_id=1, source_target_pairs={{0,3},{1,0},{2,1},{3,2},{4,7},{5,4},{6,5},{7,6},{8,11},{9,8},{10,9... | collective-permute-start | bytes 172040 | tf_op jit(solution)/shard_map/ppermute | solution.py:760
  (36 other events, 185.4 us)

commit v5 on v4

--- a/solution.py
+++ b/solution.py
@@ -1100,6 +1100,14 @@
         out_shape=[sd((rows, width), BF)],
         scratch_shapes=[pltpu.VMEM((spots, width), BF)],
     )(residual, weight, pos, *produced_home)
+    (hidden_grad, return_grad), done = kernel_call(
+        weight_last_kernel,
+        LAST_WEIGHT,
+        done,
+        vmem=SUM5_VMEM,
+        in_specs=[pl.BlockSpec()] * 3,
+        out_shape=[sd((block, hidden), F32), sd((hidden // dp_size, width), F32)],
+    )(weight_sum, swap(x_more, "dp", 4), swap(y_more, "dp", 2))
     early, late = sent_on(early), sent_on(late)
     own = width // (dp_size * group)
     (query_grad, key_grad, value_grad, outer_grad, router_grad, norms, table_grad, sharp), done = kernel_call(
@@ -1111,14 +1119,6 @@
         out_shape=[sd((own, width), F32)] * 4
         + [sd((own, route), F32), sd((4, own), F32), sd((group, route), F32), sd((1, 1), F32)],
     )(*early, *late)
-    (hidden_grad, return_grad), done = kernel_call(
-        weight_last_kernel,
-        LAST_WEIGHT,
-        done,
-        vmem=SUM5_VMEM,
-        in_specs=[pl.BlockSpec()] * 3,
-        out_shape=[sd((block, hidden), F32), sd((hidden // dp_size, width), F32)],
-    )(weight_sum, swap(x_more, "dp", 4), swap(y_more, "dp", 2))
     if group > 8:
         tiny = small_sum(tiny)
         table_grad, sharp = tiny[:group, :route], tiny[experts_padded, :1]

time: 299 us -> 295 us (0.987)
  Pallas kernels: 171 us -> 163 us
  starting transfers between devices: 51.3 us -> 57.3 us
  waiting for transfers between devices: 53.9 us -> 50.6 us
    pallas_call x26, Pallas kernels: 171 us -> 163 us  [made(): *outs, done = call(*args, *deps)]
    ppermute x12, starting transfers between devices: 26.1 us -> 32.1 us  [shift(): lax.ppermute(values, axis, [(i, (i + step) % size) for i in range(size)])]
    ppermute x12, waiting for transfers between devices: 53.8 us -> 50.2 us  [shift(): lax.ppermute(values, axis, [(i, (i + step) % size) for i in range(size)])]
    unnamed x111 -> x109, local copies, waits for them, and re-layouts: 13.2 us -> 12.4 us
where the time goes in v5:
time: 295 us; the launch traced here: 291 us
  Pallas kernels  163 us (55%)
  starting transfers between devices  57.3 us (19%)
  waiting for transfers between devices  50.6 us (17%)
  local copies, waits for them, and re-layouts  16.5 us (6%)
    pallas_call x26, Pallas kernels, made(): *outs, done = call(*args, *deps)  163 us
    ppermute x12, waiting for transfers between devices, shift(): lax.ppermute(values, axis, [(i, (i + step) % size) for i in range(size)])  50.2 us
    ppermute x12, starting transfers between devices, shift(): lax.ppermute(values, axis, [(i, (i + step) % size) for i in range(size)])  32.1 us
    ppermute x15, starting transfers between devices, swap(): return lax.ppermute(values, axis, [(i, i ^ mask) for i in range(size)])  14.2 us
    unnamed x109, local copies, waits for them, and re-layouts  12.4 us
    all_to_all x1, starting transfers between devices, body(): upstream_there = lax.all_to_all(upstream_sent, 'expert', 0, 0, tiled=True)  6.63 us
  transfers between devices with their start and end apart: 29, of which 8 were waited for; matrix products, arithmetic and copies ran while one was open for 2% of the time, Pallas kernels for 53%

profile of v5, /device:TPU:0, one launch (start us, length us, event | category | flops | bytes accessed | tf_op | source)
XLA Modules:
  0.0 291.1 jit_solution(5408069498981395507)
XLA Ops:
  1.3 1.4 copy-done.35
  3.4 5.0 %shard_map.289 = (s32[1,1024]{1,0:T(1,128)S(1)}, s32[1,1024]{1,0:T(1,128)S(1)}, bf16[4,400,768]{2,1,0:T(8,128)(2,1)}, f32[8,128]{1,0:T(8,128)}) custom-call(s32[1]{0:T(128)} %bitcast.2.refs_0_.refs_1_.refs_2_, s32[1,1024]{1,0:T(1,128)S(1)} %copy-done.39, s32[1,1024]{1,0:T(1,128)S(1)} %bitcast.21, bf16[1024,768]{1,0:T(8,128)(2,1)S(1)} %copy-done.35), custom_call_target="tpu_custom_call" | custom-call | flops 5368709120 | tf_op jit(solution)/shard_map/pallas_call | solution.py:86
  9.1 6.6 %all-to-all-start = ((bf16[4,400,768]{2,1,0:T(8,128)(2,1)}), bf16[4,400,768]{2,1,0:T(8,128)(2,1)S(1)}, u32[]{:S(2)}, u32[]{:S(2)}) async-start(bf16[4,400,768]{2,1,0:T(8,128)(2,1)} %get-tuple-element.135.refs_2_), calls=%async_computation | async-start | bytes 4915200 | tf_op jit(solution)/shard_map/all_to_all | solution.py:919
  20.0 30.7 %shard_map.290 = (bf16[768,1024]{1,0:T(8,128)(2,1)}, bf16[1024,768]{1,0:T(8,128)(2,1)}, bf16[1024,768]{1,0:T(8,128)(2,1)}, bf16[1024,768]{1,0:T(8,128)(2,1)}, bf...) custom-call(bf16[1024,768]{1,0:T(8,128)(2,1)} %refs_2_.1, ...), custom_call_target="tpu_custom_call" | custom-call | flops 21474836480 | tf_op jit(solution)/shard_map/pallas_call | solution.py:86
  50.7 2.1 collective-permute-start
  52.8 2.3 collective-permute-start.1
  55.8 1.1 copy-done.17
  56.8 12.5 %shard_map.291 = (bf16[384,768]{1,0:T(8,128)(2,1)}, bf16[400,768]{1,0:T(8,128)(2,1)S(1)}, bf16[384,3072]{1,0:T(8,128)(2,1)}, bf16[384,3072]{1,0:T(8,128)(2,1)}, f32[8,128]{1,0:T(8,128)S(1)}) custom-call(s32[1]{0:T(128)} %bitcast.4.refs_0_, s32[1]{0:T(128)} %bitcast.2.refs_0_.refs_1_.refs_2_, bf16[4,400,768]{2,1,0:T(8,128)(2,1)S(1)} %copy-done.10, ...), custom_call_target="tpu_custom_call" | custom-call | flops 10737418240 | tf_op jit(solution)/shard_map/pallas_call | solution.py:86
  69.4 4.8 %collective-permute-done.refs_3_.refs_1_.refs_5_ = bf16[400,768]{1,0:T(8,128)(2,1)S(1)} collective-permute-done((bf16[400,768]{1,0:T(8,128)(2,1)}, bf16[400,768]{1,0:T(8,128)(2,1)S(1)}, u32[]{:S(2)}, u32[]{:S(2)}) %collective-permute-start) | collective-permute-done | bytes 614432 | tf_op jit(solution)/shard_map/ppermute | solution.py:760
  74.2 19.3 %collective-permute-done.1.refs_4_.refs_2_.refs_6_ = bf16[400,768]{1,0:T(8,128)(2,1)S(1)} collective-permute-done((bf16[400,768]{1,0:T(8,128)(2,1)}, bf16[400,768]{1,0:T(8,128)(2,1)S(1)}, u32[]{:S(2)}, u32[]{:S(2)}) %collective-permute-start.1) | collective-permute-done | bytes 614432 | tf_op jit(solution)/shard_map/ppermute | solution.py:760
  94.3 5.1 %collective-permute-start.3 = (bf16[400,768]{1,0:T(8,128)(2,1)}, bf16[400,768]{1,0:T(8,128)(2,1)}, u32[]{:S(2)}, u32[]{:S(2)}) collective-permute-start(bf16[400,768]{1,0:T(8,128)(2,1)} %get-tuple-element.146), channel_id=1, source_target_pairs={{0,2},{1,3},{2,0},{3,1},{4,6},{5,7},{6,4},{7,5},{8,10},{9,11},{10,... | collective-permute-start | bytes 1843208 | tf_op jit(solution)/shard_map/ppermute | solution.py:760
  99.9 1.1 copy-done.7
  100.9 14.3 %shard_map.292 = (bf16[384,768]{1,0:T(8,128)(2,1)}, bf16[384,768]{1,0:T(8,128)(2,1)}, bf16[400,768]{1,0:T(8,128)(2,1)}, bf16[400,768]{1,0:T(8,128)(2,1)}, bf16[7...) custom-call(s32[4]{0:T(128)S(1)} %select_reduce_fusion.refs_0_, ...), custom_call_target="tpu_custom_call" | custom-call | flops 10737418240 | tf_op jit(solution)/shard_map/pallas_call | solution.py:86
  115.2 9.9 %collective-permute-start.2 = (bf16[400,768]{1,0:T(8,128)(2,1)}, bf16[400,768]{1,0:T(8,128)(2,1)}, u32[]{:S(2)}, u32[]{:S(2)}) collective-permute-start(bf16[400,768]{1,0:T(8,128)(2,1)} %get-tuple-element.144), channel_id=1, source_target_pairs={{0,3},{1,0},{2,1},{3,2},{4,7},{5,4},{6,5},{7,6},{8,11},{9,8},{10,9... | collective-permute-start | bytes 1843208 | tf_op jit(solution)/shard_map/ppermute | solution.py:760
  125.1 1.9 collective-permute-done.3.refs_3_.refs_5_.refs_7_
  126.9 12.3 %shard_map.294 = (bf16[384,768]{1,0:T(8,128)(2,1)}, bf16[400,768]{1,0:T(8,128)(2,1)}, bf16[384,3072]{1,0:T(8,128)(2,1)}, bf16[384,3072]{1,0:T(8,128)(2,1)}, f32[8,128]{1,0:T(8,128)}) custom-call(s32[4]{0:T(128)S(1)} %select_reduce_fusion.refs_0_, s32[1]{0:T(128)} %bitcast.2.refs_0_.refs_1_.refs_2_, bf16[4,400,768]{2,1,0:T(8,128)(2,1)S(1)} %all-to-all-done.refs_2_.refs_3_, ...), custom_call_target="tpu_custom_call" | custom-call | flops 10737418240 | tf_op jit(solution)/shard_map/pallas_call | solution.py:86
  140.3 1.1 copy-done.18
  141.4 12.9 %shard_map.296 = (bf16[4,96,3072]{2,1,0:T(8,128)(2,1)S(1)}, bf16[4,96,3072]{2,1,0:T(8,128)(2,1)}, f32[8,128]{1,0:T(8,128)S(1)}) custom-call(s32[4]{0:T(128)S(1)} %select_reduce_fusion.refs_0_, s32[1]{0:T(128)} %bitcast.7.refs_1_.refs_0_, bf16[400,768]{1,0:T(8,128)(2,1)S(1)} %copy-done.18, bf16[400,768]{1,0:T(8,128)(2,1)S(1)} %collective-permute-done.refs_3_.refs_1_.refs_5_, ...), custom_call_target="tpu_custom_call" | custom-call | flops 5368709120 | tf_op jit(solution)/shard_map/pallas_call | solution.py:86
  154.5 13.4 %shard_map.297 = (bf16[4,768,384]{2,1,0:T(8,128)(2,1)S(1)}, bf16[4,768,384]{2,1,0:T(8,128)(2,1)}, f32[8,128]{1,0:T(8,128)}) custom-call(s32[4]{0:T(128)S(1)} %select_reduce_fusion.refs_0_, s32[1]{0:T(128)} %bitcast.7.refs_1_.refs_0_, s32[1]{0:T(128)} %bitcast.2.refs_0_.refs_1_.refs_2_, bf16[4,400,768]{2,1,0:T(8,128)(2,1)S(1)} %all-to-all-done.refs_2_.refs_3_, ...), custom_call_target="tpu_custom_call" | custom-call | flops 1073741824 | tf_op jit(solution)/shard_map/pallas_call | solution.py:86
  168.4 9.8 %collective-permute-done.4.refs_16_ = bf16[400,768]{1,0:T(8,128)(2,1)} collective-permute-done((bf16[400,768]{1,0:T(8,128)(2,1)}, bf16[400,768]{1,0:T(8,128)(2,1)}, u32[]{:S(2)}, u32[]{:S(2)}) %collective-permute-start.4) | collective-permute-done | bytes 614432 | tf_op jit(solution)/shard_map/ppermute | solution.py:760
  178.3 12.2 %shard_map.295 = (f32[1,1024]{1,0:T(1,128)S(1)}, f32[1024,768]{1,0:T(8,128)S(1)}, bf16[1024,768]{1,0:T(8,128)(2,1)S(1)}, f32[16,1024]{1,0:T(8,128)S(1)}, bf16[76...) custom-call(f32[1]{0:T(128)S(6)} %copy.47.refs_12_.refs_0_, ...), custom_call_target="tpu_custom_call" | custom-call | flops 536870912000 | tf_op jit(solution)/shard_map/pallas_call | solution.py:86
  190.6 3.8 %shard_map.298 = (bf16[96,6144]{1,0:T(8,128)(2,1)S(1)}, bf16[96,3072]{1,0:T(8,128)(2,1)S(1)}, bf16[2,96,3072]{2,1,0:T(8,128)(2,1)S(1)}, bf16[96,3072]{1,0:T(8,12...) custom-call(bf16[4,96,3072]{2,1,0:T(8,128)(2,1)S(1)} %get-tuple-element.157.refs_0_, ...), custom_call_target="tpu_custom_call" | custom-call | flops 1073741824 | tf_op jit(solution)/shard_map/pallas_call | solution.py:86
  195.0 4.1 %collective-permute-start.8 = (bf16[384,768]{1,0:T(8,128)(2,1)S(1)}, bf16[384,768]{1,0:T(8,128)(2,1)S(1)}, u32[]{:S(2)}, u32[]{:S(2)}) collective-permute-start(bf16[384,768]{1,0:T(8,128)(2,1)S(1)} %get-tuple-element.167), channel_id=1, source_target_pairs={{0,3},{1,0},{2,1},{3,2},{4,7},{5,4},{6,5},{7,6},{8,11},{9,8},{10,9... | collective-permute-start | bytes 1769480 | tf_op jit(solution)/shard_map/ppermute | solution.py:760
  199.1 1.5 collective-permute-start.13
  200.6 1.5 collective-permute-start.14
  203.1 15.5 %shard_map.301 = (bf16[1024,512]{1,0:T(8,128)(2,1)S(1)}, bf16[1024,512]{1,0:T(8,128)(2,1)S(1)}, bf16[1024,512]{1,0:T(8,128)(2,1)S(1)}, bf16[4,96,2432]{2,1,0:T(8...) custom-call(s32[1]{0:T(128)} %bitcast.7.refs_1_.refs_0_, ...), custom_call_target="tpu_custom_call" | custom-call | flops 107374184 | tf_op jit(solution)/shard_map/pallas_call | solution.py:86
  219.2 6.9 %collective-permute-done.9.refs_2_.refs_6_ = bf16[384,768]{1,0:T(8,128)(2,1)S(1)} collective-permute-done((bf16[384,768]{1,0:T(8,128)(2,1)S(1)}, bf16[384,768]{1,0:T(8,128)(2,1)S(1)}, u32[]{:S(2)}, u32[]{:S(2)}) %collective-permute-start.9) | collective-permute-done | bytes 589856 | tf_op jit(solution)/shard_map/ppermute | solution.py:760
  226.1 1.8 collective-permute-start.10
  227.9 6.0 %shard_map.302 = (bf16[1024,256]{1,0:T(8,128)(2,1)S(1)}, bf16[1024,256]{1,0:T(8,128)(2,1)S(1)}, bf16[1024,256]{1,0:T(8,128)(2,1)S(1)}, f32[8,128]{1,0:T(8,128)S(1)}) custom-call(s32[1]{0:T(128)} %bitcast.7.refs_1_.refs_0_, s32[2,1,512]{2,1,0:T(1,128)S(1)} %copy-done.25, bf16[1024,768]{1,0:T(8,128)(2,1)S(1)} %copy-done.1, bf16[1024,768]{1,0:T(8,128)(2,1)S(1)} %copy-done.2, ...), custom_call_target="tpu_custom_call" | custom-call | flops 107374184 | tf_op jit(solution)/shard_map/pallas_call | solution.py:86
  235.1 1.6 collective-permute-start.19
  236.7 1.5 collective-permute-start.20
  238.7 10.2 %shard_map.305 = (bf16[1024,768]{1,0:T(8,128)(2,1)}, bf16[4,96,896]{2,1,0:T(8,128)(2,1)S(1)}, bf16[4,96,896]{2,1,0:T(8,128)(2,1)S(1)}, f32[8,128]{1,0:T(8,128)S(1)}) custom-call(s32[1]{0:T(128)} %bitcast.7.refs_1_.refs_0_, bf16[768,1024]{1,0:T(8,128)(2,1)S(1)} %copy-done, bf16[1024,768]{1,0:T(8,128)(2,1)S(1)} %copy-done.13, ...), custom_call_target="tpu_custom_call" | custom-call | flops 107374184 | tf_op jit(solution)/shard_map/pallas_call | solution.py:86
  248.9 5.6 %collective-permute-done.10.refs_1_.refs_5_ = bf16[384,768]{1,0:T(8,128)(2,1)S(1)} collective-permute-done((bf16[384,768]{1,0:T(8,128)(2,1)S(1)}, bf16[384,768]{1,0:T(8,128)(2,1)S(1)}, u32[]{:S(2)}, u32[]{:S(2)}) %collective-permute-start.10) | collective-permute-done | bytes 589856 | tf_op jit(solution)/shard_map/ppermute | solution.py:760
  254.5 1.2 shard_map.307
  255.8 1.4 copy-done.11
  258.7 1.5 collective-permute-start.16
  260.2 1.5 collective-permute-start.17
  262.2 1.4 shard_map.309
  264.3 4.4 %all-to-all-start.1 = ((bf16[4,32,2432]{2,1,0:T(8,128)(2,1)}), bf16[4,32,2432]{2,1,0:T(8,128)(2,1)S(1)}, u32[]{:S(2)}, u32[]{:S(2)}) async-start(bf16[4,32,2432]{2,1,0:T(8,128)(2,1)} %get-tuple-element.217), calls=%async_computation.1 | async-start | bytes 1245184 | tf_op jit(solution)/shard_map/all_to_all | solution.py:822
  269.2 1.5 collective-permute-start.25
  270.7 1.5 collective-permute-start.26
  273.1 1.2 shard_map.310
  274.4 2.1 collective-permute-start.22
  276.4 2.4 collective-permute-start.23
  278.8 1.5 collective-permute-start.24
  280.3 4.2 %shard_map.311 = (bf16[1024,768]{1,0:T(8,128)(2,1)}, f32[8,128]{1,0:T(8,128)S(1)}) custom-call(f32[1024,768]{1,0:T(8,128)S(1)} %copy-done.5, f32[1,1024]{1,0:T(1,128)S(1)} %get-tuple-element.150.refs_1_, s32[1,1024]{1,0:T(1,128)S(1)} %copy-done.29, bf16[384,768]{1,0:T(8,128)(2,1)S(1)} %copy-done.20, ...), custom_call_target="tpu_custom_call" | custom-call | flops 107374184 | tf_op jit(solution)/shard_map/pallas_call | solution.py:86
  284.8 2.2 shard_map.313
  287.0 1.9 collective-permute-done.23.refs_4_
  (162 shorter events, 19.5 us)
Async XLA Ops:
  9.1 90.3 %all-to-all-start = ((bf16[4,400,768]{2,1,0:T(8,128)(2,1)}), bf16[4,400,768]{2,1,0:T(8,128)(2,1)S(1)}, u32[]{:S(2)}, u32[]{:S(2)}) async-start(bf16[4,400,768]{2,1,0:T(8,128)(2,1)} %get-tuple-element.135.refs_2_), calls=%async_computation | async-start | bytes 4915200 | tf_op jit(solution)/shard_map/all_to_all | solution.py:919
  20.0 35.1 %copy-start.31 = (s32[1024,1]{0,1:T(1,128)S(1)}, s32[1024,1]{0,1:T(1,128)}, u32[]{:S(2)}) copy-start(s32[1024,1]{0,1:T(1,128)} %param.36) | copy-start | bytes 12292
  20.0 35.8 %copy-start.10 = (bf16[4,400,768]{2,1,0:T(8,128)(2,1)S(1)}, bf16[4,400,768]{2,1,0:T(8,128)(2,1)}, u32[]{:S(2)}) copy-start(bf16[4,400,768]{2,1,0:T(8,128)(2,1)} %get-tuple-element.135.refs_2_) | copy-start | bytes 7372804
  50.7 23.4 %collective-permute-start = (bf16[400,768]{1,0:T(8,128)(2,1)}, bf16[400,768]{1,0:T(8,128)(2,1)S(1)}, u32[]{:S(2)}, u32[]{:S(2)}) collective-permute-start(bf16[400,768]{1,0:T(8,128)(2,1)} %get-tuple-element.141), channel_id=1, source_target_pairs={{0,1},{1,2},{2,3},{3,0},{4,5},{5,6},{6,7},{7,4},{8,9},{9,10},{10,1... | collective-permute-start | bytes 1843208 | tf_op jit(solution)/shard_map/ppermute | solution.py:760
  52.8 40.6 %collective-permute-start.1 = (bf16[400,768]{1,0:T(8,128)(2,1)}, bf16[400,768]{1,0:T(8,128)(2,1)S(1)}, u32[]{:S(2)}, u32[]{:S(2)}) collective-permute-start(bf16[400,768]{1,0:T(8,128)(2,1)} %get-tuple-element.142), channel_id=1, source_target_pairs={{0,3},{1,0},{2,1},{3,2},{4,7},{5,4},{6,5},{7,6},{8,11},{9,8},{10,9... | collective-permute-start | bytes 1843208 | tf_op jit(solution)/shard_map/ppermute | solution.py:760
  69.4 24.7 %copy-start.44 = (bf16[400,768]{1,0:T(8,128)(2,1)}, bf16[400,768]{1,0:T(8,128)(2,1)S(1)}, u32[]{:S(2)}) copy-start(bf16[400,768]{1,0:T(8,128)(2,1)S(1)} %get-tuple-element.140.refs_14_) | copy-start | bytes 1843204
  94.3 32.7 %collective-permute-start.3 = (bf16[400,768]{1,0:T(8,128)(2,1)}, bf16[400,768]{1,0:T(8,128)(2,1)}, u32[]{:S(2)}, u32[]{:S(2)}) collective-permute-start(bf16[400,768]{1,0:T(8,128)(2,1)} %get-tuple-element.146), channel_id=1, source_target_pairs={{0,2},{1,3},{2,0},{3,1},{4,6},{5,7},{6,4},{7,5},{8,10},{9,11},{10,... | collective-permute-start | bytes 1843208 | tf_op jit(solution)/shard_map/ppermute | solution.py:760
  115.2 39.1 %collective-permute-start.2 = (bf16[400,768]{1,0:T(8,128)(2,1)}, bf16[400,768]{1,0:T(8,128)(2,1)}, u32[]{:S(2)}, u32[]{:S(2)}) collective-permute-start(bf16[400,768]{1,0:T(8,128)(2,1)} %get-tuple-element.144), channel_id=1, source_target_pairs={{0,3},{1,0},{2,1},{3,2},{4,7},{5,4},{6,5},{7,6},{8,11},{9,8},{10,9... | collective-permute-start | bytes 1843208 | tf_op jit(solution)/shard_map/ppermute | solution.py:760
  125.1 29.3 %collective-permute-start.5 = (bf16[400,768]{1,0:T(8,128)(2,1)}, bf16[400,768]{1,0:T(8,128)(2,1)}, u32[]{:S(2)}, u32[]{:S(2)}) collective-permute-start(bf16[400,768]{1,0:T(8,128)(2,1)} %get-tuple-element.149), channel_id=1, source_target_pairs={{0,1},{1,2},{2,3},{3,0},{4,5},{5,6},{6,7},{7,4},{8,9},{9,10},{10,1... | collective-permute-start | bytes 1843208 | tf_op jit(solution)/shard_map/ppermute | solution.py:760
  139.2 39.0 %collective-permute-start.4 = (bf16[400,768]{1,0:T(8,128)(2,1)}, bf16[400,768]{1,0:T(8,128)(2,1)}, u32[]{:S(2)}, u32[]{:S(2)}) collective-permute-start(bf16[400,768]{1,0:T(8,128)(2,1)} %get-tuple-element.148), channel_id=1, source_target_pairs={{0,2},{1,3},{2,0},{3,1},{4,6},{5,7},{6,4},{7,5},{8,10},{9,11},{10,... | collective-permute-start | bytes 1843208 | tf_op jit(solution)/shard_map/ppermute | solution.py:760
  141.4 12.9 %copy-start.9 = (bf16[400,768]{1,0:T(8,128)(2,1)S(1)}, bf16[400,768]{1,0:T(8,128)(2,1)}, u32[]{:S(2)}) copy-start(bf16[400,768]{1,0:T(8,128)(2,1)} %copy-done.6) | copy-start | bytes 1843204
  141.4 12.9 %copy-start.19 = (bf16[400,768]{1,0:T(8,128)(2,1)S(1)}, bf16[400,768]{1,0:T(8,128)(2,1)}, u32[]{:S(2)}) copy-start(bf16[400,768]{1,0:T(8,128)(2,1)} %get-tuple-element.139.refs_3_.refs_2_.refs_4_) | copy-start | bytes 1843204
  154.3 36.2 %collective-permute-start.6 = (bf16[4,96,3072]{2,1,0:T(8,128)(2,1)}, bf16[4,96,3072]{2,1,0:T(8,128)(2,1)}, u32[]{:S(2)}, u32[]{:S(2)}) collective-permute-start(bf16[4,96,3072]{2,1,0:T(8,128)(2,1)} %get-tuple-element.158), channel_id=1, source_target_pairs={{0,4},{4,0},{8,12},{12,8},{16,20},{20,16},{24,28},{28,24},{1,5},{5... | collective-permute-start | bytes 7077896 | tf_op jit(solution)/shard_map/ppermute | solution.py:755
  154.3 23.9 %copy-start.4 = (f32[1024,768]{1,0:T(8,128)S(1)}, f32[1024,768]{1,0:T(8,128)}, u32[]{:S(2)}) copy-start(f32[1024,768]{1,0:T(8,128)} %get-tuple-element.134.refs_5_.refs_0_) | copy-start | bytes 9437188
  154.4 23.9 %copy-start.29 = (s32[1,1024]{1,0:T(1,128)S(1)}, s32[1,1024]{1,0:T(1,128)}, u32[]{:S(2)}) copy-start(s32[1,1024]{1,0:T(1,128)} %copy-done.28) | copy-start | bytes 12292
  154.4 23.9 %copy-start.32 = (f32[8,16]{1,0:T(8,128)S(1)}, f32[8,16]{1,0:T(8,128)}, u32[]{:S(2)}) copy-start(f32[8,16]{1,0:T(8,128)} %scatter.4.refs_11_.refs_9_) | copy-start | bytes 1540
  154.4 23.9 %copy-start.33 = (f32[1,768]{1,0:T(1,128)S(1)}, f32[1,768]{1,0:T(1,128)}, u32[]{:S(2)}) copy-start(f32[1,768]{1,0:T(1,128)} %reshape.137.refs_8_.refs_11_) | copy-start | bytes 9220
  154.4 23.9 %copy-start.34 = (f32[1,768]{1,0:T(1,128)S(1)}, f32[1,768]{1,0:T(1,128)}, u32[]{:S(2)}) copy-start(f32[1,768]{1,0:T(1,128)} %reshape.138.refs_9_.refs_12_) | copy-start | bytes 9220
  154.4 23.9 %copy-start.36 = (bf16[1024,768]{1,0:T(8,128)(2,1)S(1)}, bf16[1024,768]{1,0:T(8,128)(2,1)}, u32[]{:S(2)}) copy-start(bf16[1024,768]{1,0:T(8,128)(2,1)} %refs_6_.4) | copy-start | bytes 4718596
  154.4 23.9 %copy-start.37 = (bf16[768,768]{1,0:T(8,128)(2,1)S(1)}, bf16[768,768]{1,0:T(8,128)(2,1)}, u32[]{:S(2)}) copy-start(bf16[768,768]{1,0:T(8,128)(2,1)} %refs_13_.1) | copy-start | bytes 3538948
  154.4 23.9 %copy-start.38 = (f32[768,16]{0,1:T(8,128)S(1)}, f32[768,16]{0,1:T(8,128)}, u32[]{:S(2)}) copy-start(f32[768,16]{0,1:T(8,128)} %param.30) | copy-start | bytes 147460
  154.4 23.9 %copy-start.45 = (bf16[400,768]{1,0:T(8,128)(2,1)S(1)}, bf16[400,768]{1,0:T(8,128)(2,1)}, u32[]{:S(2)}) copy-start(bf16[400,768]{1,0:T(8,128)(2,1)} %copy-done.44) | copy-start | bytes 1843204
  154.4 23.9 %copy-start.46 = (bf16[1024,768]{1,0:T(8,128)(2,1)S(1)}, bf16[1024,768]{1,0:T(8,128)(2,1)}, u32[]{:S(2)}) copy-start(bf16[1024,768]{1,0:T(8,128)(2,1)} %get-tuple-element.137.refs_7_) | copy-start | bytes 4718596
  154.5 23.9 %copy-start.47 = (f32[16,1024]{1,0:T(8,128)S(1)}, f32[16,1024]{1,0:T(8,128)}, u32[]{:S(2)}) copy-start(f32[16,1024]{1,0:T(8,128)} %get-tuple-element.138.refs_8_) | copy-start | bytes 196612
  167.9 22.7 %collective-permute-start.7 = (bf16[4,768,384]{2,1,0:T(8,128)(2,1)}, bf16[4,768,384]{2,1,0:T(8,128)(2,1)}, u32[]{:S(2)}, u32[]{:S(2)}) collective-permute-start(bf16[4,768,384]{2,1,0:T(8,128)(2,1)} %get-tuple-element.164), channel_id=1, source_target_pairs={{0,4},{4,0},{8,12},{12,8},{16,20},{20,16},{24,28},{28,24},{1,5},{5... | collective-permute-start | bytes 7077896 | tf_op jit(solution)/shard_map/ppermute | solution.py:755
  190.5 12.5 %copy-start = (bf16[768,1024]{1,0:T(8,128)(2,1)S(1)}, bf16[768,1024]{1,0:T(8,128)(2,1)}, u32[]{:S(2)}) copy-start(bf16[768,1024]{1,0:T(8,128)(2,1)} %get-tuple-element.171.refs_8_.refs_1_) | copy-start | bytes 4718596
  190.6 12.5 %copy-start.1 = (bf16[1024,768]{1,0:T(8,128)(2,1)S(1)}, bf16[1024,768]{1,0:T(8,128)(2,1)}, u32[]{:S(2)}) copy-start(bf16[1024,768]{1,0:T(8,128)(2,1)} %get-tuple-element.173.refs_2_) | copy-start | bytes 4718596
  195.0 23.7 %collective-permute-start.8 = (bf16[384,768]{1,0:T(8,128)(2,1)S(1)}, bf16[384,768]{1,0:T(8,128)(2,1)S(1)}, u32[]{:S(2)}, u32[]{:S(2)}) collective-permute-start(bf16[384,768]{1,0:T(8,128)(2,1)S(1)} %get-tuple-element.167), channel_id=1, source_target_pairs={{0,3},{1,0},{2,1},{3,2},{4,7},{5,4},{6,5},{7,6},{8,11},{9,8},{10,9... | collective-permute-start | bytes 1769480 | tf_op jit(solution)/shard_map/ppermute | solution.py:760
  199.1 39.1 %collective-permute-start.13 = (bf16[2,96,3072]{2,1,0:T(8,128)(2,1)S(1)}, bf16[2,96,3072]{2,1,0:T(8,128)(2,1)S(1)}, u32[]{:S(2)}, u32[]{:S(2)}) collective-permute-start(bf16[2,96,3072]{2,1,0:T(8,128)(2,1)S(1)} %get-tuple-element.194), channel_id=1, source_target_pairs={{0,8},{4,12},{8,0},{12,4},{16,24},{20,28},{24,16},{28,20},{1,9},{5... | collective-permute-start | bytes 3538952 | tf_op jit(solution)/shard_map/ppermute | solution.py:755
  200.6 38.1 %collective-permute-start.14 = (bf16[2,96,3072]{2,1,0:T(8,128)(2,1)S(1)}, bf16[2,96,3072]{2,1,0:T(8,128)(2,1)S(1)}, u32[]{:S(2)}, u32[]{:S(2)}) collective-permute-start(bf16[2,96,3072]{2,1,0:T(8,128)(2,1)S(1)} %get-tuple-element.195), channel_id=1, source_target_pairs={{0,16},{4,20},{8,24},{12,28},{16,0},{20,4},{24,8},{28,12},{1,17},{... | collective-permute-start | bytes 3538952 | tf_op jit(solution)/shard_map/ppermute | solution.py:755
  202.1 24.0 %collective-permute-start.9 = (bf16[384,768]{1,0:T(8,128)(2,1)S(1)}, bf16[384,768]{1,0:T(8,128)(2,1)S(1)}, u32[]{:S(2)}, u32[]{:S(2)}) collective-permute-start(bf16[384,768]{1,0:T(8,128)(2,1)S(1)} %get-tuple-element.169), channel_id=1, source_target_pairs={{0,1},{1,2},{2,3},{3,0},{4,5},{5,6},{6,7},{7,4},{8,9},{9,10},{10,1... | collective-permute-start | bytes 1769480 | tf_op jit(solution)/shard_map/ppermute | solution.py:760
  203.1 23.0 %copy-start.21 = (bf16[384,768]{1,0:T(8,128)(2,1)S(1)}, bf16[384,768]{1,0:T(8,128)(2,1)}, u32[]{:S(2)}) copy-start(bf16[384,768]{1,0:T(8,128)(2,1)} %get-tuple-element.168.refs_0_) | copy-start | bytes 1769476
  218.6 15.3 %collective-permute-start.11 = (bf16[2,96,2432]{2,1,0:T(8,128)(2,1)S(1)}, bf16[2,96,2432]{2,1,0:T(8,128)(2,1)S(1)}, u32[]{:S(2)}, u32[]{:S(2)}) collective-permute-start(bf16[2,96,2432]{2,1,0:T(8,128)(2,1)S(1)} %get-tuple-element.190), channel_id=1, source_target_pairs={{0,4},{4,0},{8,12},{12,8},{16,20},{20,16},{24,28},{28,24},{1,5},{5... | collective-permute-start | bytes 2801672 | tf_op jit(solution)/shard_map/ppermute | solution.py:755
  218.7 15.2 %collective-permute-start.12 = (bf16[2,96,2432]{2,1,0:T(8,128)(2,1)S(1)}, bf16[2,96,2432]{2,1,0:T(8,128)(2,1)S(1)}, u32[]{:S(2)}, u32[]{:S(2)}) collective-permute-start(bf16[2,96,2432]{2,1,0:T(8,128)(2,1)S(1)} %get-tuple-element.191), channel_id=1, source_target_pairs={{0,4},{4,0},{8,12},{12,8},{16,20},{20,16},{24,28},{28,24},{1,5},{5... | collective-permute-start | bytes 2801672 | tf_op jit(solution)/shard_map/ppermute | solution.py:755
  226.1 28.4 %collective-permute-start.10 = (bf16[384,768]{1,0:T(8,128)(2,1)S(1)}, bf16[384,768]{1,0:T(8,128)(2,1)S(1)}, u32[]{:S(2)}, u32[]{:S(2)}) collective-permute-start(bf16[384,768]{1,0:T(8,128)(2,1)S(1)} %get-tuple-element.170), channel_id=1, source_target_pairs={{0,2},{1,3},{2,0},{3,1},{4,6},{5,7},{6,4},{7,5},{8,10},{9,11},{10,... | collective-permute-start | bytes 1769480 | tf_op jit(solution)/shard_map/ppermute | solution.py:760
  235.1 26.6 %collective-permute-start.19 = (bf16[96,2432]{1,0:T(8,128)(2,1)S(1)}, bf16[96,2432]{1,0:T(8,128)(2,1)S(1)}, u32[]{:S(2)}, u32[]{:S(2)}) collective-permute-start(bf16[96,2432]{1,0:T(8,128)(2,1)S(1)} %get-tuple-element.208), channel_id=1, source_target_pairs={{0,8},{4,12},{8,0},{12,4},{16,24},{20,28},{24,16},{28,20},{1,9},{5... | collective-permute-start | bytes 1400840 | tf_op jit(solution)/shard_map/ppermute | solution.py:755
  236.7 25.5 %collective-permute-start.20 = (bf16[96,2432]{1,0:T(8,128)(2,1)S(1)}, bf16[96,2432]{1,0:T(8,128)(2,1)S(1)}, u32[]{:S(2)}, u32[]{:S(2)}) collective-permute-start(bf16[96,2432]{1,0:T(8,128)(2,1)S(1)} %get-tuple-element.209), channel_id=1, source_target_pairs={{0,16},{4,20},{8,24},{12,28},{16,0},{20,4},{24,8},{28,12},{1,17},{... | collective-permute-start | bytes 1400840 | tf_op jit(solution)/shard_map/ppermute | solution.py:755
  238.2 24.0 %collective-permute-start.21 = (bf16[96,2432]{1,0:T(8,128)(2,1)S(1)}, bf16[96,2432]{1,0:T(8,128)(2,1)S(1)}, u32[]{:S(2)}, u32[]{:S(2)}) collective-permute-start(bf16[96,2432]{1,0:T(8,128)(2,1)S(1)} %get-tuple-element.210), channel_id=1, source_target_pairs={{0,24},{4,28},{8,16},{12,20},{16,8},{20,12},{24,0},{28,4},{1,25},{... | collective-permute-start | bytes 1400840 | tf_op jit(solution)/shard_map/ppermute | solution.py:755
  248.9 8.3 %collective-permute-start.15 = (bf16[4,96,896]{2,1,0:T(8,128)(2,1)S(1)}, bf16[4,96,896]{2,1,0:T(8,128)(2,1)S(1)}, u32[]{:S(2)}, u32[]{:S(2)}) collective-permute-start(bf16[4,96,896]{2,1,0:T(8,128)(2,1)S(1)} %get-tuple-element.197), channel_id=1, source_target_pairs={{0,4},{4,0},{8,12},{12,8},{16,20},{20,16},{24,28},{28,24},{1,5},{5... | collective-permute-start | bytes 2064392 | tf_op jit(solution)/shard_map/ppermute | solution.py:755
  258.7 13.5 %collective-permute-start.16 = (bf16[96,896]{1,0:T(8,128)(2,1)}, bf16[96,896]{1,0:T(8,128)(2,1)S(1)}, u32[]{:S(2)}, u32[]{:S(2)}) collective-permute-start(bf16[96,896]{1,0:T(8,128)(2,1)} %get-tuple-element.204), channel_id=1, source_target_pairs={{0,8},{4,12},{8,0},{12,4},{16,24},{20,28},{24,16},{28,20},{1,9},{5... | collective-permute-start | bytes 516104 | tf_op jit(solution)/shard_map/ppermute | solution.py:755
  260.2 12.1 %collective-permute-start.17 = (bf16[96,896]{1,0:T(8,128)(2,1)}, bf16[96,896]{1,0:T(8,128)(2,1)S(1)}, u32[]{:S(2)}, u32[]{:S(2)}) collective-permute-start(bf16[96,896]{1,0:T(8,128)(2,1)} %get-tuple-element.205), channel_id=1, source_target_pairs={{0,16},{4,20},{8,24},{12,28},{16,0},{20,4},{24,8},{28,12},{1,17},{... | collective-permute-start | bytes 516104 | tf_op jit(solution)/shard_map/ppermute | solution.py:755
  261.7 10.5 %collective-permute-start.18 = (bf16[96,896]{1,0:T(8,128)(2,1)}, bf16[96,896]{1,0:T(8,128)(2,1)}, u32[]{:S(2)}, u32[]{:S(2)}) collective-permute-start(bf16[96,896]{1,0:T(8,128)(2,1)} %get-tuple-element.206), channel_id=1, source_target_pairs={{0,24},{4,28},{8,16},{12,20},{16,8},{20,12},{24,0},{28,4},{1,25},{... | collective-permute-start | bytes 516104 | tf_op jit(solution)/shard_map/ppermute | solution.py:755
  264.3 24.6 %all-to-all-start.1 = ((bf16[4,32,2432]{2,1,0:T(8,128)(2,1)}), bf16[4,32,2432]{2,1,0:T(8,128)(2,1)S(1)}, u32[]{:S(2)}, u32[]{:S(2)}) async-start(bf16[4,32,2432]{2,1,0:T(8,128)(2,1)} %get-tuple-element.217), calls=%async_computation.1 | async-start | bytes 1245184 | tf_op jit(solution)/shard_map/all_to_all | solution.py:822
  269.2 15.3 %collective-permute-start.25 = (bf16[96,3072]{1,0:T(8,128)(2,1)S(1)}, bf16[96,3072]{1,0:T(8,128)(2,1)S(1)}, u32[]{:S(2)}, u32[]{:S(2)}) collective-permute-start(bf16[96,3072]{1,0:T(8,128)(2,1)S(1)} %get-tuple-element.225), channel_id=1, source_target_pairs={{0,16},{4,20},{8,24},{12,28},{16,0},{20,4},{24,8},{28,12},{1,17},{... | collective-permute-start | bytes 1769480 | tf_op jit(solution)/shard_map/ppermute | solution.py:755
  270.7 14.1 %collective-permute-start.26 = (bf16[96,3072]{1,0:T(8,128)(2,1)}, bf16[96,3072]{1,0:T(8,128)(2,1)S(1)}, u32[]{:S(2)}, u32[]{:S(2)}) collective-permute-start(bf16[96,3072]{1,0:T(8,128)(2,1)} %get-tuple-element.226), channel_id=1, source_target_pairs={{0,8},{4,12},{8,0},{12,4},{16,24},{20,28},{24,16},{28,20},{1,9},{5... | collective-permute-start | bytes 1769480 | tf_op jit(solution)/shard_map/ppermute | solution.py:755
  274.4 12.6 %collective-permute-start.22 = (bf16[32,896]{1,0:T(8,128)(2,1)S(1)}, bf16[32,896]{1,0:T(8,128)(2,1)S(1)}, u32[]{:S(2)}, u32[]{:S(2)}) collective-permute-start(bf16[32,896]{1,0:T(8,128)(2,1)S(1)} %get-tuple-element.219), channel_id=1, source_target_pairs={{0,1},{1,2},{2,3},{3,0},{4,5},{5,6},{6,7},{7,4},{8,9},{9,10},{10,1... | collective-permute-start | bytes 172040 | tf_op jit(solution)/shard_map/ppermute | solution.py:760
  276.4 12.4 %collective-permute-start.23 = (bf16[32,896]{1,0:T(8,128)(2,1)S(1)}, bf16[32,896]{1,0:T(8,128)(2,1)S(1)}, u32[]{:S(2)}, u32[]{:S(2)}) collective-permute-start(bf16[32,896]{1,0:T(8,128)(2,1)S(1)} %get-tuple-element.220), channel_id=1, source_target_pairs={{0,2},{1,3},{2,0},{3,1},{4,6},{5,7},{6,4},{7,5},{8,10},{9,11},{10,... | collective-permute-start | bytes 172040 | tf_op jit(solution)/shard_map/ppermute | solution.py:760
  278.8 10.1 %collective-permute-start.24 = (bf16[32,896]{1,0:T(8,128)(2,1)S(1)}, bf16[32,896]{1,0:T(8,128)(2,1)S(1)}, u32[]{:S(2)}, u32[]{:S(2)}) collective-permute-start(bf16[32,896]{1,0:T(8,128)(2,1)S(1)} %get-tuple-element.221), channel_id=1, source_target_pairs={{0,3},{1,0},{2,1},{3,2},{4,7},{5,4},{6,5},{7,6},{8,11},{9,8},{10,9... | collective-permute-start | bytes 172040 | tf_op jit(solution)/shard_map/ppermute | solution.py:760
  (35 other events, 170.4 us)
